TPU v7x, 32 devices: a whole 2x2x4 slice. The times are simulated.
32 devices in a mesh: dp: 8 (over z, x), expert: 4 (over y, core).
Axes of the slice: x: 2, y: 2, z: 4, core: 2. Of those that a mesh axis runs over, the one named last changes fastest.
Arguments:
- grad: bfloat16 [16, 7168, 2048], P('expert', 'dp')
- momentum: float32 [16, 7168, 2048], P('expert', 'dp'), may hold values from -6 to 6
- placement: int32 [16], replicated, may hold values from 0 to 15, as said below
Outputs:
- momentum_new: float32 [16, 7168, 2048], P('expert', 'dp')
- update: bfloat16 [16, 7168, 2048], P('expert', 'dp')
Inputs may be any that keep to these rules, and one draw needn't show every extreme that they name: placement is a permutation; position e lies in group e // 4, and placement[e] // 4 is the new group. The 4 experts of each group go to 4 different groups, so every group receives exactly one expert from every group.
All inputs are finite; a program needn't handle non-finite values.
Results may differ from a plain program's by a relative error of at most 0.0074.
Values may be sent and summed in bfloat16 or wider, within the bound.
No kernel may reach another device: no remote copies, remote signals or barrier semaphores. Data moves between devices by JAX's collectives and lax.ppermute only.
A program may use at most 192 MiB of HBM per device.

v0:
```python
import math

import jax
import jax.numpy as jnp
from jax import lax
from jax.sharding import PartitionSpec as P

D = 7168


def from_partner(value, axis, stride):
    mask = 2**stride
    pairs = [(source, source ^ mask) for source in range(lax.axis_size(axis))]
    return lax.ppermute(value, axis, pairs)


def split_pair(gram_part, member, level):
    half_rows = gram_part.shape[0] // 2
    upper = member >> level & 1 == 1
    lower_half = gram_part[:half_rows]
    upper_half = gram_part[half_rows:]
    kept_half = jnp.where(upper, upper_half, lower_half)
    given_half = jnp.where(upper, lower_half, upper_half)
    return (kept_half, given_half)


def join_pair(gram_part, other_half, member, level):
    upper = member >> level & 1 == 1
    return jnp.where(
        upper,
        jnp.concatenate([other_half, gram_part], axis=0),
        jnp.concatenate([gram_part, other_half], axis=0),
    )


def reduce_halves(gram_part, swap_bits, member):
    for level in range(len(swap_bits)):
        kept_half, given_half = split_pair(gram_part, member, level)
        gram_part = kept_half + from_partner(given_half, "dp", swap_bits[level])
    return gram_part


def collect_halves(gram_part, swap_bits, member):
    for level in reversed(range(len(swap_bits))):
        other_half = from_partner(gram_part, "dp", swap_bits[level])
        gram_part = join_pair(gram_part, other_half, member, level)
    return gram_part


def shards(grad, momentum, placement):
    local_count = grad.shape[0]
    row_count = grad.shape[1]
    columns = grad.shape[2]
    dp_count = lax.axis_size("dp")
    group_size = dp_count // local_count
    piece_rows = row_count // group_size
    my_group = lax.axis_index("expert")
    my_index = lax.axis_index("dp")
    momentum_new = 0.95 * momentum + grad.astype(jnp.float32)
    moved = momentum_new.astype(jnp.bfloat16)
    slot_ids = lax.iota(jnp.int32, local_count)
    my_targets = (
        lax.dynamic_slice_in_dim(placement, my_group * local_count, local_count) // local_count
    )
    choose = (my_targets[None, :] == slot_ids[:, None]).astype(jnp.int32)
    send_slot = jnp.sum(choose * slot_ids[None, :], axis=1)
    outgoing = jnp.take(moved, send_slot, axis=0)
    arrived = lax.all_to_all(outgoing, "expert", split_axis=0, concat_axis=0, tiled=True)
    moves_table = placement.reshape(local_count, local_count)
    into_mine = moves_table // local_count == my_group
    new_slot = jnp.sum(jnp.where(into_mine, moves_table % local_count, 0), axis=1)
    picker = (new_slot[None, :] == slot_ids[:, None]).astype(jnp.int32)
    from_source = jnp.sum(picker * slot_ids[None, :], axis=1)
    by_block = jnp.take(arrived, from_source, axis=0)
    pieces = by_block.reshape(local_count, group_size, piece_rows, columns)
    outgoing_rows = pieces.reshape(local_count * group_size, piece_rows, columns)
    block_id = my_index // group_size
    member = my_index % group_size
    first_bit = 0
    swap_bits = [first_bit + level for level in range(group_size.bit_length() - 1)]
    received = lax.all_to_all(outgoing_rows, "dp", split_axis=0, concat_axis=0, tiled=True)
    owned_rows = received.reshape(dp_count * piece_rows, columns)
    values = owned_rows.astype(jnp.float32)
    partial_value = jnp.sum(values * values)
    in_block = (slot_ids == block_id).astype(jnp.float32)
    totals = lax.psum(partial_value * in_block, "dp")
    squares = jnp.sum(totals * in_block)
    factor = 0.5 * math.sqrt(columns) / jnp.sqrt(squares + 1e-06)
    normal = (values * factor).astype(jnp.bfloat16)
    gram_part = lax.dot_general(
        normal, normal, (((0,), (0,)), ((), ())), preferred_element_type=jnp.float32
    )
    gram_part = reduce_halves(gram_part, swap_bits, member)
    gram_whole = collect_halves(gram_part.astype(jnp.bfloat16), swap_bits, member)
    product = jnp.dot(normal, gram_whole, preferred_element_type=jnp.float32).astype(jnp.bfloat16)
    second = jnp.dot(product, gram_whole, preferred_element_type=jnp.float32)
    orthogonal = (
        3.4445 * normal.astype(jnp.float32) - 4.775 * product.astype(jnp.float32) + 2.0315 * second
    )
    result = (orthogonal * math.sqrt(D)).astype(jnp.bfloat16)
    returned = lax.all_to_all(
        result.reshape(dp_count, piece_rows, columns), "dp", split_axis=0, concat_axis=0, tiled=True
    )
    ordered = returned.reshape(local_count, group_size, piece_rows, columns)
    update = ordered.reshape(local_count, row_count, columns)
    return (momentum_new, update)


def solution(mesh):
    return jax.shard_map(
        shards,
        mesh=mesh,
        in_specs=(P("expert", "dp", None), P("expert", "dp", None), P()),
        out_specs=(P("expert", "dp", None), P("expert", "dp", None)),
        check_vma=False,
    )
```

profile of v0, /device:TPU:0, one launch (start us, length us, event | category | flops | bytes accessed | tf_op | source)
XLA Modules:
  0.0 1391.4 jit_solution(4587728646945738215)
XLA Ops:
  1.5 31.7 %fusion.9 = (bf16[4,896,2048]{2,1,0:T(8,128)(2,1)}, f32[4,896,2048]{2,1,0:T(8,128)}) fusion(bf16[4,896,2048]{2,1,0:T(8,128)(2,1)} %param.5, f32[4,896,2048]{2,1,0:T(8,128)} %param.6), kind=kLoop, calls=%fused_computation.46 | loop fusion | flops 29360128 | bytes 88080384 | tf_op jit(solution)/shard_map/convert_element_type | solution.py:60
  33.2 10.7 fusion.11
  44.0 7.1 gather_fusion
  51.1 7.0 gather_fusion.1
  58.1 14.7 %maximum_select_fusion = bf16[4,896,2048]{2,1,0:T(8,128)(2,1)} fusion(bf16[4,896,1024]{2,1,0:T(8,128)(2,1)} %gather_fusion.1, bf16[4,896,1024]{2,1,0:T(8,128)(2,1)} %gather_fusion, pred[4]{0:T(512)(128)(4,1)S(1)} %compare_and_fusion.1), kind=kLoop, calls=%fused_computation.11 | loop fusion | flops 36700160 | bytes 29360132 | tf_op jit(solution)/shard_map/jit(_take)/select_n | solution.py:67
  72.8 6.8 all-to-all-start
  80.0 161.0 %all-to-all-done = bf16[4,896,2048]{2,1,0:T(8,128)(2,1)} async-done(((bf16[4,896,2048]{2,1,0:T(8,128)(2,1)}), bf16[4,896,2048]{2,1,0:T(8,128)(2,1)}, u32[]{:S(2)}, u32[]{:S(2)}) %all-to-all-start) | async-done | bytes 14680096 | tf_op jit(solution)/shard_map/all_to_all | solution.py:68
  240.9 10.7 fusion.10
  251.7 7.1 gather_fusion.2
  258.8 7.1 gather_fusion.3
  265.8 14.7 %maximum_select_fusion.1 = bf16[4,896,2048]{2,1,0:T(8,128)(2,1)} fusion(bf16[4,896,1024]{2,1,0:T(8,128)(2,1)} %gather_fusion.3, bf16[4,896,1024]{2,1,0:T(8,128)(2,1)} %gather_fusion.2, pred[4]{0:T(512)(128)(4,1)S(1)} %compare_and_fusion), kind=kLoop, calls=%fused_computation.12 | loop fusion | flops 36700160 | bytes 29360132 | tf_op jit(solution)/shard_map/jit(_take)/select_n | solution.py:74
  280.5 6.5 all-to-all-start.1
  287.0 317.8 %all-to-all-done.1 = bf16[8,448,2048]{2,1,0:T(8,128)(2,1)} async-done(((bf16[8,448,2048]{2,1,0:T(8,128)(2,1)}), bf16[8,448,2048]{2,1,0:T(8,128)(2,1)}, u32[]{:S(2)}, u32[]{:S(2)}) %all-to-all-start.1) | async-done | bytes 14680096 | tf_op jit(solution)/shard_map/all_to_all | solution.py:81
  604.8 13.3 fusion
  618.8 19.7 %psum.7 = f32[4]{0:T(128)S(1)} all-reduce(f32[4]{0:T(128)S(1)} %compare_select_fusion.6), channel_id=1, replica_groups=mesh['dp'=8,'expert'=4] {'dp'}, use_global_device_ids=true, to_apply=%region_4.6 | all-reduce | flops 4 | bytes 32 | tf_op jit(solution)/shard_map/psum | solution.py:86
  639.7 14.4 %fusion.1 = bf16[8,448,2048]{2,1,0:T(8,128)(2,1)} fusion(bf16[8,448,2048]{2,1,0:T(8,128)(2,1)} %all-to-all-done.1, f32[]{:T(128)S(6)} %div.46), kind=kLoop, calls=%fused_computation.7 | loop fusion | flops 22020096 | bytes 29360132 | tf_op jit(solution)/shard_map/convert_element_type | solution.py:89
  654.1 38.5 %convolution_bitcast_fusion = f32[2048,2048]{1,0:T(8,128)} fusion(bf16[8,448,2048]{2,1,0:T(8,128)(2,1)} %fusion.1), kind=kOutput, calls=%fused_computation.13 | convolution fusion | flops 30064771072 | bytes 31457280 | tf_op jit(solution)/shard_map/dot_general | solution.py:90
  692.7 11.7 slice_select_fusion
  704.4 178.9 %collective-permute-done = f32[1024,2048]{1,0:T(8,128)S(1)} collective-permute-done((f32[1024,2048]{1,0:T(8,128)}, f32[1024,2048]{1,0:T(8,128)S(1)}, u32[]{:S(2)}, u32[]{:S(2)}) %collective-permute-start) | collective-permute-done | bytes 8388640 | tf_op jit(solution)/shard_map/ppermute | solution.py:14
  883.3 7.0 add_convert_fusion
  890.7 87.6 %collective-permute-done.1 = bf16[1024,2048]{1,0:T(8,128)(2,1)S(1)} collective-permute-done((bf16[1024,2048]{1,0:T(8,128)(2,1)S(1)}, bf16[1024,2048]{1,0:T(8,128)(2,1)S(1)}, u32[]{:S(2)}, u32[]{:S(2)}) %collective-permute-start.1) | collective-permute-done | bytes 4194336 | tf_op jit(solution)/shard_map/ppermute | solution.py:14
  980.2 40.2 %convolution_convert_fusion = bf16[3584,2048]{1,0:T(8,128)(2,1)} fusion(bf16[3584,2048]{1,0:T(8,128)(2,1)} %bitcast.13, bf16[1024,2048]{1,0:T(8,128)(2,1)S(1)} %add_convert_fusion, bf16[1024,2048]{1,0:T(8,128)(2,1)} %copy-done.2, pred[]{:T(512)S(6)} %eq.56), kind=kOutput, calls=%fused_computation.10 | convolution fusion | flops 30109859840 | bytes 37748736 | tf_op jit(solution)/shard_map/dot_general | solution.py:95
  1020.5 47.7 %multiply_convert_fusion = bf16[3584,2048]{1,0:T(8,128)(2,1)} fusion(bf16[3584,2048]{1,0:T(8,128)(2,1)} %convolution_convert_fusion, bf16[3584,2048]{1,0:T(8,128)(2,1)} %bitcast.14, bf16[1024,2048]{1,0:T(8,128)(2,1)} %copy-done, bf16[1024,2048]{1,0:T(8,128)(2,1)} %copy-done.2, pred[]{:T(512)S(6)} %eq.56), kind=kOutput, calls=%fused_computation.8 | convolution fusion | flops 30168580096 | bytes 52428800 | tf_op jit(solution)/shard_map/dot_general | solution.py:96
  1068.1 317.3 %all_to_all.15 = bf16[8,448,2048]{2,1,0:T(8,128)(2,1)S(1)} all-to-all(bf16[8,448,2048]{2,1,0:T(8,128)(2,1)} %bitcast.12), channel_id=1, replica_groups=mesh['dp'=8,'expert'=4] {'dp'}, dimensions={0} | all-to-all | bytes 29360128 | tf_op jit(solution)/shard_map/all_to_all | solution.py:101
  (22 shorter events, 10.3 us)
Async XLA Ops:
  72.8 6.8 copy-start.1
  72.8 168.1 %all-to-all-start = ((bf16[4,896,2048]{2,1,0:T(8,128)(2,1)}), bf16[4,896,2048]{2,1,0:T(8,128)(2,1)}, u32[]{:S(2)}, u32[]{:S(2)}) async-start(bf16[4,896,2048]{2,1,0:T(8,128)(2,1)} %maximum_select_fusion), calls=%async_computation | async-start | bytes 29360128 | tf_op jit(solution)/shard_map/all_to_all | solution.py:68
  280.5 324.3 %all-to-all-start.1 = ((bf16[8,448,2048]{2,1,0:T(8,128)(2,1)}), bf16[8,448,2048]{2,1,0:T(8,128)(2,1)}, u32[]{:S(2)}, u32[]{:S(2)}) async-start(bf16[8,448,2048]{2,1,0:T(8,128)(2,1)} %bitcast.11), calls=%async_computation.1 | async-start | bytes 29360128 | tf_op jit(solution)/shard_map/all_to_all | solution.py:81
  704.4 178.9 %collective-permute-start = (f32[1024,2048]{1,0:T(8,128)}, f32[1024,2048]{1,0:T(8,128)S(1)}, u32[]{:S(2)}, u32[]{:S(2)}) collective-permute-start(f32[1024,2048]{1,0:T(8,128)} %slice_select_fusion), channel_id=1, source_target_pairs={{0,4},{4,0},{8,12},{12,8},{16,20},{20,16},{24,28},{28,24},{1,5},{5... | collective-permute-start | bytes 25165832 | tf_op jit(solution)/shard_map/ppermute | solution.py:14
  890.3 89.9 %copy-start = (bf16[1024,2048]{1,0:T(8,128)(2,1)}, bf16[1024,2048]{1,0:T(8,128)(2,1)S(1)}, u32[]{:S(2)}) copy-start(bf16[1024,2048]{1,0:T(8,128)(2,1)S(1)} %add_convert_fusion) | copy-start | bytes 12582916
  890.3 87.9 %collective-permute-start.1 = (bf16[1024,2048]{1,0:T(8,128)(2,1)S(1)}, bf16[1024,2048]{1,0:T(8,128)(2,1)S(1)}, u32[]{:S(2)}, u32[]{:S(2)}) collective-permute-start(bf16[1024,2048]{1,0:T(8,128)(2,1)S(1)} %add_convert_fusion), channel_id=1, source_target_pairs={{0,4},{4,0},{8,12},{12,8},{16,20},{20,16},{24,28},{28,24},{1,5},{5... | collective-permute-start | bytes 12582920 | tf_op jit(solution)/shard_map/ppermute | solution.py:14
  978.2 2.0 copy-start.2
where the time goes:
time: 1400 us; the launch traced here: 1390 us
  waiting for transfers between devices  745 us (53%)
  blocking collectives  337 us (24%)
  matrix products  126 us (9%)
  other arithmetic  110 us (8%)
  local copies, waits for them, and re-layouts  57.3 us (4%)
    all_to_all x1, waiting for transfers between devices, shards(): lax.all_to_all(outgoing_rows, 'dp', split_axis=0, concat_axis=0, tiled=True)  318 us
    all_to_all x1, blocking collectives, shards(): lax.all_to_all(result.reshape(dp_count, piece_rows, columns), 'dp', split...  317 us
    ppermute x2, waiting for transfers between devices, from_partner(): return lax.ppermute(value, axis, pairs)  266 us
    all_to_all x1, waiting for transfers between devices, shards(): lax.all_to_all(outgoing, 'expert', split_axis=0, concat_axis=0, tiled=True)  161 us
    dot_general x1, matrix products, shards(): second = jnp.dot(product, gram_whole, preferred_element_type=jnp.float32)  47.7 us
    dot_general x1, matrix products, shards(): jnp.dot(normal, gram_whole, preferred_element_type=jnp.float32)  40.2 us
    dot_general x1, matrix products, shards(): lax.dot_general(normal, normal, (((0,), (0,)), ((), ())), preferred_eleme...  38.5 us
    convert_element_type x1, other arithmetic, shards(): moved = momentum_new.astype(jnp.bfloat16)  31.7 us
  transfers between devices with their start and end apart: 4, of which 4 were waited for; matrix products, arithmetic and copies ran while one was open for 0% of the time, Pallas kernels for 0%

commit v1 on v0

v1 whole, which is shorter than its diff:
```python
import functools
import math

import jax
import jax.numpy as jnp
from jax import lax
from jax.experimental import pallas as pl
from jax.experimental.pallas import tpu as pltpu
from jax.sharding import PartitionSpec as P

D = 7168
BLOCK = 256
VMEM_BYTES = 56 * 2**20


def row_block(rows, most):
    for size in range(most, 15, -16):
        if rows % size == 0:
            return size
    return rows


def momentum_kernel(order_ref, grad_ref, momentum_ref, *refs):
    new_ref, moved_ref, squares_ref = refs[-3:]
    new = 0.95 * momentum_ref[0] + grad_ref[0].astype(jnp.float32)
    new_ref[0] = new
    moved = new.astype(jnp.bfloat16)
    moved_ref[...] = moved
    values = moved.astype(jnp.float32)
    rows, columns = values.shape
    partial_sum = jnp.sum((values * values).reshape(rows // 8, 8, columns), axis=0)

    @pl.when(pl.program_id(0) == 0)
    def _():
        squares_ref[...] = partial_sum

    @pl.when(pl.program_id(0) > 0)
    def _():
        squares_ref[...] += partial_sum


def momentum_step(source, grad, momentum, earlier):
    local_count, rows, columns = grad.shape
    step = row_block(rows, 128)
    spot = pl.BlockSpec((1, step, columns), lambda r, order: (order[0], r, 0))
    in_specs = [spot, spot]
    operands = [source, grad, momentum]
    aliases = {}
    if earlier is not None:
        in_specs.append(pl.BlockSpec(memory_space=pl.ANY))
        operands.append(earlier)
        aliases = {3: 0}
    return pl.pallas_call(
        momentum_kernel,
        grid_spec=pltpu.PrefetchScalarGridSpec(
            num_scalar_prefetch=1,
            grid=(rows // step,),
            in_specs=in_specs,
            out_specs=[
                spot,
                pl.BlockSpec((step, columns), lambda r, order: (r, 0)),
                pl.BlockSpec((8, columns), lambda r, order: (0, 0)),
            ],
        ),
        out_shape=[
            jax.ShapeDtypeStruct(momentum.shape, jnp.float32),
            jax.ShapeDtypeStruct((rows, columns), jnp.bfloat16),
            jax.ShapeDtypeStruct((8, columns), jnp.float32),
        ],
        input_output_aliases=aliases,
        compiler_params=pltpu.CompilerParams(vmem_limit_bytes=VMEM_BYTES),
        cost_estimate=pl.CostEstimate(
            flops=4 * rows * columns, bytes_accessed=12 * rows * columns, transcendentals=0
        ),
        name="momentum",
    )(*operands)


def block_places(columns):
    count = columns // BLOCK
    return [(i, j) for i in range(count) for j in range(i, count)]


def gram_kernel(rows_ref, first_ref, second_ref):
    columns = rows_ref.shape[1]
    count = columns // BLOCK
    half = first_ref.shape[0]
    place = 0
    for i in range(count):
        turned = rows_ref[:, i * BLOCK : (i + 1) * BLOCK].T
        for j in range(i, count):
            block = jnp.dot(
                turned,
                rows_ref[:, j * BLOCK : (j + 1) * BLOCK],
                preferred_element_type=jnp.float32,
            ).astype(jnp.bfloat16)
            if place < half:
                first_ref[place] = block
            else:
                second_ref[place - half] = block
            place += 1


def gram_step(moved):
    rows, columns = moved.shape
    half = len(block_places(columns)) // 2
    part = jax.ShapeDtypeStruct((half, BLOCK, BLOCK), jnp.bfloat16)
    return pl.pallas_call(
        gram_kernel,
        in_specs=[pl.BlockSpec(memory_space=pltpu.VMEM)],
        out_specs=[pl.BlockSpec(memory_space=pltpu.VMEM)] * 2,
        out_shape=[part, part],
        compiler_params=pltpu.CompilerParams(vmem_limit_bytes=VMEM_BYTES),
        cost_estimate=pl.CostEstimate(
            flops=4 * half * BLOCK * BLOCK * rows,
            bytes_accessed=2 * rows * columns + 4 * half * BLOCK * BLOCK,
            transcendentals=0,
        ),
        name="gram",
    )(moved)


def times_gram(left_ref, gram_ref, j):
    start = j * BLOCK
    stop = start + BLOCK
    total = lax.dot_general(
        left_ref[:, start:],
        gram_ref[start:stop, start:],
        (((1,), (1,)), ((), ())),
        preferred_element_type=jnp.float32,
    )
    if j > 0:
        total += jnp.dot(
            left_ref[:, :start], gram_ref[:start, start:stop], preferred_element_type=jnp.float32
        )
    return total


def update_kernel(slot_ref, place_ref, factor_ref, rows_ref, *refs):
    pieces = refs[:4]
    out_ref, gram_ref, normal_ref, product_ref = refs[-4:]
    piece_blocks = pieces[0].shape[0]

    @pl.when(pl.program_id(0) == 0)
    def _():
        for number, piece in enumerate(pieces):
            for block in range(piece_blocks):
                index = number * piece_blocks + block
                row = pl.multiple_of(place_ref[0, index], BLOCK)
                column = pl.multiple_of(place_ref[1, index], BLOCK)
                gram_ref[pl.ds(row, BLOCK), pl.ds(column, BLOCK)] = piece[block]

    factor = factor_ref[0]
    factor_squared = factor * factor
    normal_ref[...] = (rows_ref[...].astype(jnp.float32) * factor).astype(jnp.bfloat16)
    count = gram_ref.shape[0] // BLOCK
    for j in range(count):
        product = times_gram(normal_ref, gram_ref, j) * factor_squared
        product_ref[:, j * BLOCK : (j + 1) * BLOCK] = product.astype(jnp.bfloat16)
    for j in range(count):
        here = slice(j * BLOCK, (j + 1) * BLOCK)
        second = times_gram(product_ref, gram_ref, j) * factor_squared
        orthogonal = (
            3.4445 * normal_ref[:, here].astype(jnp.float32)
            - 4.775 * product_ref[:, here].astype(jnp.float32)
            + 2.0315 * second
        )
        out_ref[0, :, here] = (orthogonal * math.sqrt(D)).astype(jnp.bfloat16)


def update_step(slot, places, factor, moved, pieces, earlier, local_count):
    rows, columns = moved.shape
    step = rows // 2 if rows % 32 == 0 and rows >= 512 else rows
    whole = pl.BlockSpec(pieces[0].shape, lambda r, *_: (0, 0, 0))
    in_specs = [
        pl.BlockSpec(memory_space=pltpu.SMEM),
        pl.BlockSpec((step, columns), lambda r, *_: (r, 0)),
    ] + [whole] * 4
    operands = [slot, places, factor, moved, *pieces]
    aliases = {}
    if earlier is not None:
        in_specs.append(pl.BlockSpec(memory_space=pl.ANY))
        operands.append(earlier)
        aliases = {8: 0}
    return pl.pallas_call(
        update_kernel,
        grid_spec=pltpu.PrefetchScalarGridSpec(
            num_scalar_prefetch=2,
            grid=(rows // step,),
            in_specs=in_specs,
            out_specs=pl.BlockSpec((1, step, columns), lambda r, slot, *_: (slot[0], r, 0)),
            scratch_shapes=[
                pltpu.VMEM((columns, columns), jnp.bfloat16),
                pltpu.VMEM((step, columns), jnp.bfloat16),
                pltpu.VMEM((step, columns), jnp.bfloat16),
            ],
        ),
        out_shape=jax.ShapeDtypeStruct((local_count, rows, columns), jnp.bfloat16),
        input_output_aliases=aliases,
        compiler_params=pltpu.CompilerParams(vmem_limit_bytes=VMEM_BYTES),
        cost_estimate=pl.CostEstimate(
            flops=4 * rows * columns * columns,
            bytes_accessed=4 * rows * columns + columns * columns,
            transcendentals=0,
        ),
        name="update",
    )(*operands)


def add_up(mine, arrived):
    return (mine.astype(jnp.float32) + arrived.astype(jnp.float32)).astype(jnp.bfloat16)


class Routes:
    def __init__(self, dp_count):
        everyone = range(dp_count)
        line = lambda i: i >> 1 & 3
        self.side = [(i, i ^ 1) for i in everyone]
        self.inner_side = [(i, i ^ 1) for i in everyone if line(i) in (1, 2)]
        self.inward = [(i, i + 2) for i in everyone if line(i) == 0]
        self.inward += [(i, i - 2) for i in everyone if line(i) == 3]
        self.outward = [(b, a) for a, b in self.inward]
        self.middle = [(i, i + 2) for i in everyone if line(i) == 1]
        self.middle += [(i, i - 2) for i in everyone if line(i) == 2]
        self.far = []
        distance = 8
        while distance < dp_count:
            self.far.append([(i, i ^ distance) for i in everyone])
            distance *= 2


def send(value, pairs):
    return lax.ppermute(value, "dp", pairs)


def halves(part, upper):
    count = part.shape[0] // 2
    kept = lax.dynamic_slice_in_dim(part, upper * count, count)
    given = lax.dynamic_slice_in_dim(part, (1 - upper) * count, count)
    return kept, given


def sum_side_first(part, routes, side, inner):
    kept, given = halves(part, side)
    total = add_up(kept, send(given, routes.side))
    total = add_up(total, send(total, routes.inward))
    total = add_up(total, send(total, routes.middle))
    for pairs in routes.far:
        total = add_up(total, send(total, pairs))
    total = jnp.where(inner, total, send(total, routes.outward))
    return total, send(total, routes.side)


def sum_line_first(part, routes, upper_line, inner):
    kept, given = halves(part, upper_line)
    given = add_up(given, send(given, routes.inward))
    kept = add_up(kept, send(kept, routes.inward))
    total = add_up(kept, send(given, routes.middle))
    total = add_up(total, send(total, routes.inner_side))
    for pairs in routes.far:
        total = add_up(total, send(total, pairs))
    other = send(total, routes.middle)
    total = jnp.where(inner, total, send(total, routes.outward))
    other = jnp.where(inner, other, send(other, routes.outward))
    return total, other


def shards(grad, momentum, placement):
    local_count, row_count, columns = grad.shape
    dp_count = lax.axis_size("dp")
    group_count = lax.axis_size("expert")
    routes = Routes(dp_count)
    my_group = lax.axis_index("expert")
    my_index = lax.axis_index("dp")
    side = my_index & 1
    line = my_index >> 1 & 3
    upper_line = line >> 1
    inner = (line == 1) | (line == 2)

    slot_ids = lax.iota(jnp.int32, local_count)
    moves = placement.reshape(group_count, local_count)

    def route(group, target):
        row = lax.dynamic_index_in_dim(moves, group, keepdims=False)
        chosen = row // local_count == target
        old_slot = jnp.sum(jnp.where(chosen, slot_ids, 0))
        new_slot = jnp.sum(jnp.where(chosen, row % local_count, 0))
        return old_slot, new_slot

    momentum_new = None
    outgoing = []
    squares = jnp.zeros((group_count, local_count), jnp.float32)
    for step in range(group_count):
        old_slot, _ = route(my_group, my_group ^ step)
        momentum_new, moved, sums = momentum_step(
            old_slot.reshape(1), grad, momentum, momentum_new
        )
        outgoing.append(moved)
        squares = squares.at[my_group, old_slot].add(jnp.sum(sums))
    squares = lax.psum(squares, ("dp", "expert"))
    factors = 0.5 * math.sqrt(columns) / jnp.sqrt(squares + 1e-06)

    owned = [outgoing[0]]
    for step in range(1, group_count):
        pairs = [(group, group ^ step) for group in range(group_count)]
        owned.append(lax.ppermute(outgoing[step], "expert", pairs))

    places = jnp.array(block_places(columns), jnp.int32) * BLOCK
    quarter = places.shape[0] // 4
    quarters = places.reshape(4, quarter, 2)
    order = jnp.stack([side, 1 - side, 2 + upper_line, 3 - upper_line])
    my_places = jnp.take(quarters, order, axis=0).reshape(4 * quarter, 2).T

    sums = []
    for step in range(group_count):
        first, second = gram_step(owned[step])
        pieces = sum_side_first(first, routes, side, inner)
        pieces += sum_line_first(second, routes, upper_line, inner)
        sums.append(pieces)

    update = None
    for step in range(group_count):
        group = my_group ^ step
        old_slot, new_slot = route(group, my_group)
        factor = lax.dynamic_slice(factors, (group, old_slot), (1, 1)).reshape(1)
        update = update_step(
            new_slot.reshape(1), my_places, factor, owned[step], sums[step], update, local_count
        )
    return momentum_new, update


def solution(mesh):
    return jax.shard_map(
        shards,
        mesh=mesh,
        in_specs=(P("expert", "dp", None), P("expert", "dp", None), P()),
        out_specs=(P("expert", "dp", None), P("expert", "dp", None)),
        check_vma=False,
    )
```

time: 1400 us -> 856 us (0.61)
  waiting for transfers between devices: 745 us -> 361 us
  blocking collectives: 337 us -> 131 us
  Pallas kernels: 0 us -> 174 us
  matrix products: 126 us -> 0 us
  starting transfers between devices: 13.6 us -> 87.6 us
  other arithmetic: 110 us -> 46 us
  local copies, waits for them, and re-layouts: 57.3 us -> 21.1 us
  between operations: 1.85 us -> 23.3 us
    all_to_all x2 -> x0, waiting for transfers between devices: 479 us -> none  [the longest x1 318 us: shards(): lax.all_to_all(outgoing_rows, 'dp', split_axis=0, concat_axis=0, tiled=True)]
    all_to_all x1 -> x0, blocking collectives: 317 us -> none  [shards(): lax.all_to_all(result.reshape(dp_count, piece_rows, columns), 'dp', split...]
    pallas_call x0 -> x12, Pallas kernels: none -> 174 us  [the longest x4 91.4 us: update_step(): pl.pallas_call(update_kernel, grid_spec=pltpu.PrefetchScalarGridSpec(num_...]
    dot_general x3 -> x0, matrix products: 126 us -> none  [the longest x1 47.7 us: shards(): second = jnp.dot(product, gram_whole, preferred_element_type=jnp.float32)]
    psum x1, blocking collectives: 19.7 us -> 131 us  [shards(): squares = lax.psum(squares, ('dp', 'expert'))]
    ppermute x2 -> x51, waiting for transfers between devices: 266 us -> 361 us  [the longest x48 361 us: send(): return lax.ppermute(value, 'dp', pairs)]
    ppermute x2 -> x51, starting transfers between devices: 0.35 us -> 87.6 us  [the longest x48 85.9 us: send(): return lax.ppermute(value, 'dp', pairs)]
    gather x6 -> x3, local copies, waits for them, and re-layouts: 49.8 us -> 0.66 us  [shards(): my_places = jnp.take(quarters, order, axis=0).reshape(4 * quarter, 2).T]
  transfers between devices with their start and end apart: 4 -> 51, of which waited for: 4 -> 20; matrix products, arithmetic and copies ran while one was open for 0% -> 7% of each run, Pallas kernels for 0% -> 15%
where the time goes in v1:
time: 856 us; the launch traced here: 844 us
  waiting for transfers between devices  361 us (42%)
  Pallas kernels  174 us (20%)
  blocking collectives  131 us (15%)
  starting transfers between devices  87.6 us (10%)
  other arithmetic  46 us (5%)
  between operations  23.3 us (3%)
  local copies, waits for them, and re-layouts  21.1 us (2%)
    ppermute x48, waiting for transfers between devices, send(): return lax.ppermute(value, 'dp', pairs)  361 us
    psum x1, blocking collectives, shards(): squares = lax.psum(squares, ('dp', 'expert'))  131 us
    pallas_call x4, Pallas kernels, update_step(): pl.pallas_call(update_kernel, grid_spec=pltpu.PrefetchScalarGridSpec(num_...  91.4 us
    ppermute x48, starting transfers between devices, send(): return lax.ppermute(value, 'dp', pairs)  85.9 us
    pallas_call x4, Pallas kernels, momentum_step(): pl.pallas_call(momentum_kernel, grid_spec=pltpu.PrefetchScalarGridSpec(nu...  48.1 us
    pallas_call x4, Pallas kernels, gram_step(): pl.pallas_call(gram_kernel, in_specs=[pl.BlockSpec(memory_space=pltpu.VME...  34.2 us
    convert_element_type x24, other arithmetic, add_up(): (mine.astype(jnp.float32) + arrived.astype(jnp.float32)).astype(jnp.bfloa...  24.4 us
  transfers between devices with their start and end apart: 51, of which 20 were waited for; matrix products, arithmetic and copies ran while one was open for 7% of the time, Pallas kernels for 15%

profile of v1, /device:TPU:0, one launch (start us, length us, event | category | flops | bytes accessed | tf_op | source)
XLA Modules:
  0.0 844.4 jit_solution(11044258544566179188)
XLA Ops:
  2.2 12.0 %momentum.4 = (f32[4,896,2048]{2,1,0:T(8,128)}, bf16[896,2048]{1,0:T(8,128)(2,1)}, f32[8,2048]{1,0:T(8,128)}) custom-call(s32[1]{0:T(128)} %bitcast.4.order_ref, bf16[4,896,2048]{2,1,0:T(8,128)(2,1)} %grad_ref.7, f32[4,896,2048]{2,1,0:T(8,128)} %momentum_ref.7), custom_call_target="tpu_custom_call" | custom-call | flops 7340032 | bytes 22020096 | tf_op jit(solution)/shard_map/momentum/pallas_call | solution.py:53
  35.8 12.0 %momentum.5 = (f32[4,896,2048]{2,1,0:T(8,128)}, bf16[896,2048]{1,0:T(8,128)(2,1)}, f32[8,2048]{1,0:T(8,128)}) custom-call(s32[1]{0:T(128)} %bitcast.3.order_ref, bf16[4,896,2048]{2,1,0:T(8,128)(2,1)} %grad_ref.7, f32[4,896,2048]{2,1,0:T(8,128)} %momentum_ref.7, f32[4,896,2048]{2,1,0:T(8,128)} %get-tuple-element.70.refs_0_), custom_call_target="tpu_custom_call", output_to_operand_aliasing={{0}: (3, {})} | custom-call | flops 7340032 | bytes 22020096 | tf_op jit(solution)/shard_map/momentum/pallas_call | solution.py:53
  58.9 12.1 %momentum.6 = (f32[4,896,2048]{2,1,0:T(8,128)}, bf16[896,2048]{1,0:T(8,128)(2,1)}, f32[8,2048]{1,0:T(8,128)}) custom-call(s32[1]{0:T(128)} %bitcast.2.order_ref, bf16[4,896,2048]{2,1,0:T(8,128)(2,1)} %grad_ref.7, f32[4,896,2048]{2,1,0:T(8,128)} %momentum_ref.7, f32[4,896,2048]{2,1,0:T(8,128)} %get-tuple-element.71.refs_0_), custom_call_target="tpu_custom_call", output_to_operand_aliasing={{0}: (3, {})} | custom-call | flops 7340032 | bytes 22020096 | tf_op jit(solution)/shard_map/momentum/pallas_call | solution.py:53
  80.5 11.9 %momentum.7 = (f32[4,896,2048]{2,1,0:T(8,128)}, bf16[896,2048]{1,0:T(8,128)(2,1)}, f32[8,2048]{1,0:T(8,128)}) custom-call(s32[1]{0:T(128)} %bitcast.1.order_ref, bf16[4,896,2048]{2,1,0:T(8,128)(2,1)} %grad_ref.7, f32[4,896,2048]{2,1,0:T(8,128)} %momentum_ref.7, f32[4,896,2048]{2,1,0:T(8,128)} %get-tuple-element.72.refs_0_), custom_call_target="tpu_custom_call", output_to_operand_aliasing={{0}: (3, {})} | custom-call | flops 7340032 | bytes 22020096 | tf_op jit(solution)/shard_map/momentum/pallas_call | solution.py:53
  132.1 131.5 %psum.7 = f32[4,4]{1,0:T(4,128)S(1)} all-reduce(f32[4,4]{1,0:T(4,128)S(1)} %scatter-add.19), channel_id=1, replica_groups=mesh['dp'=8,'expert'=4] {'dp','expert'}, use_global_device_ids=true, to_apply=%region_13.14 | all-reduce | flops 16 | bytes 128 | tf_op jit(solution)/shard_map/psum | solution.py:300
  343.1 18.9 %collective-permute-done.14 = bf16[9,256,256]{2,1,0:T(8,128)(2,1)S(1)} collective-permute-done((bf16[9,256,256]{2,1,0:T(8,128)(2,1)S(1)}, bf16[9,256,256]{2,1,0:T(8,128)(2,1)S(1)}, u32[]{:S(2)}, u32[]{:S(2)}) %collective-permute-start.14) | collective-permute-done | bytes 1179680 | tf_op jit(solution)/shard_map/ppermute | solution.py:233
  363.7 20.8 %collective-permute-done.1 = bf16[9,256,256]{2,1,0:T(8,128)(2,1)S(1)} collective-permute-done((bf16[9,256,256]{2,1,0:T(8,128)(2,1)S(1)}, bf16[9,256,256]{2,1,0:T(8,128)(2,1)S(1)}, u32[]{:S(2)}, u32[]{:S(2)}) %collective-permute-start.1) | collective-permute-done | bytes 1179680 | tf_op jit(solution)/shard_map/ppermute | solution.py:233
  397.2 12.3 %collective-permute-done.32 = bf16[9,256,256]{2,1,0:T(8,128)(2,1)S(1)} collective-permute-done((bf16[9,256,256]{2,1,0:T(8,128)(2,1)S(1)}, bf16[9,256,256]{2,1,0:T(8,128)(2,1)S(1)}, u32[]{:S(2)}, u32[]{:S(2)}) %collective-permute-start.32) | collective-permute-done | bytes 1179680 | tf_op jit(solution)/shard_map/ppermute | solution.py:233
  417.7 22.8 %update.4.refs_4_ = bf16[4,896,2048]{2,1,0:T(8,128)(2,1)} custom-call(s32[1]{0:T(128)} %bitcast.36.slot_ref, s32[2,36]{1,0:T(2,128)} %select_bitcast_fusion.place_ref, f32[1]{0:T(128)} %bitcast.37.factor_ref, bf16[896,2048]{1,0:T(8,128)(2,1)} %get-tuple-element.87.rows_ref, bf16[9,256,256]{2,1,0:T(8,128)(2,1)} %copy-done.9, bf16[9,256,256]{2,1,0:T(8,128)(2,1)} %copy-done.15, ...), custom_call_target="tpu_custom_call" | custom-call | flops 15032385536 | bytes 11534336 | tf_op jit(solution)/shard_map/update/pallas_call | solution.py:185
  462.4 22.9 %collective-permute-done.15 = bf16[9,256,256]{2,1,0:T(8,128)(2,1)} collective-permute-done((bf16[9,256,256]{2,1,0:T(8,128)(2,1)S(1)}, bf16[9,256,256]{2,1,0:T(8,128)(2,1)}, u32[]{:S(2)}, u32[]{:S(2)}) %collective-permute-start.15) | collective-permute-done | bytes 1179680 | tf_op jit(solution)/shard_map/ppermute | solution.py:233
  487.7 23.0 %collective-permute-done.6 = bf16[9,256,256]{2,1,0:T(8,128)(2,1)S(1)} collective-permute-done((bf16[9,256,256]{2,1,0:T(8,128)(2,1)S(1)}, bf16[9,256,256]{2,1,0:T(8,128)(2,1)S(1)}, u32[]{:S(2)}, u32[]{:S(2)}) %collective-permute-start.6) | collective-permute-done | bytes 1179680 | tf_op jit(solution)/shard_map/ppermute | solution.py:233
  512.7 20.6 %collective-permute-done.2 = bf16[9,256,256]{2,1,0:T(8,128)(2,1)S(1)} collective-permute-done((bf16[9,256,256]{2,1,0:T(8,128)(2,1)S(1)}, bf16[9,256,256]{2,1,0:T(8,128)(2,1)S(1)}, u32[]{:S(2)}, u32[]{:S(2)}) %collective-permute-start.2) | collective-permute-done | bytes 1179680 | tf_op jit(solution)/shard_map/ppermute | solution.py:233
  544.2 29.2 %collective-permute-done.36 = bf16[9,256,256]{2,1,0:T(8,128)(2,1)S(1)} collective-permute-done((bf16[9,256,256]{2,1,0:T(8,128)(2,1)S(1)}, bf16[9,256,256]{2,1,0:T(8,128)(2,1)S(1)}, u32[]{:S(2)}, u32[]{:S(2)}) %collective-permute-start.36) | collective-permute-done | bytes 1179680 | tf_op jit(solution)/shard_map/ppermute | solution.py:233
  574.1 24.5 %collective-permute-done.30 = bf16[9,256,256]{2,1,0:T(8,128)(2,1)S(1)} collective-permute-done((bf16[9,256,256]{2,1,0:T(8,128)(2,1)S(1)}, bf16[9,256,256]{2,1,0:T(8,128)(2,1)S(1)}, u32[]{:S(2)}, u32[]{:S(2)}) %collective-permute-start.30) | collective-permute-done | bytes 1179680 | tf_op jit(solution)/shard_map/ppermute | solution.py:233
  602.6 21.4 %collective-permute-done.23 = bf16[9,256,256]{2,1,0:T(8,128)(2,1)S(1)} collective-permute-done((bf16[9,256,256]{2,1,0:T(8,128)(2,1)S(1)}, bf16[9,256,256]{2,1,0:T(8,128)(2,1)S(1)}, u32[]{:S(2)}, u32[]{:S(2)}) %collective-permute-start.23) | collective-permute-done | bytes 1179680 | tf_op jit(solution)/shard_map/ppermute | solution.py:233
  626.4 22.9 %collective-permute-done.17 = bf16[9,256,256]{2,1,0:T(8,128)(2,1)S(1)} collective-permute-done((bf16[9,256,256]{2,1,0:T(8,128)(2,1)S(1)}, bf16[9,256,256]{2,1,0:T(8,128)(2,1)S(1)}, u32[]{:S(2)}, u32[]{:S(2)}) %collective-permute-start.17) | collective-permute-done | bytes 1179680 | tf_op jit(solution)/shard_map/ppermute | solution.py:233
  652.4 22.2 %collective-permute-done.10 = bf16[9,256,256]{2,1,0:T(8,128)(2,1)S(1)} collective-permute-done((bf16[9,256,256]{2,1,0:T(8,128)(2,1)S(1)}, bf16[9,256,256]{2,1,0:T(8,128)(2,1)S(1)}, u32[]{:S(2)}, u32[]{:S(2)}) %collective-permute-start.10) | collective-permute-done | bytes 1179680 | tf_op jit(solution)/shard_map/ppermute | solution.py:233
  677.0 22.8 %collective-permute-done.4 = bf16[9,256,256]{2,1,0:T(8,128)(2,1)S(1)} collective-permute-done((bf16[9,256,256]{2,1,0:T(8,128)(2,1)S(1)}, bf16[9,256,256]{2,1,0:T(8,128)(2,1)S(1)}, u32[]{:S(2)}, u32[]{:S(2)}) %collective-permute-start.4) | collective-permute-done | bytes 1179680 | tf_op jit(solution)/shard_map/ppermute | solution.py:233
  701.6 23.5 %collective-permute-done.38 = bf16[9,256,256]{2,1,0:T(8,128)(2,1)S(1)} collective-permute-done((bf16[9,256,256]{2,1,0:T(8,128)(2,1)S(1)}, bf16[9,256,256]{2,1,0:T(8,128)(2,1)S(1)}, u32[]{:S(2)}, u32[]{:S(2)}) %collective-permute-start.38) | collective-permute-done | bytes 1179680 | tf_op jit(solution)/shard_map/ppermute | solution.py:233
  727.8 22.5 %collective-permute-done.25 = bf16[9,256,256]{2,1,0:T(8,128)(2,1)S(1)} collective-permute-done((bf16[9,256,256]{2,1,0:T(8,128)(2,1)S(1)}, bf16[9,256,256]{2,1,0:T(8,128)(2,1)S(1)}, u32[]{:S(2)}, u32[]{:S(2)}) %collective-permute-start.25) | collective-permute-done | bytes 1179680 | tf_op jit(solution)/shard_map/ppermute | solution.py:233
  751.5 19.8 %collective-permute-done.12 = bf16[9,256,256]{2,1,0:T(8,128)(2,1)S(1)} collective-permute-done((bf16[9,256,256]{2,1,0:T(8,128)(2,1)S(1)}, bf16[9,256,256]{2,1,0:T(8,128)(2,1)S(1)}, u32[]{:S(2)}, u32[]{:S(2)}) %collective-permute-start.12) | collective-permute-done | bytes 1179680 | tf_op jit(solution)/shard_map/ppermute | solution.py:233
  773.5 22.7 %update.5.refs_4_ = bf16[4,896,2048]{2,1,0:T(8,128)(2,1)} custom-call(s32[1]{0:T(128)} %bitcast.34.slot_ref, s32[2,36]{1,0:T(2,128)} %select_bitcast_fusion.place_ref, f32[1]{0:T(128)} %bitcast.35.factor_ref, bf16[896,2048]{1,0:T(8,128)(2,1)} %collective-permute-done.26.rows_ref, bf16[9,256,256]{2,1,0:T(8,128)(2,1)} %copy-done.11, ...), custom_call_target="tpu_custom_call", output_to_operand_aliasing={{}: (8, {})} | custom-call | flops 15032385536 | bytes 11534336 | tf_op jit(solution)/shard_map/update/pallas_call | solution.py:185
  797.3 23.0 %update.6.refs_4_ = bf16[4,896,2048]{2,1,0:T(8,128)(2,1)} custom-call(s32[1]{0:T(128)} %bitcast.31.slot_ref, s32[2,36]{1,0:T(2,128)} %select_bitcast_fusion.place_ref, f32[1]{0:T(128)} %bitcast.32.factor_ref, bf16[896,2048]{1,0:T(8,128)(2,1)} %collective-permute-done.13.rows_ref, bf16[9,256,256]{2,1,0:T(8,128)(2,1)} %copy-done.12, ...), custom_call_target="tpu_custom_call", output_to_operand_aliasing={{}: (8, {})} | custom-call | flops 15032385536 | bytes 11534336 | tf_op jit(solution)/shard_map/update/pallas_call | solution.py:185
  821.3 22.9 %update.7 = bf16[4,896,2048]{2,1,0:T(8,128)(2,1)} custom-call(s32[1]{0:T(128)} %bitcast.6.slot_ref, s32[2,36]{1,0:T(2,128)} %select_bitcast_fusion.place_ref, f32[1]{0:T(128)} %bitcast.29.factor_ref, bf16[896,2048]{1,0:T(8,128)(2,1)} %collective-permute-done.rows_ref, bf16[9,256,256]{2,1,0:T(8,128)(2,1)} %copy-done.13, ...), custom_call_target="tpu_custom_call", output_to_operand_aliasing={{}: (8, {})} | custom-call | flops 15032385536 | bytes 11534336 | tf_op jit(solution)/shard_map/update/pallas_call | solution.py:185
  (201 shorter events, 222.8 us)
Async XLA Ops:
  47.8 229.8 %collective-permute-start.26 = (bf16[896,2048]{1,0:T(8,128)(2,1)}, bf16[896,2048]{1,0:T(8,128)(2,1)}, u32[]{:S(2)}, u32[]{:S(2)}) collective-permute-start(bf16[896,2048]{1,0:T(8,128)(2,1)} %get-tuple-element.84), channel_id=1, source_target_pairs={{0,1},{1,0},{2,3},{3,2},{4,5},{5,4},{6,7},{7,6},{8,9},{9,8},{10,11... | collective-permute-start | bytes 11010056 | tf_op jit(solution)/shard_map/ppermute | solution.py:306
  71.1 218.6 %collective-permute-start.13 = (bf16[896,2048]{1,0:T(8,128)(2,1)}, bf16[896,2048]{1,0:T(8,128)(2,1)}, u32[]{:S(2)}, u32[]{:S(2)}) collective-permute-start(bf16[896,2048]{1,0:T(8,128)(2,1)} %get-tuple-element.81), channel_id=1, source_target_pairs={{0,2},{1,3},{2,0},{3,1},{4,6},{5,7},{6,4},{7,5},{8,10},{9,11},{10,... | collective-permute-start | bytes 11010056 | tf_op jit(solution)/shard_map/ppermute | solution.py:306
  92.5 214.9 %collective-permute-start = (bf16[896,2048]{1,0:T(8,128)(2,1)}, bf16[896,2048]{1,0:T(8,128)(2,1)}, u32[]{:S(2)}, u32[]{:S(2)}) collective-permute-start(bf16[896,2048]{1,0:T(8,128)(2,1)} %get-tuple-element.78), channel_id=1, source_target_pairs={{0,3},{1,2},{2,1},{3,0},{4,7},{5,6},{6,5},{7,4},{8,11},{9,10},{10,... | collective-permute-start | bytes 11010056 | tf_op jit(solution)/shard_map/ppermute | solution.py:306
  94.6 178.1 %collective-permute-start.47 = (bf16[9,256,256]{2,1,0:T(8,128)(2,1)S(1)}, bf16[9,256,256]{2,1,0:T(8,128)(2,1)}, u32[]{:S(2)}, u32[]{:S(2)}) collective-permute-start(bf16[9,256,256]{2,1,0:T(8,128)(2,1)S(1)} %add_convert_fusion.1), channel_id=1, source_target_pairs={{8,12},{12,8},{16,20},{20,16},{9,13},{13,9},{17,21},{21,17},{10,14... | collective-permute-start | bytes 3538952 | tf_op jit(solution)/shard_map/ppermute | solution.py:233
  105.6 170.4 %collective-permute-start.41 = (bf16[9,256,256]{2,1,0:T(8,128)(2,1)S(1)}, bf16[9,256,256]{2,1,0:T(8,128)(2,1)S(1)}, u32[]{:S(2)}, u32[]{:S(2)}) collective-permute-start(bf16[9,256,256]{2,1,0:T(8,128)(2,1)S(1)} %add_convert_fusion.5), channel_id=1, source_target_pairs={{8,16},{12,20},{16,8},{20,12},{9,17},{13,21},{17,9},{21,13},{10,18... | collective-permute-start | bytes 3538952 | tf_op jit(solution)/shard_map/ppermute | solution.py:233
  274.3 67.5 %collective-permute-start.49 = (bf16[9,256,256]{2,1,0:T(8,128)(2,1)S(1)}, bf16[9,256,256]{2,1,0:T(8,128)(2,1)}, u32[]{:S(2)}, u32[]{:S(2)}) collective-permute-start(bf16[9,256,256]{2,1,0:T(8,128)(2,1)S(1)} %add_convert_fusion), channel_id=1, source_target_pairs={{8,16},{12,20},{16,8},{20,12},{9,17},{13,21},{17,9},{21,13},{10,18... | collective-permute-start | bytes 3538952 | tf_op jit(solution)/shard_map/ppermute | solution.py:233
  341.7 67.8 %collective-permute-start.32 = (bf16[9,256,256]{2,1,0:T(8,128)(2,1)S(1)}, bf16[9,256,256]{2,1,0:T(8,128)(2,1)S(1)}, u32[]{:S(2)}, u32[]{:S(2)}) collective-permute-start(bf16[9,256,256]{2,1,0:T(8,128)(2,1)S(1)} %get-tuple-element.103), channel_id=1, source_target_pairs={{0,8},{4,12},{24,16},{28,20},{1,9},{5,13},{25,17},{29,21},{2,10},{... | collective-permute-start | bytes 3538952 | tf_op jit(solution)/shard_map/ppermute | solution.py:233
  393.7 66.4 %collective-permute-start.28 = (bf16[9,256,256]{2,1,0:T(8,128)(2,1)S(1)}, bf16[9,256,256]{2,1,0:T(8,128)(2,1)}, u32[]{:S(2)}, u32[]{:S(2)}) collective-permute-start(bf16[9,256,256]{2,1,0:T(8,128)(2,1)S(1)} %add_convert_fusion.13), channel_id=1, source_target_pairs={{0,8},{4,12},{24,16},{28,20},{1,9},{5,13},{25,17},{29,21},{2,10},{... | collective-permute-start | bytes 3538952 | tf_op jit(solution)/shard_map/ppermute | solution.py:233
  411.3 74.1 %collective-permute-start.15 = (bf16[9,256,256]{2,1,0:T(8,128)(2,1)S(1)}, bf16[9,256,256]{2,1,0:T(8,128)(2,1)}, u32[]{:S(2)}, u32[]{:S(2)}) collective-permute-start(bf16[9,256,256]{2,1,0:T(8,128)(2,1)S(1)} %add_convert_fusion.20), channel_id=1, source_target_pairs={{0,8},{4,12},{24,16},{28,20},{1,9},{5,13},{25,17},{29,21},{2,10},{... | collective-permute-start | bytes 3538952 | tf_op jit(solution)/shard_map/ppermute | solution.py:233
  440.5 70.2 %collective-permute-start.6 = (bf16[9,256,256]{2,1,0:T(8,128)(2,1)S(1)}, bf16[9,256,256]{2,1,0:T(8,128)(2,1)S(1)}, u32[]{:S(2)}, u32[]{:S(2)}) collective-permute-start(bf16[9,256,256]{2,1,0:T(8,128)(2,1)S(1)} %get-tuple-element.107), channel_id=1, source_target_pairs={{0,8},{4,12},{24,16},{28,20},{1,9},{5,13},{25,17},{29,21},{2,10},{... | collective-permute-start | bytes 3538952 | tf_op jit(solution)/shard_map/ppermute | solution.py:233
  441.9 69.5 %collective-permute-start.8 = (bf16[9,256,256]{2,1,0:T(8,128)(2,1)}, bf16[9,256,256]{2,1,0:T(8,128)(2,1)S(1)}, u32[]{:S(2)}, u32[]{:S(2)}) collective-permute-start(bf16[9,256,256]{2,1,0:T(8,128)(2,1)} %add_convert_fusion.23), channel_id=1, source_target_pairs={{8,16},{12,20},{16,8},{20,12},{9,17},{13,21},{17,9},{21,13},{10,18... | collective-permute-start | bytes 3538952 | tf_op jit(solution)/shard_map/ppermute | solution.py:233
  444.7 88.5 %collective-permute-start.2 = (bf16[9,256,256]{2,1,0:T(8,128)(2,1)S(1)}, bf16[9,256,256]{2,1,0:T(8,128)(2,1)S(1)}, u32[]{:S(2)}, u32[]{:S(2)}) collective-permute-start(bf16[9,256,256]{2,1,0:T(8,128)(2,1)S(1)} %add_convert_fusion.27), channel_id=1, source_target_pairs={{0,8},{4,12},{24,16},{28,20},{1,9},{5,13},{25,17},{29,21},{2,10},{... | collective-permute-start | bytes 3538952 | tf_op jit(solution)/shard_map/ppermute | solution.py:233
  460.1 74.2 %collective-permute-start.35 = (bf16[9,256,256]{2,1,0:T(8,128)(2,1)S(1)}, bf16[9,256,256]{2,1,0:T(8,128)(2,1)S(1)}, u32[]{:S(2)}, u32[]{:S(2)}) collective-permute-start(bf16[9,256,256]{2,1,0:T(8,128)(2,1)S(1)} %add_convert_fusion.8), channel_id=1, source_target_pairs={{8,12},{12,8},{16,20},{20,16},{9,13},{13,9},{17,21},{21,17},{10,14... | collective-permute-start | bytes 3538952 | tf_op jit(solution)/shard_map/ppermute | solution.py:233
  540.9 83.1 %collective-permute-start.23 = (bf16[9,256,256]{2,1,0:T(8,128)(2,1)S(1)}, bf16[9,256,256]{2,1,0:T(8,128)(2,1)S(1)}, u32[]{:S(2)}, u32[]{:S(2)}) collective-permute-start(bf16[9,256,256]{2,1,0:T(8,128)(2,1)S(1)} %add_convert_fusion.14), channel_id=1, source_target_pairs={{8,0},{12,4},{16,24},{20,28},{9,1},{13,5},{17,25},{21,29},{10,2},{... | collective-permute-start | bytes 3538952 | tf_op jit(solution)/shard_map/ppermute | solution.py:233
  542.6 106.7 %collective-permute-start.17 = (bf16[9,256,256]{2,1,0:T(8,128)(2,1)S(1)}, bf16[9,256,256]{2,1,0:T(8,128)(2,1)S(1)}, u32[]{:S(2)}, u32[]{:S(2)}) collective-permute-start(bf16[9,256,256]{2,1,0:T(8,128)(2,1)S(1)} %add_convert_fusion.18), channel_id=1, source_target_pairs={{8,0},{12,4},{16,24},{20,28},{9,1},{13,5},{17,25},{21,29},{10,2},{... | collective-permute-start | bytes 3538952 | tf_op jit(solution)/shard_map/ppermute | solution.py:233
  573.4 77.3 %collective-permute-start.11 = (bf16[9,256,256]{2,1,0:T(8,128)(2,1)S(1)}, bf16[9,256,256]{2,1,0:T(8,128)(2,1)S(1)}, u32[]{:S(2)}, u32[]{:S(2)}) collective-permute-start(bf16[9,256,256]{2,1,0:T(8,128)(2,1)S(1)} %add_convert_fusion.21), channel_id=1, source_target_pairs={{8,16},{12,20},{16,8},{20,12},{9,17},{13,21},{17,9},{21,13},{10,18... | collective-permute-start | bytes 3538952 | tf_op jit(solution)/shard_map/ppermute | solution.py:233
  598.7 75.8 %collective-permute-start.10 = (bf16[9,256,256]{2,1,0:T(8,128)(2,1)S(1)}, bf16[9,256,256]{2,1,0:T(8,128)(2,1)S(1)}, u32[]{:S(2)}, u32[]{:S(2)}) collective-permute-start(bf16[9,256,256]{2,1,0:T(8,128)(2,1)S(1)} %add_convert_fusion.21), channel_id=1, source_target_pairs={{8,0},{12,4},{16,24},{20,28},{9,1},{13,5},{17,25},{21,29},{10,2},{... | collective-permute-start | bytes 3538952 | tf_op jit(solution)/shard_map/ppermute | solution.py:233
  601.1 98.7 %collective-permute-start.4 = (bf16[9,256,256]{2,1,0:T(8,128)(2,1)S(1)}, bf16[9,256,256]{2,1,0:T(8,128)(2,1)S(1)}, u32[]{:S(2)}, u32[]{:S(2)}) collective-permute-start(bf16[9,256,256]{2,1,0:T(8,128)(2,1)S(1)} %add_convert_fusion.25), channel_id=1, source_target_pairs={{8,0},{12,4},{16,24},{20,28},{9,1},{13,5},{17,25},{21,29},{10,2},{... | collective-permute-start | bytes 3538952 | tf_op jit(solution)/shard_map/ppermute | solution.py:233
  624.0 101.1 %collective-permute-start.38 = (bf16[9,256,256]{2,1,0:T(8,128)(2,1)S(1)}, bf16[9,256,256]{2,1,0:T(8,128)(2,1)S(1)}, u32[]{:S(2)}, u32[]{:S(2)}) collective-permute-start(bf16[9,256,256]{2,1,0:T(8,128)(2,1)S(1)} %collective-permute-done.37), channel_id=1, source_target_pairs={{8,0},{12,4},{16,24},{20,28},{9,1},{13,5},{17,25},{21,29},{10,2},{... | collective-permute-start | bytes 3538952 | tf_op jit(solution)/shard_map/ppermute | solution.py:233
  649.3 101.1 %collective-permute-start.25 = (bf16[9,256,256]{2,1,0:T(8,128)(2,1)S(1)}, bf16[9,256,256]{2,1,0:T(8,128)(2,1)S(1)}, u32[]{:S(2)}, u32[]{:S(2)}) collective-permute-start(bf16[9,256,256]{2,1,0:T(8,128)(2,1)S(1)} %collective-permute-done.24), channel_id=1, source_target_pairs={{8,0},{12,4},{16,24},{20,28},{9,1},{13,5},{17,25},{21,29},{10,2},{... | collective-permute-start | bytes 3538952 | tf_op jit(solution)/shard_map/ppermute | solution.py:233
  650.7 121.7 %collective-permute-start.31 = (bf16[9,256,256]{2,1,0:T(8,128)(2,1)S(1)}, bf16[9,256,256]{2,1,0:T(8,128)(2,1)S(1)}, u32[]{:S(2)}, u32[]{:S(2)}) collective-permute-start(bf16[9,256,256]{2,1,0:T(8,128)(2,1)S(1)} %broadcast_select_fusion.5.refs_0_), channel_id=1, source_target_pairs={{0,4},{4,0},{8,12},{12,8},{16,20},{20,16},{24,28},{28,24},{1,5},{5... | collective-permute-start | bytes 3538952 | tf_op jit(solution)/shard_map/ppermute | solution.py:233
  674.5 96.8 %collective-permute-start.12 = (bf16[9,256,256]{2,1,0:T(8,128)(2,1)S(1)}, bf16[9,256,256]{2,1,0:T(8,128)(2,1)S(1)}, u32[]{:S(2)}, u32[]{:S(2)}) collective-permute-start(bf16[9,256,256]{2,1,0:T(8,128)(2,1)S(1)} %collective-permute-done.11), channel_id=1, source_target_pairs={{8,0},{12,4},{16,24},{20,28},{9,1},{13,5},{17,25},{21,29},{10,2},{... | collective-permute-start | bytes 3538952 | tf_op jit(solution)/shard_map/ppermute | solution.py:233
  699.8 96.4 %collective-permute-start.18 = (bf16[9,256,256]{2,1,0:T(8,128)(2,1)S(1)}, bf16[9,256,256]{2,1,0:T(8,128)(2,1)S(1)}, u32[]{:S(2)}, u32[]{:S(2)}) collective-permute-start(bf16[9,256,256]{2,1,0:T(8,128)(2,1)S(1)} %broadcast_select_fusion.8.refs_0_), channel_id=1, source_target_pairs={{0,4},{4,0},{8,12},{12,8},{16,20},{20,16},{24,28},{28,24},{1,5},{5... | collective-permute-start | bytes 3538952 | tf_op jit(solution)/shard_map/ppermute | solution.py:233
  725.1 95.2 %collective-permute-start.5 = (bf16[9,256,256]{2,1,0:T(8,128)(2,1)S(1)}, bf16[9,256,256]{2,1,0:T(8,128)(2,1)S(1)}, u32[]{:S(2)}, u32[]{:S(2)}) collective-permute-start(bf16[9,256,256]{2,1,0:T(8,128)(2,1)S(1)} %broadcast_select_fusion.11.refs_0_), channel_id=1, source_target_pairs={{0,4},{4,0},{8,12},{12,8},{16,20},{20,16},{24,28},{28,24},{1,5},{5... | collective-permute-start | bytes 3538952 | tf_op jit(solution)/shard_map/ppermute | solution.py:233
  (46 other events, 1482.7 us)

commit v2 on v1

v2 whole, which is shorter than its diff:
```python
import functools
import math

import jax
import jax.numpy as jnp
from jax import lax
from jax.experimental import pallas as pl
from jax.experimental.pallas import tpu as pltpu
from jax.sharding import PartitionSpec as P

D = 7168
BLOCK = 256
VMEM_BYTES = 56 * 2**20


def row_block(rows, most):
    for size in range(most, 15, -16):
        if rows % size == 0:
            return size
    return rows


def momentum_kernel(grad_ref, momentum_ref, new_ref, moved_ref, squares_ref):
    new = 0.95 * momentum_ref[0] + grad_ref[0].astype(jnp.float32)
    new_ref[0] = new
    moved = new.astype(jnp.bfloat16)
    moved_ref[0] = moved
    values = moved.astype(jnp.float32)
    rows, columns = values.shape
    partial_sum = jnp.sum((values * values).reshape(rows // 8, 8, columns), axis=0)

    @pl.when(pl.program_id(1) == 0)
    def _():
        squares_ref[0] = partial_sum

    @pl.when(pl.program_id(1) > 0)
    def _():
        squares_ref[0] += partial_sum


def momentum_step(grad, momentum):
    count, rows, columns = grad.shape
    step = row_block(rows, 128)
    spot = pl.BlockSpec((1, step, columns), lambda e, r: (e, r, 0))
    return pl.pallas_call(
        momentum_kernel,
        grid=(count, rows // step),
        in_specs=[spot, spot],
        out_specs=[spot, spot, pl.BlockSpec((1, 8, columns), lambda e, r: (e, 0, 0))],
        out_shape=[
            jax.ShapeDtypeStruct(momentum.shape, jnp.float32),
            jax.ShapeDtypeStruct(grad.shape, jnp.bfloat16),
            jax.ShapeDtypeStruct((count, 8, columns), jnp.float32),
        ],
        compiler_params=pltpu.CompilerParams(vmem_limit_bytes=VMEM_BYTES),
        cost_estimate=pl.CostEstimate(
            flops=4 * count * rows * columns,
            bytes_accessed=12 * count * rows * columns,
            transcendentals=0,
        ),
        name="momentum",
    )(grad, momentum)


def block_places(columns):
    count = columns // BLOCK
    return [(i, j) for i in range(count) for j in range(i, count)]


def gram_kernel(slot_ref, rows_ref, out_ref):
    columns = rows_ref.shape[2]
    count = columns // BLOCK
    place = 0
    for i in range(count):
        turned = rows_ref[0, :, i * BLOCK : (i + 1) * BLOCK].T
        for j in range(i, count):
            out_ref[place] = jnp.dot(
                turned,
                rows_ref[0, :, j * BLOCK : (j + 1) * BLOCK],
                preferred_element_type=jnp.float32,
            ).astype(jnp.bfloat16)
            place += 1


def gram_step(slot, moved):
    _, rows, columns = moved.shape
    blocks = len(block_places(columns))
    return pl.pallas_call(
        gram_kernel,
        grid_spec=pltpu.PrefetchScalarGridSpec(
            num_scalar_prefetch=1,
            grid=(1,),
            in_specs=[pl.BlockSpec((1, rows, columns), lambda _, slot: (slot[0], 0, 0))],
            out_specs=pl.BlockSpec((blocks, BLOCK, BLOCK), lambda _, slot: (0, 0, 0)),
        ),
        out_shape=jax.ShapeDtypeStruct((blocks, BLOCK, BLOCK), jnp.bfloat16),
        compiler_params=pltpu.CompilerParams(vmem_limit_bytes=VMEM_BYTES),
        cost_estimate=pl.CostEstimate(
            flops=2 * blocks * BLOCK * BLOCK * rows,
            bytes_accessed=2 * rows * columns + 2 * blocks * BLOCK * BLOCK,
            transcendentals=0,
        ),
        name="gram",
    )(slot, moved)


def times_gram(left_ref, gram_ref, j):
    start = j * BLOCK
    stop = start + BLOCK
    total = lax.dot_general(
        left_ref[:, start:],
        gram_ref[start:stop, start:],
        (((1,), (1,)), ((), ())),
        preferred_element_type=jnp.float32,
    )
    if j > 0:
        total += jnp.dot(
            left_ref[:, :start], gram_ref[:start, start:stop], preferred_element_type=jnp.float32
        )
    return total


def update_kernel(slots_ref, factor_ref, rows_ref, packed_ref, *refs):
    out_ref, gram_ref, normal_ref, product_ref = refs[-4:]

    @pl.when(pl.program_id(0) == 0)
    def _():
        for place, (i, j) in enumerate(block_places(gram_ref.shape[0])):
            gram_ref[i * BLOCK : (i + 1) * BLOCK, j * BLOCK : (j + 1) * BLOCK] = packed_ref[place]

    factor = factor_ref[0]
    factor_squared = factor * factor
    normal_ref[...] = (rows_ref[0].astype(jnp.float32) * factor).astype(jnp.bfloat16)
    count = gram_ref.shape[0] // BLOCK
    for j in range(count):
        product = times_gram(normal_ref, gram_ref, j) * factor_squared
        product_ref[:, j * BLOCK : (j + 1) * BLOCK] = product.astype(jnp.bfloat16)
    for j in range(count):
        here = slice(j * BLOCK, (j + 1) * BLOCK)
        second = times_gram(product_ref, gram_ref, j) * factor_squared
        orthogonal = (
            3.4445 * normal_ref[:, here].astype(jnp.float32)
            - 4.775 * product_ref[:, here].astype(jnp.float32)
            + 2.0315 * second
        )
        out_ref[0, :, here] = (orthogonal * math.sqrt(D)).astype(jnp.bfloat16)


def update_step(slots, factor, moved, packed, earlier=None):
    count, rows, columns = moved.shape
    step = rows // 2 if rows % 32 == 0 and rows >= 512 else rows
    in_specs = [
        pl.BlockSpec(memory_space=pltpu.SMEM),
        pl.BlockSpec((1, step, columns), lambda r, slots: (slots[0], r, 0)),
        pl.BlockSpec(packed.shape, lambda r, slots: (0, 0, 0)),
    ]
    operands = [slots, factor, moved, packed]
    aliases = {}
    if earlier is not None:
        in_specs.append(pl.BlockSpec(memory_space=pl.ANY))
        operands.append(earlier)
        aliases = {4: 0}
    else:
        count = 1
    return pl.pallas_call(
        update_kernel,
        grid_spec=pltpu.PrefetchScalarGridSpec(
            num_scalar_prefetch=1,
            grid=(rows // step,),
            in_specs=in_specs,
            out_specs=pl.BlockSpec((1, step, columns), lambda r, slots: (slots[1], r, 0)),
            scratch_shapes=[
                pltpu.VMEM((columns, columns), jnp.bfloat16),
                pltpu.VMEM((step, columns), jnp.bfloat16),
                pltpu.VMEM((step, columns), jnp.bfloat16),
            ],
        ),
        out_shape=jax.ShapeDtypeStruct((count, rows, columns), jnp.bfloat16),
        input_output_aliases=aliases,
        compiler_params=pltpu.CompilerParams(vmem_limit_bytes=VMEM_BYTES),
        cost_estimate=pl.CostEstimate(
            flops=4 * rows * columns * columns,
            bytes_accessed=4 * rows * columns + columns * columns,
            transcendentals=0,
        ),
        name="update",
    )(*operands)


def place_kernel(slot_ref, arrived_ref, *refs):
    refs[-1][...] = arrived_ref[...]


def place_step(slot, arrived, earlier, count):
    _, rows, columns = arrived.shape
    step = row_block(rows, 256)
    in_specs = [pl.BlockSpec((1, step, columns), lambda r, slot: (0, r, 0))]
    operands = [slot, arrived]
    aliases = {}
    if earlier is not None:
        in_specs.append(pl.BlockSpec(memory_space=pl.ANY))
        operands.append(earlier)
        aliases = {2: 0}
    return pl.pallas_call(
        place_kernel,
        grid_spec=pltpu.PrefetchScalarGridSpec(
            num_scalar_prefetch=1,
            grid=(rows // step,),
            in_specs=in_specs,
            out_specs=pl.BlockSpec((1, step, columns), lambda r, slot: (slot[0], r, 0)),
        ),
        out_shape=jax.ShapeDtypeStruct((count, rows, columns), jnp.bfloat16),
        input_output_aliases=aliases,
        compiler_params=pltpu.CompilerParams(vmem_limit_bytes=VMEM_BYTES),
        cost_estimate=pl.CostEstimate(
            flops=0, bytes_accessed=4 * rows * columns, transcendentals=0
        ),
        name="place",
    )(*operands)


def sum_over_dp(packed):
    flat = packed.reshape(-1, BLOCK)
    share = lax.psum_scatter(flat, "dp", scatter_dimension=0, tiled=True)
    return lax.all_gather(share, "dp", axis=0, tiled=True).reshape(packed.shape)


def shards(grad, momentum, placement):
    local_count, row_count, columns = grad.shape
    group_count = lax.axis_size("expert")
    my_group = lax.axis_index("expert")
    slot_ids = lax.iota(jnp.int32, local_count)
    moves = placement.reshape(group_count, local_count)

    def route(group, target):
        row = lax.dynamic_index_in_dim(moves, group, keepdims=False)
        chosen = row // local_count == target
        old_slot = jnp.sum(jnp.where(chosen, slot_ids, 0))
        new_slot = jnp.sum(jnp.where(chosen, row % local_count, 0))
        return old_slot, new_slot

    momentum_new, moved, sums = momentum_step(grad, momentum)
    squares = lax.psum(jnp.sum(sums, axis=(1, 2)), "dp")
    moved, squares = lax.optimization_barrier((moved, squares))
    factors = 0.5 * math.sqrt(columns) / jnp.sqrt(squares + 1e-06)

    steps = [step for step in range(group_count - 1, -1, -1)]
    old_slots = {step: route(my_group, my_group ^ step)[0] for step in steps}
    new_slots = {step: route(my_group ^ step, my_group)[1] for step in steps}
    grams = {step: gram_step(old_slots[step].reshape(1), moved) for step in steps}
    grams = {step: sum_over_dp(grams[step]) for step in steps}
    update = None
    for step in steps:
        old_slot = old_slots[step]
        factor = lax.dynamic_index_in_dim(factors, old_slot)
        if step == 0:
            slots = jnp.stack([old_slot, new_slots[0]])
            update = update_step(slots, factor, moved, grams[step], update)
        else:
            slots = jnp.stack([old_slot, 0])
            mine = update_step(slots, factor, moved, grams[step])
            pairs = [(group, group ^ step) for group in range(group_count)]
            arrived = lax.ppermute(mine, "expert", pairs)
            update = place_step(new_slots[step].reshape(1), arrived, update, local_count)
    return momentum_new, update


def solution(mesh):
    return jax.shard_map(
        shards,
        mesh=mesh,
        in_specs=(P("expert", "dp", None), P("expert", "dp", None), P()),
        out_specs=(P("expert", "dp", None), P("expert", "dp", None)),
        check_vma=False,
    )
```

time: 856 us -> 832 us (0.972)
  waiting for transfers between devices: 361 us -> 582 us
  blocking collectives: 131 us -> 23.1 us
  starting transfers between devices: 87.6 us -> 2.26 us
  other arithmetic: 46 us -> 7.52 us
  local copies, waits for them, and re-layouts: 21.1 us -> 2.65 us
  Pallas kernels: 174 us -> 184 us
    ppermute x51 -> x3, waiting for transfers between devices: 361 us -> 0.01 us  [shards(): arrived = lax.ppermute(mine, 'expert', pairs)]
    reduce_scatter x0 -> x4, waiting for transfers between devices: none -> 358 us  [sum_over_dp(): share = lax.psum_scatter(flat, 'dp', scatter_dimension=0, tiled=True)]
    all_gather x0 -> x4, waiting for transfers between devices: none -> 223 us  [sum_over_dp(): return lax.all_gather(share, 'dp', axis=0, tiled=True).reshape(packed.shape)]
    psum x1, blocking collectives: 131 us -> 23.1 us  [shards(): squares = lax.psum(jnp.sum(sums, axis=(1, 2)), 'dp')]
    ppermute x51 -> x3, starting transfers between devices: 87.6 us -> 1.47 us  [shards(): arrived = lax.ppermute(mine, 'expert', pairs)]
    convert_element_type x24 -> x0, other arithmetic: 24.4 us -> none  [add_up(): (mine.astype(jnp.float32) + arrived.astype(jnp.float32)).astype(jnp.bfloa...]
    pallas_call x8, Pallas kernels: 82.3 us -> 95.3 us  [the longest x1 40.4 us: momentum_step(): pl.pallas_call(momentum_kernel, grid=(count, rows // step), in_specs=[spo...]
    select_n x14 -> x0, other arithmetic: 12.5 us -> none  [the longest x4 5.97 us: sum_line_first(): total = jnp.where(inner, total, send(total, routes.outward))]
  transfers between devices with their start and end apart: 51 -> 11, of which waited for: 20 -> 8; matrix products, arithmetic and copies ran while one was open for 7% -> 1% of each run, Pallas kernels for 15% -> 14%
where the time goes in v2:
time: 832 us; the launch traced here: 823 us
  waiting for transfers between devices  582 us (70%)
  Pallas kernels  184 us (22%)
  blocking collectives  23.1 us (3%)
  between operations  21.9 us (3%)
    reduce_scatter x4, waiting for transfers between devices, sum_over_dp(): share = lax.psum_scatter(flat, 'dp', scatter_dimension=0, tiled=True)  358 us
    all_gather x4, waiting for transfers between devices, sum_over_dp(): return lax.all_gather(share, 'dp', axis=0, tiled=True).reshape(packed.shape)  223 us
    pallas_call x4, Pallas kernels, update_step(): pl.pallas_call(update_kernel, grid_spec=pltpu.PrefetchScalarGridSpec(num_...  88.8 us
    pallas_call x1, Pallas kernels, momentum_step(): pl.pallas_call(momentum_kernel, grid=(count, rows // step), in_specs=[spo...  40.4 us
    pallas_call x4, Pallas kernels, gram_step(): pl.pallas_call(gram_kernel, grid_spec=pltpu.PrefetchScalarGridSpec(num_sc...  39.7 us
    psum x1, blocking collectives, shards(): squares = lax.psum(jnp.sum(sums, axis=(1, 2)), 'dp')  23.1 us
  transfers between devices with their start and end apart: 11, of which 8 were waited for; matrix products, arithmetic and copies ran while one was open for 1% of the time, Pallas kernels for 14%

profile of v2, /device:TPU:0, one launch (start us, length us, event | category | flops | bytes accessed | tf_op | source)
XLA Modules:
  0.0 823.4 jit_solution(1570100298794571188)
XLA Ops:
  7.2 40.4 %momentum.1 = (f32[4,896,2048]{2,1,0:T(8,128)}, bf16[4,896,2048]{2,1,0:T(8,128)(2,1)}, f32[4,8,2048]{2,1,0:T(8,128)}) custom-call(bf16[4,896,2048]{2,1,0:T(8,128)(2,1)} %grad_ref.1, f32[4,896,2048]{2,1,0:T(8,128)} %momentum_ref.1), custom_call_target="tpu_custom_call" | custom-call | flops 29360128 | bytes 88080384 | tf_op jit(solution)/shard_map/momentum/pallas_call | solution.py:45
  48.8 23.1 %psum.7 = f32[4]{0:T(128)S(1)} all-reduce(f32[4]{0:T(128)S(1)} %reduce_sum.83), channel_id=1, replica_groups=mesh['dp'=8,'expert'=4] {'dp'}, use_global_device_ids=true, to_apply=%region_3.4 | all-reduce | flops 4 | bytes 32 | tf_op jit(solution)/shard_map/psum | solution.py:243
  72.7 9.9 %gram.7 = bf16[36,256,256]{2,1,0:T(8,128)(2,1)} custom-call(s32[1]{0:T(128)} %bitcast.17.slot_ref, bf16[4,896,2048]{2,1,0:T(8,128)(2,1)} %get-tuple-element.11.rows_ref), custom_call_target="tpu_custom_call" | custom-call | flops 4227858432 | bytes 8388608 | tf_op jit(solution)/shard_map/gram/pallas_call | solution.py:88
  82.7 9.9 %gram.6 = bf16[36,256,256]{2,1,0:T(8,128)(2,1)} custom-call(s32[1]{0:T(128)} %bitcast.12.slot_ref, bf16[4,896,2048]{2,1,0:T(8,128)(2,1)} %get-tuple-element.11.rows_ref), custom_call_target="tpu_custom_call" | custom-call | flops 4227858432 | bytes 8388608 | tf_op jit(solution)/shard_map/gram/pallas_call | solution.py:88
  92.9 9.8 %gram.5 = bf16[36,256,256]{2,1,0:T(8,128)(2,1)} custom-call(s32[1]{0:T(128)} %bitcast.7.slot_ref, bf16[4,896,2048]{2,1,0:T(8,128)(2,1)} %get-tuple-element.11.rows_ref), custom_call_target="tpu_custom_call" | custom-call | flops 4227858432 | bytes 8388608 | tf_op jit(solution)/shard_map/gram/pallas_call | solution.py:88
  102.8 10.0 %gram.4 = bf16[36,256,256]{2,1,0:T(8,128)(2,1)} custom-call(s32[1]{0:T(128)} %bitcast.1.slot_ref, bf16[4,896,2048]{2,1,0:T(8,128)(2,1)} %get-tuple-element.11.rows_ref), custom_call_target="tpu_custom_call" | custom-call | flops 4227858432 | bytes 8388608 | tf_op jit(solution)/shard_map/gram/pallas_call | solution.py:88
  112.9 62.4 %reduce-scatter.11.cloned.1.call-done = bf16[1152,256]{1,0:T(8,128)(2,1)} async-done(((bf16[9216,256]{1,0:T(8,128)(2,1)}), bf16[1152,256]{1,0:T(8,128)(2,1)}) %reduce-scatter.11.cloned.1.call-update) | async-done | bytes 589840 | tf_op jit(solution)/shard_map/reduce_scatter | solution.py:224
  175.4 98.6 %reduce-scatter.9.cloned.1.call-done = bf16[1152,256]{1,0:T(8,128)(2,1)} async-done(((bf16[9216,256]{1,0:T(8,128)(2,1)}), bf16[1152,256]{1,0:T(8,128)(2,1)}) %reduce-scatter.9.cloned.1.call-update) | async-done | bytes 589840 | tf_op jit(solution)/shard_map/reduce_scatter | solution.py:224
  274.1 98.6 %reduce-scatter.7.cloned.1.call-done = bf16[1152,256]{1,0:T(8,128)(2,1)} async-done(((bf16[9216,256]{1,0:T(8,128)(2,1)}), bf16[1152,256]{1,0:T(8,128)(2,1)}) %reduce-scatter.7.cloned.1.call-update) | async-done | bytes 589840 | tf_op jit(solution)/shard_map/reduce_scatter | solution.py:224
  373.1 98.8 %reduce-scatter.5.cloned.1.call-done = bf16[1152,256]{1,0:T(8,128)(2,1)} async-done(((bf16[9216,256]{1,0:T(8,128)(2,1)}), bf16[1152,256]{1,0:T(8,128)(2,1)}) %reduce-scatter.5.cloned.1.call-update) | async-done | bytes 589840 | tf_op jit(solution)/shard_map/reduce_scatter | solution.py:224
  483.8 69.8 %all-gather.11.cloned.1.call-done = bf16[9216,256]{1,0:T(8,128)(2,1)} async-done(((bf16[1152,256]{1,0:T(8,128)(2,1)}), bf16[9216,256]{1,0:T(8,128)(2,1)}) %all-gather.11.cloned.1.call-update) | async-done | bytes 4718608 | tf_op jit(solution)/shard_map/all_gather | solution.py:225
  553.6 22.0 %update.6 = bf16[1,896,2048]{2,1,0:T(8,128)(2,1)} custom-call(s32[2]{0:T(128)} %pad_add_fusion.slots_ref, f32[1]{0:T(128)} %get-tuple-element.20.factor_ref, bf16[4,896,2048]{2,1,0:T(8,128)(2,1)} %get-tuple-element.11.rows_ref, bf16[36,256,256]{2,1,0:T(8,128)(2,1)} %bitcast.49), custom_call_target="tpu_custom_call" | custom-call | flops 15032385536 | bytes 11534336 | tf_op jit(solution)/shard_map/update/pallas_call | solution.py:165
  575.6 58.0 %all-gather.9.cloned.1.call-done = bf16[9216,256]{1,0:T(8,128)(2,1)} async-done(((bf16[1152,256]{1,0:T(8,128)(2,1)}), bf16[9216,256]{1,0:T(8,128)(2,1)}) %all-gather.9.cloned.1.call-update) | async-done | bytes 4718608 | tf_op jit(solution)/shard_map/all_gather | solution.py:225
  633.7 22.4 %update.5 = bf16[1,896,2048]{2,1,0:T(8,128)(2,1)} custom-call(s32[2]{0:T(128)} %pad_add_fusion.1.slots_ref, f32[1]{0:T(128)} %get-tuple-element.21.factor_ref, bf16[4,896,2048]{2,1,0:T(8,128)(2,1)} %get-tuple-element.11.rows_ref, bf16[36,256,256]{2,1,0:T(8,128)(2,1)} %bitcast.50), custom_call_target="tpu_custom_call" | custom-call | flops 15032385536 | bytes 11534336 | tf_op jit(solution)/shard_map/update/pallas_call | solution.py:165
  656.1 1.5 collective-permute-start.1
  657.6 56.3 %all-gather.7.cloned.1.call-done = bf16[9216,256]{1,0:T(8,128)(2,1)} async-done(((bf16[1152,256]{1,0:T(8,128)(2,1)}), bf16[9216,256]{1,0:T(8,128)(2,1)}) %all-gather.7.cloned.1.call-update) | async-done | bytes 4718608 | tf_op jit(solution)/shard_map/all_gather | solution.py:225
  713.9 22.2 %update.4 = bf16[1,896,2048]{2,1,0:T(8,128)(2,1)} custom-call(s32[2]{0:T(128)} %pad_add_fusion.2.slots_ref, f32[1]{0:T(128)} %get-tuple-element.22.factor_ref, bf16[4,896,2048]{2,1,0:T(8,128)(2,1)} %get-tuple-element.11.rows_ref, bf16[36,256,256]{2,1,0:T(8,128)(2,1)} %bitcast.51), custom_call_target="tpu_custom_call" | custom-call | flops 15032385536 | bytes 11534336 | tf_op jit(solution)/shard_map/update/pallas_call | solution.py:165
  736.1 1.9 pad_add_fusion.3.slots_ref
  738.0 5.1 place.3.refs_0_
  743.1 5.0 place.4.refs_0_
  748.1 1.9 copy-done
  750.0 5.1 place.5.refs_0_
  755.1 39.1 %all-gather.5.cloned.1.call-done = bf16[9216,256]{1,0:T(8,128)(2,1)} async-done(((bf16[1152,256]{1,0:T(8,128)(2,1)}), bf16[9216,256]{1,0:T(8,128)(2,1)}) %all-gather.5.cloned.1.call-update) | async-done | bytes 4718608 | tf_op jit(solution)/shard_map/all_gather | solution.py:225
  794.2 22.2 %update.7 = bf16[4,896,2048]{2,1,0:T(8,128)(2,1)} custom-call(s32[2]{0:T(128)} %pad_add_fusion.3.slots_ref, f32[1]{0:T(128)} %get-tuple-element.23.factor_ref, bf16[4,896,2048]{2,1,0:T(8,128)(2,1)} %get-tuple-element.11.rows_ref, bf16[36,256,256]{2,1,0:T(8,128)(2,1)} %bitcast.48, bf16[4,896,2048]{2,1,0:T(8,128)(2,1)} %place.5.refs_0_), custom_call_target="tpu_custom_call", output_to_operand_aliasing={{}: (4, {})} | custom-call | flops 15032385536 | bytes 11534336 | tf_op jit(solution)/shard_map/update/pallas_call | solution.py:165
  (32 shorter events, 7.3 us)
Async XLA Ops:
  7.2 168.2 %reduce-scatter.11.cloned.1.call-start = ((), (), s32[]{:S(2)}) async-start(), calls=%async_computation.10 | async-start | bytes 5308416 | tf_op jit(solution)/shard_map/reduce_scatter | solution.py:224
  7.2 41.5 %copy-start.1 = (s32[16]{0:T(128)S(1)}, s32[16]{0:T(128)}, u32[]{:S(2)}) copy-start(s32[16]{0:T(128)} %param.5) | copy-start | bytes 196
  82.7 191.4 %reduce-scatter.9.cloned.1.call-start = ((), (), s32[]{:S(2)}) async-start(), calls=%async_computation.8 | async-start | bytes 5308416 | tf_op jit(solution)/shard_map/reduce_scatter | solution.py:224
  92.7 280.1 %reduce-scatter.7.cloned.1.call-start = ((), (), s32[]{:S(2)}) async-start(), calls=%async_computation.6 | async-start | bytes 5308416 | tf_op jit(solution)/shard_map/reduce_scatter | solution.py:224
  102.8 369.1 %reduce-scatter.5.cloned.1.call-start = ((), (), s32[]{:S(2)}) async-start(), calls=%async_computation.4 | async-start | bytes 5308416 | tf_op jit(solution)/shard_map/reduce_scatter | solution.py:224
  112.9 440.7 %all-gather.11.cloned.1.call-start = ((), (), s32[]{:S(2)}) async-start(), calls=%async_computation.11 | async-start | bytes 5308416 | tf_op jit(solution)/shard_map/all_gather | solution.py:225
  175.4 458.3 %all-gather.9.cloned.1.call-start = ((), (), s32[]{:S(2)}) async-start(), calls=%async_computation.9 | async-start | bytes 5308416 | tf_op jit(solution)/shard_map/all_gather | solution.py:225
  274.1 439.8 %all-gather.7.cloned.1.call-start = ((), (), s32[]{:S(2)}) async-start(), calls=%async_computation.7 | async-start | bytes 5308416 | tf_op jit(solution)/shard_map/all_gather | solution.py:225
  372.8 421.4 %all-gather.5.cloned.1.call-start = ((), (), s32[]{:S(2)}) async-start(), calls=%async_computation.5 | async-start | bytes 5308416 | tf_op jit(solution)/shard_map/all_gather | solution.py:225
  575.6 162.4 %collective-permute-start.2 = (bf16[1,896,2048]{2,1,0:T(8,128)(2,1)}, bf16[1,896,2048]{2,1,0:T(8,128)(2,1)}, u32[]{:S(2)}, u32[]{:S(2)}) collective-permute-start(bf16[1,896,2048]{2,1,0:T(8,128)(2,1)} %update.6), channel_id=1, source_target_pairs={{0,3},{1,2},{2,1},{3,0},{4,7},{5,6},{6,5},{7,4},{8,11},{9,10},{10,... | collective-permute-start | bytes 11010056 | tf_op jit(solution)/shard_map/ppermute | solution.py:263
  656.1 87.0 %collective-permute-start.1 = (bf16[1,896,2048]{2,1,0:T(8,128)(2,1)}, bf16[1,896,2048]{2,1,0:T(8,128)(2,1)}, u32[]{:S(2)}, u32[]{:S(2)}) collective-permute-start(bf16[1,896,2048]{2,1,0:T(8,128)(2,1)} %update.5), channel_id=1, source_target_pairs={{0,2},{1,3},{2,0},{3,1},{4,6},{5,7},{6,4},{7,5},{8,10},{9,11},{10,... | collective-permute-start | bytes 11010056 | tf_op jit(solution)/shard_map/ppermute | solution.py:263
  736.1 12.0 %collective-permute-start = (bf16[1,896,2048]{2,1,0:T(8,128)(2,1)}, bf16[1,896,2048]{2,1,0:T(8,128)(2,1)S(1)}, u32[]{:S(2)}, u32[]{:S(2)}) collective-permute-start(bf16[1,896,2048]{2,1,0:T(8,128)(2,1)} %update.4), channel_id=1, source_target_pairs={{0,1},{1,0},{2,3},{3,2},{4,5},{5,4},{6,7},{7,6},{8,9},{9,8},{10,11... | collective-permute-start | bytes 11010056 | tf_op jit(solution)/shard_map/ppermute | solution.py:263
  748.1 1.9 copy-start
Sparse Core Ops, SparseCore 0:
  82.8 92.5 reduce-scatter.10
  179.0 95.0 reduce-scatter.8
  277.7 95.0 reduce-scatter.6
  376.8 95.0 reduce-scatter.4
  473.9 79.6 all-gather.10
  555.6 78.0 all-gather.8
  635.9 78.0 all-gather.6
  716.1 78.0 all-gather.4

commit v3 on v1

--- a/solution.py
+++ b/solution.py
@@ -10,6 +10,7 @@
 
 D = 7168
 BLOCK = 256
+TRAVEL = 3
 VMEM_BYTES = 56 * 2**20
 
 
@@ -168,7 +169,7 @@
         out_ref[0, :, here] = (orthogonal * math.sqrt(D)).astype(jnp.bfloat16)
 
 
-def update_step(slot, places, factor, moved, pieces, earlier, local_count):
+def update_step(slot, places, factor, moved, pieces, earlier=None, count=1):
     rows, columns = moved.shape
     step = rows // 2 if rows % 32 == 0 and rows >= 512 else rows
     whole = pl.BlockSpec(pieces[0].shape, lambda r, *_: (0, 0, 0))
@@ -195,15 +196,45 @@
                 pltpu.VMEM((step, columns), jnp.bfloat16),
             ],
         ),
-        out_shape=jax.ShapeDtypeStruct((local_count, rows, columns), jnp.bfloat16),
+        out_shape=jax.ShapeDtypeStruct((count, rows, columns), jnp.bfloat16),
         input_output_aliases=aliases,
         compiler_params=pltpu.CompilerParams(vmem_limit_bytes=VMEM_BYTES),
         cost_estimate=pl.CostEstimate(
-            flops=4 * rows * columns * columns,
-            bytes_accessed=4 * rows * columns + columns * columns,
-            transcendentals=0,
+            flops=rows * columns * columns // 4, bytes_accessed=rows * columns, transcendentals=0
         ),
         name="update",
+    )(*operands)
+
+
+def place_kernel(slot_ref, arrived_ref, *refs):
+    refs[-1][...] = arrived_ref[...]
+
+
+def place_step(slot, arrived, earlier, count):
+    _, rows, columns = arrived.shape
+    step = row_block(rows, 256)
+    in_specs = [pl.BlockSpec((1, step, columns), lambda r, slot: (0, r, 0))]
+    operands = [slot, arrived]
+    aliases = {}
+    if earlier is not None:
+        in_specs.append(pl.BlockSpec(memory_space=pl.ANY))
+        operands.append(earlier)
+        aliases = {2: 0}
+    return pl.pallas_call(
+        place_kernel,
+        grid_spec=pltpu.PrefetchScalarGridSpec(
+            num_scalar_prefetch=1,
+            grid=(rows // step,),
+            in_specs=in_specs,
+            out_specs=pl.BlockSpec((1, step, columns), lambda r, slot: (slot[0], r, 0)),
+        ),
+        out_shape=jax.ShapeDtypeStruct((count, rows, columns), jnp.bfloat16),
+        input_output_aliases=aliases,
+        compiler_params=pltpu.CompilerParams(vmem_limit_bytes=VMEM_BYTES),
+        cost_estimate=pl.CostEstimate(
+            flops=0, bytes_accessed=4 * rows * columns, transcendentals=0
+        ),
+        name="place",
     )(*operands)
 
 
@@ -222,6 +253,7 @@
         self.outward = [(b, a) for a, b in self.inward]
         self.middle = [(i, i + 2) for i in everyone if line(i) == 1]
         self.middle += [(i, i - 2) for i in everyone if line(i) == 2]
+        self.swaps = [[(i, i ^ 1 << bit) for i in everyone] for bit in range(dp_count.bit_length() - 1)]
         self.far = []
         distance = 8
         while distance < dp_count:
@@ -240,42 +272,124 @@
     return kept, given
 
 
-def sum_side_first(part, routes, side, inner):
-    kept, given = halves(part, side)
-    total = add_up(kept, send(given, routes.side))
-    total = add_up(total, send(total, routes.inward))
-    total = add_up(total, send(total, routes.middle))
-    for pairs in routes.far:
-        total = add_up(total, send(total, pairs))
-    total = jnp.where(inner, total, send(total, routes.outward))
-    return total, send(total, routes.side)
-
-
-def sum_line_first(part, routes, upper_line, inner):
-    kept, given = halves(part, upper_line)
-    given = add_up(given, send(given, routes.inward))
-    kept = add_up(kept, send(kept, routes.inward))
-    total = add_up(kept, send(given, routes.middle))
-    total = add_up(total, send(total, routes.inner_side))
-    for pairs in routes.far:
-        total = add_up(total, send(total, pairs))
-    other = send(total, routes.middle)
-    total = jnp.where(inner, total, send(total, routes.outward))
-    other = jnp.where(inner, other, send(other, routes.outward))
-    return total, other
+class SideFirst:
+    hops = {
+        "side": ("side", ()),
+        "in": ("inward", ("side",)),
+        "middle": ("middle", ("in",)),
+        "out": ("outward", ("middle",)),
+        "gather": ("side", ("out",)),
+    }
+
+    def __init__(self, routes, place, part):
+        self.routes = routes
+        self.inner = place.inner
+        self.kept, self.given = halves(part, place.side)
+
+    def value(self, hop, got):
+        if hop == "side":
+            return self.given
+        if hop == "in":
+            self.total = add_up(self.kept, got["side"])
+        elif hop == "middle":
+            self.total = add_up(self.total, got["in"])
+        elif hop == "out":
+            self.total = add_up(self.total, got["middle"])
+            for pairs in self.routes.far:
+                self.total = add_up(self.total, send(self.total, pairs))
+        else:
+            self.total = jnp.where(self.inner, self.total, got["out"])
+        return self.total
+
+    def pieces(self, got):
+        return self.total, got["gather"]
+
+
+class LineFirst:
+    hops = {
+        "in given": ("inward", ()),
+        "in kept": ("inward", ()),
+        "middle": ("middle", ("in given",)),
+        "side": ("inner_side", ("in kept", "middle")),
+        "middle back": ("middle", ("side",)),
+        "out": ("outward", ("side",)),
+        "out other": ("outward", ("middle back",)),
+    }
+
+    def __init__(self, routes, place, part):
+        self.routes = routes
+        self.inner = place.inner
+        self.kept, self.given = halves(part, place.upper_line)
+        self.total = None
+
+    def value(self, hop, got):
+        if hop == "in given":
+            return self.given
+        if hop == "in kept":
+            return self.kept
+        if hop == "middle":
+            return add_up(self.given, got["in given"])
+        if hop == "side":
+            self.kept = add_up(add_up(self.kept, got["in kept"]), got["middle"])
+            return self.kept
+        if hop == "out other":
+            return got["middle back"]
+        if self.total is None:
+            self.total = add_up(self.kept, got["side"])
+            for pairs in self.routes.far:
+                self.total = add_up(self.total, send(self.total, pairs))
+        return self.total
+
+    def pieces(self, got):
+        return (
+            jnp.where(self.inner, self.total, got["out"]),
+            jnp.where(self.inner, got["middle back"], got["out other"]),
+        )
+
+
+def plan(experts):
+    hops = {}
+    for expert in range(experts):
+        for kind in (LineFirst, SideFirst):
+            for name, (link, needs) in kind.hops.items():
+                needed = [(expert, kind, need) for need in needs]
+                hops[expert, kind, name] = (link.replace("inner_", ""), needed)
+
+    def length(hop):
+        return 1 + max([length(h) for h in hops if hop in hops[h][1]], default=0)
+
+    waiting = sorted(hops, key=lambda hop: (hop[0], -length(hop)))
+    slot_of = {}
+    slots = []
+    while waiting:
+        now = len(slots)
+        taken = {}
+        for hop in waiting:
+            link, needed = hops[hop]
+            in_time = hop[0] * 2 <= now and all(slot_of.get(h, now) < now for h in needed)
+            if link not in taken and in_time:
+                taken[link] = hop
+        for hop in taken.values():
+            slot_of[hop] = now
+            waiting.remove(hop)
+        slots.append(list(taken.values()))
+    return slots
+
+
+class Place:
+    def __init__(self, index):
+        line = index >> 1 & 3
+        self.side = index & 1
+        self.upper_line = line >> 1
+        self.inner = (line == 1) | (line == 2)
 
 
 def shards(grad, momentum, placement):
     local_count, row_count, columns = grad.shape
-    dp_count = lax.axis_size("dp")
     group_count = lax.axis_size("expert")
-    routes = Routes(dp_count)
+    routes = Routes(lax.axis_size("dp"))
     my_group = lax.axis_index("expert")
-    my_index = lax.axis_index("dp")
-    side = my_index & 1
-    line = my_index >> 1 & 3
-    upper_line = line >> 1
-    inner = (line == 1) | (line == 2)
+    my_place = Place(lax.axis_index("dp"))
 
     slot_ids = lax.iota(jnp.int32, local_count)
     moves = placement.reshape(group_count, local_count)
@@ -287,45 +401,113 @@
         new_slot = jnp.sum(jnp.where(chosen, row % local_count, 0))
         return old_slot, new_slot
 
-    momentum_new = None
-    outgoing = []
-    squares = jnp.zeros((group_count, local_count), jnp.float32)
-    for step in range(group_count):
-        old_slot, _ = route(my_group, my_group ^ step)
-        momentum_new, moved, sums = momentum_step(
-            old_slot.reshape(1), grad, momentum, momentum_new
-        )
-        outgoing.append(moved)
-        squares = squares.at[my_group, old_slot].add(jnp.sum(sums))
-    squares = lax.psum(squares, ("dp", "expert"))
-    factors = 0.5 * math.sqrt(columns) / jnp.sqrt(squares + 1e-06)
-
-    owned = [outgoing[0]]
-    for step in range(1, group_count):
-        pairs = [(group, group ^ step) for group in range(group_count)]
-        owned.append(lax.ppermute(outgoing[step], "expert", pairs))
-
     places = jnp.array(block_places(columns), jnp.int32) * BLOCK
     quarter = places.shape[0] // 4
     quarters = places.reshape(4, quarter, 2)
-    order = jnp.stack([side, 1 - side, 2 + upper_line, 3 - upper_line])
+    order = jnp.stack(
+        [my_place.side, 1 - my_place.side, 2 + my_place.upper_line, 3 - my_place.upper_line]
+    )
     my_places = jnp.take(quarters, order, axis=0).reshape(4 * quarter, 2).T
 
-    sums = []
-    for step in range(group_count):
-        first, second = gram_step(owned[step])
-        pieces = sum_side_first(first, routes, side, inner)
-        pieces += sum_line_first(second, routes, upper_line, inner)
-        sums.append(pieces)
-
+    distances = list(range(group_count - 1, -1, -1))
+    slots = plan(group_count)
+    first_slot = [
+        min(s for s, hops in enumerate(slots) if any(h[0] == e for h in hops))
+        for e in range(group_count)
+    ]
+    last_slot = [
+        max(s for s, hops in enumerate(slots) if any(h[0] == e for h in hops))
+        for e in range(group_count)
+    ]
+    momentum_new = None
     update = None
-    for step in range(group_count):
-        group = my_group ^ step
-        old_slot, new_slot = route(group, my_group)
-        factor = lax.dynamic_slice(factors, (group, old_slot), (1, 1)).reshape(1)
-        update = update_step(
-            new_slot.reshape(1), my_places, factor, owned[step], sums[step], update, local_count
-        )
+    factors = None
+    moved, partial_squares, chains, got, leaving = {}, {}, {}, {}, {}
+    arrivals = []
+    due = {now: [] for now in range(len(slots) + 8)}
+
+    def after_arrivals(*values):
+        return lax.optimization_barrier((values, arrivals))[0]
+
+    def take_momentum(e, limit):
+        nonlocal momentum_new
+        old_slot, _ = route(my_group, my_group ^ distances[e])
+        (old_slot,) = after_arrivals(old_slot.reshape(1))
+        momentum_new, moved[e], sums = momentum_step(old_slot, grad, momentum, momentum_new)
+        partial_squares[e] = jnp.sum(sums)
+        due[limit].append(sums)
+
+    def take_gram(e, limit):
+        (rows,) = after_arrivals(moved[e])
+        first, second = gram_step(rows)
+        chains[e, SideFirst] = SideFirst(routes, my_place, first)
+        chains[e, LineFirst] = LineFirst(routes, my_place, second)
+        got[e, SideFirst], got[e, LineFirst] = {}, {}
+        due[limit].append(second)
+
+    def take_update(e, limit):
+        nonlocal update
+        pieces = chains[e, SideFirst].pieces(got[e, SideFirst])
+        pieces += chains[e, LineFirst].pieces(got[e, LineFirst])
+        pieces = after_arrivals(*pieces)
+        new_slot = route(my_group ^ distances[e], my_group)[1].reshape(1)
+        factor = factors[e].reshape(1)
+        if distances[e] == 0:
+            update = update_step(
+                new_slot, my_places, factor, moved[e], pieces, update, local_count
+            )
+            return
+        here = jnp.zeros((1,), jnp.int32)
+        mine = update_step(here, my_places, factor, moved[e], pieces)
+        due[limit].append(mine)
+        pairs = [(g, g ^ distances[e]) for g in range(group_count)]
+        arrived = lax.ppermute(mine, "expert", pairs)
+        leaving[e] = new_slot, arrived
+        due[limit + TRAVEL].append(arrived)
+
+    def take_place(e, limit):
+        nonlocal update
+        new_slot, arrived = leaving.pop(e)
+        (new_slot,) = after_arrivals(new_slot)
+        update = place_step(new_slot, arrived, update, local_count)
+        due[limit].append(update)
+
+    take_momentum(0, 0)
+    take_gram(0, 0)
+    swaps = None
+    for now, hops in enumerate(slots):
+        values = [chains[e, kind].value(name, got[e, kind]) for e, kind, name in hops]
+        values = lax.optimization_barrier((values, arrivals, due[now]))[0]
+        if now + 1 < group_count:
+            take_momentum(now + 1, now + 1)
+        for e in range(1, group_count):
+            if first_slot[e] == now + 2 or (now == 0 and first_slot[e] < 2):
+                take_gram(e, now + 1)
+        for e in list(leaving):
+            if last_slot[e] + 2 + TRAVEL == now:
+                take_place(e, now + 1)
+        for e in range(group_count - 1):
+            if last_slot[e] + 1 == now:
+                take_update(e, now + 1)
+        arrivals = []
+        for (e, kind, name), value in zip(hops, values):
+            arrival = send(value, getattr(routes, kind.hops[name][0]))
+            got[e, kind][name] = arrival
+            arrivals.append(arrival)
+        if now + 1 == group_count:
+            small = jnp.stack([partial_squares[e] for e in range(group_count)])
+            swaps = list(routes.swaps)
+            at_once = -(-len(swaps) // 3)
+        if swaps:
+            for _ in range(min(at_once, len(swaps))):
+                arrival = send(small, swaps.pop())
+                small = small + arrival
+                arrivals.append(arrival)
+            if not swaps:
+                factors = 0.5 * math.sqrt(columns) / jnp.sqrt(small + 1e-06)
+    for e in sorted(leaving):
+        take_place(e, len(slots))
+    take_update(group_count - 1, len(slots))
     return momentum_new, update
 
 

time: 856 us -> 600 us (0.70)
  waiting for transfers between devices: 361 us -> 202 us
  blocking collectives: 131 us -> 0 us
  starting transfers between devices: 87.6 us -> 127 us
  between operations: 23.3 us -> 1.86 us
  Pallas kernels: 174 us -> 187 us
  other arithmetic: 46 us -> 57.6 us
    ppermute x48 -> x51, waiting for transfers between devices: 361 us -> 182 us  [send(): return lax.ppermute(value, 'dp', pairs)]
    psum x1 -> x0, blocking collectives: 131 us -> none  [shards(): squares = lax.psum(squares, ('dp', 'expert'))]
    ppermute x48 -> x51, starting transfers between devices: 85.9 us -> 126 us  [send(): return lax.ppermute(value, 'dp', pairs)]
    ppermute x3, waiting for transfers between devices: 0.01 us -> 19.9 us  [take_update(): arrived = lax.ppermute(mine, 'expert', pairs)]
    pallas_call x0 -> x3, Pallas kernels: none -> 15.2 us  [place_step(): pl.pallas_call(place_kernel, grid_spec=pltpu.PrefetchScalarGridSpec(num_s...]
  transfers between devices with their start and end apart: 51 -> 54, of which waited for: 20 -> 22; matrix products, arithmetic and copies ran while one was open for 7% -> 11% of each run, Pallas kernels for 15% -> 23%
where the time goes in v3:
time: 600 us; the launch traced here: 589 us
  waiting for transfers between devices  202 us (34%)
  Pallas kernels  187 us (31%)
  starting transfers between devices  127 us (21%)
  other arithmetic  57.6 us (10%)
  local copies, waits for them, and re-layouts  14.1 us (2%)
    ppermute x51, waiting for transfers between devices, send(): return lax.ppermute(value, 'dp', pairs)  182 us
    ppermute x51, starting transfers between devices, send(): return lax.ppermute(value, 'dp', pairs)  126 us
    pallas_call x4, Pallas kernels, update_step(): pl.pallas_call(update_kernel, grid_spec=pltpu.PrefetchScalarGridSpec(num_...  89 us
    pallas_call x4, Pallas kernels, momentum_step(): pl.pallas_call(momentum_kernel, grid_spec=pltpu.PrefetchScalarGridSpec(nu...  48.1 us
    pallas_call x4, Pallas kernels, gram_step(): pl.pallas_call(gram_kernel, in_specs=[pl.BlockSpec(memory_space=pltpu.VME...  34.3 us
    convert_element_type x24, other arithmetic, add_up(): (mine.astype(jnp.float32) + arrived.astype(jnp.float32)).astype(jnp.bfloa...  27.2 us
    ppermute x3, waiting for transfers between devices, take_update(): arrived = lax.ppermute(mine, 'expert', pairs)  19.9 us
    pallas_call x3, Pallas kernels, place_step(): pl.pallas_call(place_kernel, grid_spec=pltpu.PrefetchScalarGridSpec(num_s...  15.2 us
  transfers between devices with their start and end apart: 54, of which 22 were waited for; matrix products, arithmetic and copies ran while one was open for 11% of the time, Pallas kernels for 23%

profile of v3, /device:TPU:0, one launch (start us, length us, event | category | flops | bytes accessed | tf_op | source)
XLA Modules:
  0.0 588.8 jit_solution(10661626850821495798)
XLA Ops:
  2.2 11.9 %momentum.4 = (f32[4,896,2048]{2,1,0:T(8,128)}, bf16[896,2048]{1,0:T(8,128)(2,1)}, f32[8,2048]{1,0:T(8,128)}) custom-call(s32[1]{0:T(128)} %bitcast.2.order_ref, bf16[4,896,2048]{2,1,0:T(8,128)(2,1)} %grad_ref.7, f32[4,896,2048]{2,1,0:T(8,128)} %momentum_ref.7), custom_call_target="tpu_custom_call" | custom-call | flops 7340032 | bytes 22020096 | tf_op jit(solution)/shard_map/momentum/pallas_call | solution.py:54
  14.1 8.6 %gram.4 = (bf16[18,256,256]{2,1,0:T(8,128)(2,1)}, bf16[18,256,256]{2,1,0:T(8,128)(2,1)}) custom-call(bf16[896,2048]{1,0:T(8,128)(2,1)} %get-tuple-element.94.rows_ref), custom_call_target="tpu_custom_call" | custom-call | flops 4227858432 | bytes 8388608 | tf_op jit(solution)/shard_map/gram/pallas_call | solution.py:109
  31.6 12.0 %momentum.5 = (f32[4,896,2048]{2,1,0:T(8,128)}, bf16[896,2048]{1,0:T(8,128)(2,1)}, f32[8,2048]{1,0:T(8,128)}) custom-call(s32[1]{0:T(128)} %bitcast.3.order_ref, bf16[4,896,2048]{2,1,0:T(8,128)(2,1)} %grad_ref.7, f32[4,896,2048]{2,1,0:T(8,128)} %momentum_ref.7, f32[4,896,2048]{2,1,0:T(8,128)} %get-tuple-element.100.refs_0_), custom_call_target="tpu_custom_call", output_to_operand_aliasing={{0}: (3, {})} | custom-call | flops 7340032 | bytes 22020096 | tf_op jit(solution)/shard_map/momentum/pallas_call | solution.py:54
  43.6 11.6 %collective-permute-done = bf16[9,256,256]{2,1,0:T(8,128)(2,1)S(1)} collective-permute-done((bf16[9,256,256]{2,1,0:T(8,128)(2,1)S(1)}, bf16[9,256,256]{2,1,0:T(8,128)(2,1)S(1)}, u32[]{:S(2)}, u32[]{:S(2)}) %collective-permute-start) | collective-permute-done | bytes 1179680 | tf_op jit(solution)/shard_map/ppermute | solution.py:265
  62.6 12.2 %momentum.6 = (f32[4,896,2048]{2,1,0:T(8,128)}, bf16[896,2048]{1,0:T(8,128)(2,1)}, f32[8,2048]{1,0:T(8,128)}) custom-call(s32[1]{0:T(128)} %bitcast.4.order_ref, bf16[4,896,2048]{2,1,0:T(8,128)(2,1)} %grad_ref.7, f32[4,896,2048]{2,1,0:T(8,128)} %momentum_ref.7, f32[4,896,2048]{2,1,0:T(8,128)} %get-tuple-element.106.refs_0_), custom_call_target="tpu_custom_call", output_to_operand_aliasing={{0}: (3, {})} | custom-call | flops 7340032 | bytes 22020096 | tf_op jit(solution)/shard_map/momentum/pallas_call | solution.py:54
  75.1 8.5 %gram.5 = (bf16[18,256,256]{2,1,0:T(8,128)(2,1)}, bf16[18,256,256]{2,1,0:T(8,128)(2,1)}) custom-call(bf16[896,2048]{1,0:T(8,128)(2,1)} %get-tuple-element.113.rows_ref), custom_call_target="tpu_custom_call" | custom-call | flops 4227858432 | bytes 8388608 | tf_op jit(solution)/shard_map/gram/pallas_call | solution.py:109
  87.2 9.5 %collective-permute-start.8 = (bf16[9,256,256]{2,1,0:T(8,128)(2,1)S(1)}, bf16[9,256,256]{2,1,0:T(8,128)(2,1)}, u32[]{:S(2)}, u32[]{:S(2)}) collective-permute-start(bf16[9,256,256]{2,1,0:T(8,128)(2,1)S(1)} %add_convert_fusion.24), channel_id=1, source_target_pairs={{0,8},{4,12},{24,16},{28,20},{1,9},{5,13},{25,17},{29,21},{2,10},{... | collective-permute-start | bytes 3538952 | tf_op jit(solution)/shard_map/ppermute | solution.py:265
  100.0 12.0 %momentum.7 = (f32[4,896,2048]{2,1,0:T(8,128)}, bf16[896,2048]{1,0:T(8,128)(2,1)}, f32[8,2048]{1,0:T(8,128)}) custom-call(s32[1]{0:T(128)} %bitcast.1.order_ref, bf16[4,896,2048]{2,1,0:T(8,128)(2,1)} %grad_ref.7, f32[4,896,2048]{2,1,0:T(8,128)} %momentum_ref.7, f32[4,896,2048]{2,1,0:T(8,128)} %get-tuple-element.107.refs_0_), custom_call_target="tpu_custom_call", output_to_operand_aliasing={{0}: (3, {})} | custom-call | flops 7340032 | bytes 22020096 | tf_op jit(solution)/shard_map/momentum/pallas_call | solution.py:54
  112.0 8.6 %gram.6 = (bf16[18,256,256]{2,1,0:T(8,128)(2,1)}, bf16[18,256,256]{2,1,0:T(8,128)(2,1)}) custom-call(bf16[896,2048]{1,0:T(8,128)(2,1)} %get-tuple-element.119.rows_ref), custom_call_target="tpu_custom_call" | custom-call | flops 4227858432 | bytes 8388608 | tf_op jit(solution)/shard_map/gram/pallas_call | solution.py:109
  160.2 8.5 %collective-permute-start.15 = (bf16[9,256,256]{2,1,0:T(8,128)(2,1)}, bf16[9,256,256]{2,1,0:T(8,128)(2,1)}, u32[]{:S(2)}, u32[]{:S(2)}) collective-permute-start(bf16[9,256,256]{2,1,0:T(8,128)(2,1)} %get-tuple-element.128), channel_id=1, source_target_pairs={{0,8},{4,12},{24,16},{28,20},{1,9},{5,13},{25,17},{29,21},{2,10},{... | collective-permute-start | bytes 3538952 | tf_op jit(solution)/shard_map/ppermute | solution.py:265
  208.1 8.5 %gram.7 = (bf16[18,256,256]{2,1,0:T(8,128)(2,1)}, bf16[18,256,256]{2,1,0:T(8,128)(2,1)}) custom-call(bf16[896,2048]{1,0:T(8,128)(2,1)} %get-tuple-element.130.rows_ref), custom_call_target="tpu_custom_call" | custom-call | flops 4227858432 | bytes 8388608 | tf_op jit(solution)/shard_map/gram/pallas_call | solution.py:109
  230.3 10.2 %collective-permute-start.23 = (bf16[9,256,256]{2,1,0:T(8,128)(2,1)S(1)}, bf16[9,256,256]{2,1,0:T(8,128)(2,1)}, u32[]{:S(2)}, u32[]{:S(2)}) collective-permute-start(bf16[9,256,256]{2,1,0:T(8,128)(2,1)S(1)} %get-tuple-element.139), channel_id=1, source_target_pairs={{0,8},{4,12},{24,16},{28,20},{1,9},{5,13},{25,17},{29,21},{2,10},{... | collective-permute-start | bytes 3538952 | tf_op jit(solution)/shard_map/ppermute | solution.py:265
  245.5 22.1 %update.4 = bf16[1,896,2048]{2,1,0:T(8,128)(2,1)} custom-call(s32[1]{0:T(128)} %constant.131.clone.1.slot_ref, s32[2,36]{1,0:T(2,128)} %select_bitcast_fusion.place_ref, f32[1]{0:T(128)} %get-tuple-element.204.factor_ref, bf16[896,2048]{1,0:T(8,128)(2,1)} %get-tuple-element.94.rows_ref, bf16[9,256,256]{2,1,0:T(8,128)(2,1)} %copy-done, ...), custom_call_target="tpu_custom_call" | custom-call | flops 939524096 | bytes 1835008 | tf_op jit(solution)/shard_map/update/pallas_call | solution.py:186
  304.8 12.8 %collective-permute-done.29 = bf16[9,256,256]{2,1,0:T(8,128)(2,1)S(1)} collective-permute-done((bf16[9,256,256]{2,1,0:T(8,128)(2,1)S(1)}, bf16[9,256,256]{2,1,0:T(8,128)(2,1)S(1)}, u32[]{:S(2)}, u32[]{:S(2)}) %collective-permute-start.29) | collective-permute-done | bytes 1179680 | tf_op jit(solution)/shard_map/ppermute | solution.py:265
  326.3 15.6 %collective-permute-start.35 = (bf16[9,256,256]{2,1,0:T(8,128)(2,1)S(1)}, bf16[9,256,256]{2,1,0:T(8,128)(2,1)S(1)}, u32[]{:S(2)}, u32[]{:S(2)}) collective-permute-start(bf16[9,256,256]{2,1,0:T(8,128)(2,1)S(1)} %get-tuple-element.155), channel_id=1, source_target_pairs={{0,8},{4,12},{24,16},{28,20},{1,9},{5,13},{25,17},{29,21},{2,10},{... | collective-permute-start | bytes 3538952 | tf_op jit(solution)/shard_map/ppermute | solution.py:265
  342.7 19.9 %collective-permute-done.36.arrived_ref = bf16[1,896,2048]{2,1,0:T(8,128)(2,1)S(1)} collective-permute-done((bf16[1,896,2048]{2,1,0:T(8,128)(2,1)S(1)}, bf16[1,896,2048]{2,1,0:T(8,128)(2,1)S(1)}, u32[]{:S(2)}, u32[]{:S(2)}) %collective-permute-start.36) | collective-permute-done | bytes 3670048 | tf_op jit(solution)/shard_map/ppermute | solution.py:464
  365.0 9.4 %collective-permute-start.39 = (bf16[9,256,256]{2,1,0:T(8,128)(2,1)S(1)}, bf16[9,256,256]{2,1,0:T(8,128)(2,1)}, u32[]{:S(2)}, u32[]{:S(2)}) collective-permute-start(bf16[9,256,256]{2,1,0:T(8,128)(2,1)S(1)} %get-tuple-element.158), channel_id=1, source_target_pairs={{0,8},{4,12},{24,16},{28,20},{1,9},{5,13},{25,17},{29,21},{2,10},{... | collective-permute-start | bytes 3538952 | tf_op jit(solution)/shard_map/ppermute | solution.py:265
  381.9 22.1 %update.5 = bf16[1,896,2048]{2,1,0:T(8,128)(2,1)} custom-call(s32[1]{0:T(128)} %constant.131.clone.1.slot_ref, s32[2,36]{1,0:T(2,128)} %select_bitcast_fusion.place_ref, f32[1]{0:T(128)} %get-tuple-element.203.factor_ref, bf16[896,2048]{1,0:T(8,128)(2,1)} %get-tuple-element.113.rows_ref, bf16[9,256,256]{2,1,0:T(8,128)(2,1)} %copy-done.1, ...), custom_call_target="tpu_custom_call" | custom-call | flops 939524096 | bytes 1835008 | tf_op jit(solution)/shard_map/update/pallas_call | solution.py:186
  412.3 20.5 %collective-permute-done.40 = bf16[9,256,256]{2,1,0:T(8,128)(2,1)S(1)} collective-permute-done((bf16[9,256,256]{2,1,0:T(8,128)(2,1)S(1)}, bf16[9,256,256]{2,1,0:T(8,128)(2,1)S(1)}, u32[]{:S(2)}, u32[]{:S(2)}) %collective-permute-start.40) | collective-permute-done | bytes 1179680 | tf_op jit(solution)/shard_map/ppermute | solution.py:265
  440.7 27.9 %collective-permute-done.46 = bf16[9,256,256]{2,1,0:T(8,128)(2,1)S(1)} collective-permute-done((bf16[9,256,256]{2,1,0:T(8,128)(2,1)S(1)}, bf16[9,256,256]{2,1,0:T(8,128)(2,1)S(1)}, u32[]{:S(2)}, u32[]{:S(2)}) %collective-permute-start.46) | collective-permute-done | bytes 1179680 | tf_op jit(solution)/shard_map/ppermute | solution.py:265
  473.0 22.1 %update.6 = bf16[1,896,2048]{2,1,0:T(8,128)(2,1)} custom-call(s32[1]{0:T(128)} %constant.131.clone.1.slot_ref, s32[2,36]{1,0:T(2,128)} %select_bitcast_fusion.place_ref, f32[1]{0:T(128)} %get-tuple-element.202.factor_ref, bf16[896,2048]{1,0:T(8,128)(2,1)} %get-tuple-element.119.rows_ref, bf16[9,256,256]{2,1,0:T(8,128)(2,1)} %copy-done.2, ...), custom_call_target="tpu_custom_call" | custom-call | flops 939524096 | bytes 1835008 | tf_op jit(solution)/shard_map/update/pallas_call | solution.py:186
  503.1 20.6 %collective-permute-done.50.refs_1_ = bf16[9,256,256]{2,1,0:T(8,128)(2,1)S(1)} collective-permute-done((bf16[9,256,256]{2,1,0:T(8,128)(2,1)S(1)}, bf16[9,256,256]{2,1,0:T(8,128)(2,1)S(1)}, u32[]{:S(2)}, u32[]{:S(2)}) %collective-permute-start.50) | collective-permute-done | bytes 1179680 | tf_op jit(solution)/shard_map/ppermute | solution.py:265
  532.7 26.8 %collective-permute-done.52 = bf16[9,256,256]{2,1,0:T(8,128)(2,1)S(1)} collective-permute-done((bf16[9,256,256]{2,1,0:T(8,128)(2,1)S(1)}, bf16[9,256,256]{2,1,0:T(8,128)(2,1)S(1)}, u32[]{:S(2)}, u32[]{:S(2)}) %collective-permute-start.52) | collective-permute-done | bytes 1179680 | tf_op jit(solution)/shard_map/ppermute | solution.py:265
  565.7 22.6 %update.7 = bf16[4,896,2048]{2,1,0:T(8,128)(2,1)} custom-call(s32[1]{0:T(128)} %bitcast.5.slot_ref, s32[2,36]{1,0:T(2,128)} %select_bitcast_fusion.place_ref, f32[1]{0:T(128)} %get-tuple-element.205.factor_ref, bf16[896,2048]{1,0:T(8,128)(2,1)} %get-tuple-element.130.rows_ref, bf16[9,256,256]{2,1,0:T(8,128)(2,1)} %copy-done.3, ...), custom_call_target="tpu_custom_call", output_to_operand_aliasing={{}: (8, {})} | custom-call | flops 939524096 | bytes 1835008 | tf_op jit(solution)/shard_map/update/pallas_call | solution.py:186
  (204 shorter events, 222.2 us)
Async XLA Ops:
  25.0 30.1 %collective-permute-start = (bf16[9,256,256]{2,1,0:T(8,128)(2,1)S(1)}, bf16[9,256,256]{2,1,0:T(8,128)(2,1)S(1)}, u32[]{:S(2)}, u32[]{:S(2)}) collective-permute-start(bf16[9,256,256]{2,1,0:T(8,128)(2,1)S(1)} %get-tuple-element.98), channel_id=1, source_target_pairs={{0,8},{4,12},{24,16},{28,20},{1,9},{5,13},{25,17},{29,21},{2,10},{... | collective-permute-start | bytes 3538952 | tf_op jit(solution)/shard_map/ppermute | solution.py:265
  86.4 34.2 %collective-permute-start.7 = (bf16[9,256,256]{2,1,0:T(8,128)(2,1)S(1)}, bf16[9,256,256]{2,1,0:T(8,128)(2,1)S(1)}, u32[]{:S(2)}, u32[]{:S(2)}) collective-permute-start(bf16[9,256,256]{2,1,0:T(8,128)(2,1)S(1)} %add_convert_fusion.25), channel_id=1, source_target_pairs={{8,12},{12,8},{16,20},{20,16},{9,13},{13,9},{17,21},{21,17},{10,14... | collective-permute-start | bytes 3538952 | tf_op jit(solution)/shard_map/ppermute | solution.py:265
  87.2 33.8 %collective-permute-start.8 = (bf16[9,256,256]{2,1,0:T(8,128)(2,1)S(1)}, bf16[9,256,256]{2,1,0:T(8,128)(2,1)}, u32[]{:S(2)}, u32[]{:S(2)}) collective-permute-start(bf16[9,256,256]{2,1,0:T(8,128)(2,1)S(1)} %add_convert_fusion.24), channel_id=1, source_target_pairs={{0,8},{4,12},{24,16},{28,20},{1,9},{5,13},{25,17},{29,21},{2,10},{... | collective-permute-start | bytes 3538952 | tf_op jit(solution)/shard_map/ppermute | solution.py:265
  124.3 29.5 %collective-permute-start.10 = (bf16[9,256,256]{2,1,0:T(8,128)(2,1)S(1)}, bf16[9,256,256]{2,1,0:T(8,128)(2,1)}, u32[]{:S(2)}, u32[]{:S(2)}) collective-permute-start(bf16[9,256,256]{2,1,0:T(8,128)(2,1)S(1)} %add_convert_fusion.23), channel_id=1, source_target_pairs={{8,0},{12,4},{16,24},{20,28},{9,1},{13,5},{17,25},{21,29},{10,2},{... | collective-permute-start | bytes 3538952 | tf_op jit(solution)/shard_map/ppermute | solution.py:265
  125.6 28.2 %collective-permute-start.11 = (bf16[9,256,256]{2,1,0:T(8,128)(2,1)S(1)}, bf16[9,256,256]{2,1,0:T(8,128)(2,1)}, u32[]{:S(2)}, u32[]{:S(2)}) collective-permute-start(bf16[9,256,256]{2,1,0:T(8,128)(2,1)S(1)} %get-tuple-element.124), channel_id=1, source_target_pairs={{0,8},{4,12},{24,16},{28,20},{1,9},{5,13},{25,17},{29,21},{2,10},{... | collective-permute-start | bytes 3538952 | tf_op jit(solution)/shard_map/ppermute | solution.py:265
  158.5 30.9 %collective-permute-start.13 = (bf16[9,256,256]{2,1,0:T(8,128)(2,1)S(1)}, bf16[9,256,256]{2,1,0:T(8,128)(2,1)}, u32[]{:S(2)}, u32[]{:S(2)}) collective-permute-start(bf16[9,256,256]{2,1,0:T(8,128)(2,1)S(1)} %add_convert_fusion.23), channel_id=1, source_target_pairs={{8,16},{12,20},{16,8},{20,12},{9,17},{13,21},{17,9},{21,13},{10,18... | collective-permute-start | bytes 3538952 | tf_op jit(solution)/shard_map/ppermute | solution.py:265
  160.2 29.2 %collective-permute-start.15 = (bf16[9,256,256]{2,1,0:T(8,128)(2,1)}, bf16[9,256,256]{2,1,0:T(8,128)(2,1)}, u32[]{:S(2)}, u32[]{:S(2)}) collective-permute-start(bf16[9,256,256]{2,1,0:T(8,128)(2,1)} %get-tuple-element.128), channel_id=1, source_target_pairs={{0,8},{4,12},{24,16},{28,20},{1,9},{5,13},{25,17},{29,21},{2,10},{... | collective-permute-start | bytes 3538952 | tf_op jit(solution)/shard_map/ppermute | solution.py:265
  226.2 41.4 %collective-permute-start.21 = (bf16[9,256,256]{2,1,0:T(8,128)(2,1)S(1)}, bf16[9,256,256]{2,1,0:T(8,128)(2,1)}, u32[]{:S(2)}, u32[]{:S(2)}) collective-permute-start(bf16[9,256,256]{2,1,0:T(8,128)(2,1)S(1)} %add_convert_fusion.17), channel_id=1, source_target_pairs={{8,12},{12,8},{16,20},{20,16},{9,13},{13,9},{17,21},{21,17},{10,14... | collective-permute-start | bytes 3538952 | tf_op jit(solution)/shard_map/ppermute | solution.py:265
  227.9 41.2 %collective-permute-start.22 = (bf16[9,256,256]{2,1,0:T(8,128)(2,1)S(1)}, bf16[9,256,256]{2,1,0:T(8,128)(2,1)}, u32[]{:S(2)}, u32[]{:S(2)}) collective-permute-start(bf16[9,256,256]{2,1,0:T(8,128)(2,1)S(1)} %add_convert_fusion.16), channel_id=1, source_target_pairs={{8,16},{12,20},{16,8},{20,12},{9,17},{13,21},{17,9},{21,13},{10,18... | collective-permute-start | bytes 3538952 | tf_op jit(solution)/shard_map/ppermute | solution.py:265
  230.3 40.6 %collective-permute-start.23 = (bf16[9,256,256]{2,1,0:T(8,128)(2,1)S(1)}, bf16[9,256,256]{2,1,0:T(8,128)(2,1)}, u32[]{:S(2)}, u32[]{:S(2)}) collective-permute-start(bf16[9,256,256]{2,1,0:T(8,128)(2,1)S(1)} %get-tuple-element.139), channel_id=1, source_target_pairs={{0,8},{4,12},{24,16},{28,20},{1,9},{5,13},{25,17},{29,21},{2,10},{... | collective-permute-start | bytes 3538952 | tf_op jit(solution)/shard_map/ppermute | solution.py:265
  281.0 81.6 %collective-permute-start.36 = (bf16[1,896,2048]{2,1,0:T(8,128)(2,1)S(1)}, bf16[1,896,2048]{2,1,0:T(8,128)(2,1)S(1)}, u32[]{:S(2)}, u32[]{:S(2)}) collective-permute-start(bf16[1,896,2048]{2,1,0:T(8,128)(2,1)S(1)} %copy-done.5), channel_id=1, source_target_pairs={{0,3},{1,2},{2,1},{3,0},{4,7},{5,6},{6,5},{7,4},{8,11},{9,10},{10,... | collective-permute-start | bytes 11010056 | tf_op jit(solution)/shard_map/ppermute | solution.py:464
  325.0 37.6 %collective-permute-start.34 = (bf16[9,256,256]{2,1,0:T(8,128)(2,1)S(1)}, bf16[9,256,256]{2,1,0:T(8,128)(2,1)S(1)}, u32[]{:S(2)}, u32[]{:S(2)}) collective-permute-start(bf16[9,256,256]{2,1,0:T(8,128)(2,1)S(1)} %collective-permute-done.27), channel_id=1, source_target_pairs={{8,0},{12,4},{16,24},{20,28},{9,1},{13,5},{17,25},{21,29},{10,2},{... | collective-permute-start | bytes 3538952 | tf_op jit(solution)/shard_map/ppermute | solution.py:265
  326.3 36.3 %collective-permute-start.35 = (bf16[9,256,256]{2,1,0:T(8,128)(2,1)S(1)}, bf16[9,256,256]{2,1,0:T(8,128)(2,1)S(1)}, u32[]{:S(2)}, u32[]{:S(2)}) collective-permute-start(bf16[9,256,256]{2,1,0:T(8,128)(2,1)S(1)} %get-tuple-element.155), channel_id=1, source_target_pairs={{0,8},{4,12},{24,16},{28,20},{1,9},{5,13},{25,17},{29,21},{2,10},{... | collective-permute-start | bytes 3538952 | tf_op jit(solution)/shard_map/ppermute | solution.py:265
  362.6 41.7 %collective-permute-start.37 = (bf16[9,256,256]{2,1,0:T(8,128)(2,1)S(1)}, bf16[9,256,256]{2,1,0:T(8,128)(2,1)}, u32[]{:S(2)}, u32[]{:S(2)}) collective-permute-start(bf16[9,256,256]{2,1,0:T(8,128)(2,1)S(1)} %add_convert_fusion.6), channel_id=1, source_target_pairs={{8,0},{12,4},{16,24},{20,28},{9,1},{13,5},{17,25},{21,29},{10,2},{... | collective-permute-start | bytes 3538952 | tf_op jit(solution)/shard_map/ppermute | solution.py:265
  364.3 41.5 %collective-permute-start.38 = (bf16[9,256,256]{2,1,0:T(8,128)(2,1)S(1)}, bf16[9,256,256]{2,1,0:T(8,128)(2,1)S(1)}, u32[]{:S(2)}, u32[]{:S(2)}) collective-permute-start(bf16[9,256,256]{2,1,0:T(8,128)(2,1)S(1)} %add_convert_fusion.7), channel_id=1, source_target_pairs={{8,16},{12,20},{16,8},{20,12},{9,17},{13,21},{17,9},{21,13},{10,18... | collective-permute-start | bytes 3538952 | tf_op jit(solution)/shard_map/ppermute | solution.py:265
  365.0 40.8 %collective-permute-start.39 = (bf16[9,256,256]{2,1,0:T(8,128)(2,1)S(1)}, bf16[9,256,256]{2,1,0:T(8,128)(2,1)}, u32[]{:S(2)}, u32[]{:S(2)}) collective-permute-start(bf16[9,256,256]{2,1,0:T(8,128)(2,1)S(1)} %get-tuple-element.158), channel_id=1, source_target_pairs={{0,8},{4,12},{24,16},{28,20},{1,9},{5,13},{25,17},{29,21},{2,10},{... | collective-permute-start | bytes 3538952 | tf_op jit(solution)/shard_map/ppermute | solution.py:265
  407.9 29.0 %collective-permute-start.42 = (bf16[9,256,256]{2,1,0:T(8,128)(2,1)S(1)}, bf16[9,256,256]{2,1,0:T(8,128)(2,1)S(1)}, u32[]{:S(2)}, u32[]{:S(2)}) collective-permute-start(bf16[9,256,256]{2,1,0:T(8,128)(2,1)S(1)} %add_convert_fusion.7), channel_id=1, source_target_pairs={{8,0},{12,4},{16,24},{20,28},{9,1},{13,5},{17,25},{21,29},{10,2},{... | collective-permute-start | bytes 3538952 | tf_op jit(solution)/shard_map/ppermute | solution.py:265
  409.2 27.8 %collective-permute-start.43 = (bf16[9,256,256]{2,1,0:T(8,128)(2,1)S(1)}, bf16[9,256,256]{2,1,0:T(8,128)(2,1)S(1)}, u32[]{:S(2)}, u32[]{:S(2)}) collective-permute-start(bf16[9,256,256]{2,1,0:T(8,128)(2,1)S(1)} %broadcast_select_fusion.7.refs_0_), channel_id=1, source_target_pairs={{0,4},{4,0},{8,12},{12,8},{16,20},{20,16},{24,28},{28,24},{1,5},{5... | collective-permute-start | bytes 3538952 | tf_op jit(solution)/shard_map/ppermute | solution.py:265
  409.9 85.5 %collective-permute-start.49 = (bf16[1,896,2048]{2,1,0:T(8,128)(2,1)}, bf16[1,896,2048]{2,1,0:T(8,128)(2,1)}, u32[]{:S(2)}, u32[]{:S(2)}) collective-permute-start(bf16[1,896,2048]{2,1,0:T(8,128)(2,1)} %update.5), channel_id=1, source_target_pairs={{0,2},{1,3},{2,0},{3,1},{4,6},{5,7},{6,4},{7,5},{8,10},{9,11},{10,... | collective-permute-start | bytes 11010056 | tf_op jit(solution)/shard_map/ppermute | solution.py:464
  438.5 30.1 %collective-permute-start.46 = (bf16[9,256,256]{2,1,0:T(8,128)(2,1)S(1)}, bf16[9,256,256]{2,1,0:T(8,128)(2,1)S(1)}, u32[]{:S(2)}, u32[]{:S(2)}) collective-permute-start(bf16[9,256,256]{2,1,0:T(8,128)(2,1)S(1)} %collective-permute-done.38), channel_id=1, source_target_pairs={{8,0},{12,4},{16,24},{20,28},{9,1},{13,5},{17,25},{21,29},{10,2},{... | collective-permute-start | bytes 3538952 | tf_op jit(solution)/shard_map/ppermute | solution.py:265
  495.1 65.6 %collective-permute-start.53 = (bf16[1,896,2048]{2,1,0:T(8,128)(2,1)}, bf16[1,896,2048]{2,1,0:T(8,128)(2,1)}, u32[]{:S(2)}, u32[]{:S(2)}) collective-permute-start(bf16[1,896,2048]{2,1,0:T(8,128)(2,1)} %update.6), channel_id=1, source_target_pairs={{0,1},{1,0},{2,3},{3,2},{4,5},{5,4},{6,7},{7,6},{8,9},{9,8},{10,11... | collective-permute-start | bytes 11010056 | tf_op jit(solution)/shard_map/ppermute | solution.py:464
  495.3 28.4 %collective-permute-start.50 = (bf16[9,256,256]{2,1,0:T(8,128)(2,1)S(1)}, bf16[9,256,256]{2,1,0:T(8,128)(2,1)S(1)}, u32[]{:S(2)}, u32[]{:S(2)}) collective-permute-start(bf16[9,256,256]{2,1,0:T(8,128)(2,1)S(1)} %broadcast_select_fusion.4.refs_0_), channel_id=1, source_target_pairs={{0,4},{4,0},{8,12},{12,8},{16,20},{20,16},{24,28},{28,24},{1,5},{5... | collective-permute-start | bytes 3538952 | tf_op jit(solution)/shard_map/ppermute | solution.py:265
  496.9 33.2 %collective-permute-start.51 = (bf16[9,256,256]{2,1,0:T(8,128)(2,1)S(1)}, bf16[9,256,256]{2,1,0:T(8,128)(2,1)S(1)}, u32[]{:S(2)}, u32[]{:S(2)}) collective-permute-start(bf16[9,256,256]{2,1,0:T(8,128)(2,1)S(1)} %add_convert_fusion), channel_id=1, source_target_pairs={{8,0},{12,4},{16,24},{20,28},{9,1},{13,5},{17,25},{21,29},{10,2},{... | collective-permute-start | bytes 3538952 | tf_op jit(solution)/shard_map/ppermute | solution.py:265
  530.0 29.5 %collective-permute-start.52 = (bf16[9,256,256]{2,1,0:T(8,128)(2,1)S(1)}, bf16[9,256,256]{2,1,0:T(8,128)(2,1)S(1)}, u32[]{:S(2)}, u32[]{:S(2)}) collective-permute-start(bf16[9,256,256]{2,1,0:T(8,128)(2,1)S(1)} %collective-permute-done.48), channel_id=1, source_target_pairs={{8,0},{12,4},{16,24},{20,28},{9,1},{13,5},{17,25},{21,29},{10,2},{... | collective-permute-start | bytes 3538952 | tf_op jit(solution)/shard_map/ppermute | solution.py:265
  (51 other events, 834.6 us)

commit v4 on v3

--- a/solution.py
+++ b/solution.py
@@ -10,8 +10,8 @@
 
 D = 7168
 BLOCK = 256
-TRAVEL = 3
 VMEM_BYTES = 56 * 2**20
+SMALL_COST = pl.CostEstimate(flops=2**20, bytes_accessed=2**10, transcendentals=0)
 
 
 def row_block(rows, most):
@@ -70,9 +70,7 @@
         ],
         input_output_aliases=aliases,
         compiler_params=pltpu.CompilerParams(vmem_limit_bytes=VMEM_BYTES),
-        cost_estimate=pl.CostEstimate(
-            flops=4 * rows * columns, bytes_accessed=12 * rows * columns, transcendentals=0
-        ),
+        cost_estimate=SMALL_COST,
         name="momentum",
     )(*operands)
 
@@ -82,43 +80,59 @@
     return [(i, j) for i in range(count) for j in range(i, count)]
 
 
-def gram_kernel(rows_ref, first_ref, second_ref):
+def gram_kernel(upper_ref, rows_ref, *refs):
+    outputs, halves, sems = refs[:4], refs[4:6], refs[6]
     columns = rows_ref.shape[1]
     count = columns // BLOCK
-    half = first_ref.shape[0]
+    quarter = halves[0].shape[1]
+    copies = []
     place = 0
     for i in range(count):
         turned = rows_ref[:, i * BLOCK : (i + 1) * BLOCK].T
         for j in range(i, count):
-            block = jnp.dot(
+            half, inside = divmod(place, 2 * quarter)
+            part, slot = divmod(inside, quarter)
+            halves[half][part, slot] = jnp.dot(
                 turned,
                 rows_ref[:, j * BLOCK : (j + 1) * BLOCK],
                 preferred_element_type=jnp.float32,
             ).astype(jnp.bfloat16)
-            if place < half:
-                first_ref[place] = block
-            else:
-                second_ref[place - half] = block
             place += 1
-
-
-def gram_step(moved):
+            if place % (2 * quarter) == 0:
+                upper = upper_ref[half]
+                for given in range(2):
+                    number = 2 * half + given
+                    source = upper if given == 0 else 1 - upper
+                    copy = pltpu.make_async_copy(
+                        halves[half].at[source], outputs[number], sems.at[number]
+                    )
+                    copy.start()
+                    copies.append(copy)
+    for copy in copies:
+        copy.wait()
+
+
+def gram_step(uppers, moved):
     rows, columns = moved.shape
-    half = len(block_places(columns)) // 2
-    part = jax.ShapeDtypeStruct((half, BLOCK, BLOCK), jnp.bfloat16)
+    quarter = len(block_places(columns)) // 4
+    part = jax.ShapeDtypeStruct((quarter, BLOCK, BLOCK), jnp.bfloat16)
     return pl.pallas_call(
         gram_kernel,
-        in_specs=[pl.BlockSpec(memory_space=pltpu.VMEM)],
-        out_specs=[pl.BlockSpec(memory_space=pltpu.VMEM)] * 2,
-        out_shape=[part, part],
+        in_specs=[
+            pl.BlockSpec(memory_space=pltpu.SMEM),
+            pl.BlockSpec(memory_space=pltpu.VMEM),
+        ],
+        out_specs=[pl.BlockSpec(memory_space=pl.ANY)] * 4,
+        out_shape=[part] * 4,
+        scratch_shapes=[
+            pltpu.VMEM((2, quarter, BLOCK, BLOCK), jnp.bfloat16),
+            pltpu.VMEM((2, quarter, BLOCK, BLOCK), jnp.bfloat16),
+            pltpu.SemaphoreType.DMA((4,)),
+        ],
         compiler_params=pltpu.CompilerParams(vmem_limit_bytes=VMEM_BYTES),
-        cost_estimate=pl.CostEstimate(
-            flops=4 * half * BLOCK * BLOCK * rows,
-            bytes_accessed=2 * rows * columns + 4 * half * BLOCK * BLOCK,
-            transcendentals=0,
-        ),
+        cost_estimate=SMALL_COST,
         name="gram",
-    )(moved)
+    )(uppers, moved)
 
 
 def times_gram(left_ref, gram_ref, j):
@@ -199,9 +213,7 @@
         out_shape=jax.ShapeDtypeStruct((count, rows, columns), jnp.bfloat16),
         input_output_aliases=aliases,
         compiler_params=pltpu.CompilerParams(vmem_limit_bytes=VMEM_BYTES),
-        cost_estimate=pl.CostEstimate(
-            flops=rows * columns * columns // 4, bytes_accessed=rows * columns, transcendentals=0
-        ),
+        cost_estimate=SMALL_COST,
         name="update",
     )(*operands)
 
@@ -231,9 +243,7 @@
         out_shape=jax.ShapeDtypeStruct((count, rows, columns), jnp.bfloat16),
         input_output_aliases=aliases,
         compiler_params=pltpu.CompilerParams(vmem_limit_bytes=VMEM_BYTES),
-        cost_estimate=pl.CostEstimate(
-            flops=0, bytes_accessed=4 * rows * columns, transcendentals=0
-        ),
+        cost_estimate=SMALL_COST,
         name="place",
     )(*operands)
 
@@ -265,26 +275,18 @@
     return lax.ppermute(value, "dp", pairs)
 
 
-def halves(part, upper):
-    count = part.shape[0] // 2
-    kept = lax.dynamic_slice_in_dim(part, upper * count, count)
-    given = lax.dynamic_slice_in_dim(part, (1 - upper) * count, count)
-    return kept, given
-
-
 class SideFirst:
     hops = {
-        "side": ("side", ()),
-        "in": ("inward", ("side",)),
-        "middle": ("middle", ("in",)),
-        "out": ("outward", ("middle",)),
-        "gather": ("side", ("out",)),
+        "side": ("side", (), 0),
+        "in": ("inward", ("side",), 1),
+        "middle": ("middle", ("in",), 1),
+        "out": ("outward", ("middle",), 1),
+        "gather": ("side", ("out",), 1),
     }
 
-    def __init__(self, routes, place, part):
-        self.routes = routes
-        self.inner = place.inner
-        self.kept, self.given = halves(part, place.side)
+    def __init__(self, routes, place, kept, given):
+        self.routes, self.inner = routes, place.inner
+        self.kept, self.given = kept, given
 
     def value(self, hop, got):
         if hop == "side":
@@ -307,19 +309,18 @@
 
 class LineFirst:
     hops = {
-        "in given": ("inward", ()),
-        "in kept": ("inward", ()),
-        "middle": ("middle", ("in given",)),
-        "side": ("inner_side", ("in kept", "middle")),
-        "middle back": ("middle", ("side",)),
-        "out": ("outward", ("side",)),
-        "out other": ("outward", ("middle back",)),
+        "in given": ("inward", (), 0),
+        "in kept": ("inward", (), 0),
+        "middle": ("middle", ("in given",), 1),
+        "side": ("inner_side", ("in kept", "middle"), 2),
+        "middle back": ("middle", ("side",), 1),
+        "out": ("outward", ("side",), 0),
+        "out other": ("outward", ("middle back",), 0),
     }
 
-    def __init__(self, routes, place, part):
-        self.routes = routes
-        self.inner = place.inner
-        self.kept, self.given = halves(part, place.upper_line)
+    def __init__(self, routes, place, kept, given):
+        self.routes, self.inner = routes, place.inner
+        self.kept, self.given = kept, given
         self.total = None
 
     def value(self, hop, got):
@@ -348,32 +349,82 @@
 
 
 def plan(experts):
+    transfer, latency, issue, pass_over = 23.3, 3.0, 1.5, 1.6
+    takes = {"momentum": 12.0, "gram": 9.0, "update": 23.0, "place": 5.0}
+    swaps_take, near, far = 30.0, 20.0, 78.0
     hops = {}
     for expert in range(experts):
         for kind in (LineFirst, SideFirst):
-            for name, (link, needs) in kind.hops.items():
+            for name, (link, needs, passes) in kind.hops.items():
                 needed = [(expert, kind, need) for need in needs]
-                hops[expert, kind, name] = (link.replace("inner_", ""), needed)
+                hops[expert, kind, name] = (link.replace("inner_", ""), needed, passes)
+    last_hops = {}
 
     def length(hop):
-        return 1 + max([length(h) for h in hops if hop in hops[h][1]], default=0)
-
-    waiting = sorted(hops, key=lambda hop: (hop[0], -length(hop)))
-    slot_of = {}
-    slots = []
-    while waiting:
-        now = len(slots)
-        taken = {}
-        for hop in waiting:
-            link, needed = hops[hop]
-            in_time = hop[0] * 2 <= now and all(slot_of.get(h, now) < now for h in needed)
-            if link not in taken and in_time:
-                taken[link] = hop
-        for hop in taken.values():
-            slot_of[hop] = now
-            waiting.remove(hop)
-        slots.append(list(taken.values()))
-    return slots
+        if hop not in last_hops:
+            later = [length(h) for h in hops if hop in hops[h][1]]
+            last_hops[hop] = 1 + max(later, default=0)
+        return last_hops[hop]
+
+    first_choice = sorted(hops, key=lambda hop: (hop[0], -length(hop)))
+    order = []
+    now = 0.0
+    count = dict.fromkeys(takes, 0)
+    arrival = {}
+    queues = {}
+    update_arrival = {}
+    far_free = 0.0
+
+    def do(kernel):
+        nonlocal now
+        order.append((kernel, count[kernel]))
+        count[kernel] += 1
+        now += takes[kernel]
+
+    def next_hop():
+        for hop in first_choice:
+            link, needed, _ = hops[hop]
+            queued = sum(time > now for time in queues.setdefault(link, []))
+            if hop[0] < count["gram"] and hop not in arrival and queued < 2:
+                if all(arrival.get(need, math.inf) <= now for need in needed):
+                    return hop
+        return None
+
+    do("momentum")
+    do("gram")
+    while count["update"] < experts:
+        hop = next_hop()
+        updating = count["update"]
+        last = updating == experts - 1
+        mine = [h for h in hops if h[0] == updating]
+        whole = all(arrival.get(h, math.inf) <= now for h in mine)
+        if hop is not None:
+            link, _, passes = hops[hop]
+            order.append(("hop", hop))
+            now += issue + passes * pass_over
+            queue = queues[link]
+            queue.append(max([now + 1, *queue[-1:]]) + transfer)
+            arrival[hop] = queue[-1] + latency
+        elif count["gram"] < count["momentum"]:
+            do("gram")
+        elif count["momentum"] < experts:
+            do("momentum")
+            if count["momentum"] == experts:
+                order.append(("swaps", 0))
+                squares_arrival = now + swaps_take
+        elif whole and squares_arrival <= now and (not last or count["place"] == updating):
+            do("update")
+            if updating < experts - 2:
+                far_free = max(now, far_free) + far
+                update_arrival[updating] = far_free
+            else:
+                update_arrival[updating] = now + near
+        elif update_arrival.get(count["place"], math.inf) <= now:
+            do("place")
+        else:
+            times = [*arrival.values(), *update_arrival.values(), squares_arrival]
+            now = min(time for time in times if time > now)
+    return order
 
 
 class Place:
@@ -409,105 +460,68 @@
     )
     my_places = jnp.take(quarters, order, axis=0).reshape(4 * quarter, 2).T
 
+    uppers = jnp.stack([my_place.side, my_place.upper_line])
+
     distances = list(range(group_count - 1, -1, -1))
-    slots = plan(group_count)
-    first_slot = [
-        min(s for s, hops in enumerate(slots) if any(h[0] == e for h in hops))
-        for e in range(group_count)
-    ]
-    last_slot = [
-        max(s for s, hops in enumerate(slots) if any(h[0] == e for h in hops))
-        for e in range(group_count)
-    ]
     momentum_new = None
     update = None
     factors = None
     moved, partial_squares, chains, got, leaving = {}, {}, {}, {}, {}
-    arrivals = []
-    due = {now: [] for now in range(len(slots) + 8)}
-
-    def after_arrivals(*values):
-        return lax.optimization_barrier((values, arrivals))[0]
-
-    def take_momentum(e, limit):
-        nonlocal momentum_new
-        old_slot, _ = route(my_group, my_group ^ distances[e])
-        (old_slot,) = after_arrivals(old_slot.reshape(1))
-        momentum_new, moved[e], sums = momentum_step(old_slot, grad, momentum, momentum_new)
-        partial_squares[e] = jnp.sum(sums)
-        due[limit].append(sums)
-
-    def take_gram(e, limit):
-        (rows,) = after_arrivals(moved[e])
-        first, second = gram_step(rows)
-        chains[e, SideFirst] = SideFirst(routes, my_place, first)
-        chains[e, LineFirst] = LineFirst(routes, my_place, second)
-        got[e, SideFirst], got[e, LineFirst] = {}, {}
-        due[limit].append(second)
-
-    def take_update(e, limit):
-        nonlocal update
-        pieces = chains[e, SideFirst].pieces(got[e, SideFirst])
-        pieces += chains[e, LineFirst].pieces(got[e, LineFirst])
-        pieces = after_arrivals(*pieces)
-        new_slot = route(my_group ^ distances[e], my_group)[1].reshape(1)
-        factor = factors[e].reshape(1)
-        if distances[e] == 0:
-            update = update_step(
-                new_slot, my_places, factor, moved[e], pieces, update, local_count
+    front = ()
+
+    def follow(*values):
+        return lax.optimization_barrier((values, front))[0]
+
+    for action, which in plan(group_count):
+        if action == "hop":
+            e, kind, name = which
+            needs = kind.hops[name][1]
+            arrived = dict(zip(needs, follow(*[got[e, kind][need] for need in needs])))
+            (value,) = follow(chains[e, kind].value(name, arrived))
+            got[e, kind][name] = send(value, getattr(routes, kind.hops[name][0]))
+            front = (value,)
+        elif action == "momentum":
+            old_slot, _ = route(my_group, my_group ^ distances[which])
+            (old_slot,) = follow(old_slot.reshape(1))
+            momentum_new, moved[which], sums = momentum_step(
+                old_slot, grad, momentum, momentum_new
             )
-            return
-        here = jnp.zeros((1,), jnp.int32)
-        mine = update_step(here, my_places, factor, moved[e], pieces)
-        due[limit].append(mine)
-        pairs = [(g, g ^ distances[e]) for g in range(group_count)]
-        arrived = lax.ppermute(mine, "expert", pairs)
-        leaving[e] = new_slot, arrived
-        due[limit + TRAVEL].append(arrived)
-
-    def take_place(e, limit):
-        nonlocal update
-        new_slot, arrived = leaving.pop(e)
-        (new_slot,) = after_arrivals(new_slot)
-        update = place_step(new_slot, arrived, update, local_count)
-        due[limit].append(update)
-
-    take_momentum(0, 0)
-    take_gram(0, 0)
-    swaps = None
-    for now, hops in enumerate(slots):
-        values = [chains[e, kind].value(name, got[e, kind]) for e, kind, name in hops]
-        values = lax.optimization_barrier((values, arrivals, due[now]))[0]
-        if now + 1 < group_count:
-            take_momentum(now + 1, now + 1)
-        for e in range(1, group_count):
-            if first_slot[e] == now + 2 or (now == 0 and first_slot[e] < 2):
-                take_gram(e, now + 1)
-        for e in list(leaving):
-            if last_slot[e] + 2 + TRAVEL == now:
-                take_place(e, now + 1)
-        for e in range(group_count - 1):
-            if last_slot[e] + 1 == now:
-                take_update(e, now + 1)
-        arrivals = []
-        for (e, kind, name), value in zip(hops, values):
-            arrival = send(value, getattr(routes, kind.hops[name][0]))
-            got[e, kind][name] = arrival
-            arrivals.append(arrival)
-        if now + 1 == group_count:
-            small = jnp.stack([partial_squares[e] for e in range(group_count)])
-            swaps = list(routes.swaps)
-            at_once = -(-len(swaps) // 3)
-        if swaps:
-            for _ in range(min(at_once, len(swaps))):
-                arrival = send(small, swaps.pop())
-                small = small + arrival
-                arrivals.append(arrival)
-            if not swaps:
-                factors = 0.5 * math.sqrt(columns) / jnp.sqrt(small + 1e-06)
-    for e in sorted(leaving):
-        take_place(e, len(slots))
-    take_update(group_count - 1, len(slots))
+            partial_squares[which] = jnp.sum(sums)
+            front = (sums,)
+        elif action == "gram":
+            (rows,) = follow(moved[which])
+            parts = gram_step(uppers, rows)
+            chains[which, SideFirst] = SideFirst(routes, my_place, *parts[:2])
+            chains[which, LineFirst] = LineFirst(routes, my_place, *parts[2:])
+            got[which, SideFirst], got[which, LineFirst] = {}, {}
+            front = tuple(parts[3:])
+        elif action == "swaps":
+            squares = jnp.stack([partial_squares[e] for e in range(group_count)])
+            for pairs in routes.swaps:
+                squares = squares + send(squares, pairs)
+            factors = 0.5 * math.sqrt(columns) / jnp.sqrt(squares + 1e-06)
+        elif action == "update":
+            pieces = chains[which, SideFirst].pieces(got[which, SideFirst])
+            pieces += chains[which, LineFirst].pieces(got[which, LineFirst])
+            pieces = follow(*pieces)
+            new_slot = route(my_group ^ distances[which], my_group)[1].reshape(1)
+            factor = factors[which].reshape(1)
+            rows = moved[which]
+            if distances[which] == 0:
+                update = update_step(
+                    new_slot, my_places, factor, rows, pieces, update, local_count
+                )
+            else:
+                here = jnp.zeros((1,), jnp.int32)
+                mine = update_step(here, my_places, factor, rows, pieces)
+                pairs = [(g, g ^ distances[which]) for g in range(group_count)]
+                leaving[which] = new_slot, lax.ppermute(mine, "expert", pairs)
+                front = (mine,)
+        else:
+            new_slot, arrived = leaving[which]
+            (new_slot,) = follow(new_slot)
+            update = place_step(new_slot, arrived, update, local_count)
+            front = (update,)
     return momentum_new, update
 
 

time: 600 us -> 613 us (1.022)
  waiting for transfers between devices: 202 us -> 222 us
  local copies, waits for them, and re-layouts: 14.1 us -> 4.37 us
  other arithmetic: 57.6 us -> 65 us
    ppermute x51, waiting for transfers between devices: 182 us -> 222 us  [send(): return lax.ppermute(value, 'dp', pairs)]
    ppermute x3, waiting for transfers between devices: 19.9 us -> 0.01 us  [shards(): leaving[which] = (new_slot, lax.ppermute(mine, 'expert', pairs))]
    dynamic_slice x7 -> x0, local copies, waits for them, and re-layouts: 9.1 us -> none  [the longest x4 5.91 us: halves(): given = lax.dynamic_slice_in_dim(part, (1 - upper) * count, count)]
    convert_element_type x24, other arithmetic: 27.2 us -> 34.3 us  [add_up(): (mine.astype(jnp.float32) + arrived.astype(jnp.float32)).astype(jnp.bfloa...]
  transfers between devices with their start and end apart: 54 -> 54, of which waited for: 22 -> 16; matrix products, arithmetic and copies ran while one was open for 11% -> 11% of each run, Pallas kernels for 23% -> 24%
where the time goes in v4:
time: 613 us; the launch traced here: 603 us
  waiting for transfers between devices  222 us (36%)
  Pallas kernels  187 us (31%)
  starting transfers between devices  123 us (20%)
  other arithmetic  65 us (11%)
    ppermute x51, waiting for transfers between devices, send(): return lax.ppermute(value, 'dp', pairs)  222 us
    ppermute x51, starting transfers between devices, send(): return lax.ppermute(value, 'dp', pairs)  121 us
    pallas_call x4, Pallas kernels, update_step(): pl.pallas_call(update_kernel, grid_spec=pltpu.PrefetchScalarGridSpec(num_...  88.7 us
    pallas_call x4, Pallas kernels, momentum_step(): pl.pallas_call(momentum_kernel, grid_spec=pltpu.PrefetchScalarGridSpec(nu...  48 us
    pallas_call x4, Pallas kernels, gram_step(): pl.pallas_call(gram_kernel, in_specs=[pl.BlockSpec(memory_space=pltpu.SME...  34.5 us
    convert_element_type x24, other arithmetic, add_up(): (mine.astype(jnp.float32) + arrived.astype(jnp.float32)).astype(jnp.bfloa...  34.3 us
    pallas_call x3, Pallas kernels, place_step(): pl.pallas_call(place_kernel, grid_spec=pltpu.PrefetchScalarGridSpec(num_s...  15.3 us
  transfers between devices with their start and end apart: 54, of which 16 were waited for; matrix products, arithmetic and copies ran while one was open for 11% of the time, Pallas kernels for 24%

profile of v4, /device:TPU:0, one launch (start us, length us, event | category | flops | bytes accessed | tf_op | source)
XLA Modules:
  0.0 603.2 jit_solution(10831862496988445471)
XLA Ops:
  2.2 12.0 %momentum.4 = (f32[4,896,2048]{2,1,0:T(8,128)}, bf16[896,2048]{1,0:T(8,128)(2,1)}, f32[8,2048]{1,0:T(8,128)}) custom-call(s32[1]{0:T(128)} %bitcast.6.order_ref, bf16[4,896,2048]{2,1,0:T(8,128)(2,1)} %grad_ref.7, f32[4,896,2048]{2,1,0:T(8,128)} %momentum_ref.7), custom_call_target="tpu_custom_call" | custom-call | flops 1048576 | bytes 1024 | tf_op jit(solution)/shard_map/momentum/pallas_call | solution.py:54
  32.3 11.9 %momentum.5 = (f32[4,896,2048]{2,1,0:T(8,128)}, bf16[896,2048]{1,0:T(8,128)(2,1)}, f32[8,2048]{1,0:T(8,128)}) custom-call(s32[1]{0:T(128)} %bitcast.5.order_ref, bf16[4,896,2048]{2,1,0:T(8,128)(2,1)} %grad_ref.7, f32[4,896,2048]{2,1,0:T(8,128)} %momentum_ref.7, f32[4,896,2048]{2,1,0:T(8,128)} %get-tuple-element.150.refs_0_), custom_call_target="tpu_custom_call", output_to_operand_aliasing={{0}: (3, {})} | custom-call | flops 1048576 | bytes 1024 | tf_op jit(solution)/shard_map/momentum/pallas_call | solution.py:54
  44.2 8.6 %gram.5 = (bf16[9,256,256]{2,1,0:T(8,128)(2,1)}, bf16[9,256,256]{2,1,0:T(8,128)(2,1)}, bf16[9,256,256]{2,1,0:T(8,128)(2,1)}, bf16[9,256,256]{2,1,0:T(8,128)(2,1)}) custom-call(s32[2]{0:T(128)} %pad_add_fusion.upper_ref, bf16[896,2048]{1,0:T(8,128)(2,1)} %get-tuple-element.153.rows_ref), custom_call_target="tpu_custom_call" | custom-call | flops 1048576 | bytes 1024 | tf_op jit(solution)/shard_map/gram/pallas_call | solution.py:119
  52.8 12.0 %momentum.6 = (f32[4,896,2048]{2,1,0:T(8,128)}, bf16[896,2048]{1,0:T(8,128)(2,1)}, f32[8,2048]{1,0:T(8,128)}) custom-call(s32[1]{0:T(128)} %bitcast.4.order_ref, bf16[4,896,2048]{2,1,0:T(8,128)(2,1)} %grad_ref.7, f32[4,896,2048]{2,1,0:T(8,128)} %momentum_ref.7, f32[4,896,2048]{2,1,0:T(8,128)} %get-tuple-element.159.refs_0_), custom_call_target="tpu_custom_call", output_to_operand_aliasing={{0}: (3, {})} | custom-call | flops 1048576 | bytes 1024 | tf_op jit(solution)/shard_map/momentum/pallas_call | solution.py:54
  69.3 8.6 %gram.6 = (bf16[9,256,256]{2,1,0:T(8,128)(2,1)}, bf16[9,256,256]{2,1,0:T(8,128)(2,1)}, bf16[9,256,256]{2,1,0:T(8,128)(2,1)}, bf16[9,256,256]{2,1,0:T(8,128)(2,1)}) custom-call(s32[2]{0:T(128)} %pad_add_fusion.upper_ref, bf16[896,2048]{1,0:T(8,128)(2,1)} %get-tuple-element.164.rows_ref), custom_call_target="tpu_custom_call" | custom-call | flops 1048576 | bytes 1024 | tf_op jit(solution)/shard_map/gram/pallas_call | solution.py:119
  81.2 12.1 %momentum.7 = (f32[4,896,2048]{2,1,0:T(8,128)}, bf16[896,2048]{1,0:T(8,128)(2,1)}, f32[8,2048]{1,0:T(8,128)}) custom-call(s32[1]{0:T(128)} %bitcast.1.order_ref, bf16[4,896,2048]{2,1,0:T(8,128)(2,1)} %grad_ref.7, f32[4,896,2048]{2,1,0:T(8,128)} %momentum_ref.7, f32[4,896,2048]{2,1,0:T(8,128)} %get-tuple-element.172.refs_0_), custom_call_target="tpu_custom_call", output_to_operand_aliasing={{0}: (3, {})} | custom-call | flops 1048576 | bytes 1024 | tf_op jit(solution)/shard_map/momentum/pallas_call | solution.py:54
  93.3 8.7 %gram.7 = (bf16[9,256,256]{2,1,0:T(8,128)(2,1)}, bf16[9,256,256]{2,1,0:T(8,128)(2,1)}, bf16[9,256,256]{2,1,0:T(8,128)(2,1)}, bf16[9,256,256]{2,1,0:T(8,128)(2,1)}) custom-call(s32[2]{0:T(128)} %pad_add_fusion.upper_ref, bf16[896,2048]{1,0:T(8,128)(2,1)} %get-tuple-element.176.rows_ref), custom_call_target="tpu_custom_call" | custom-call | flops 1048576 | bytes 1024 | tf_op jit(solution)/shard_map/gram/pallas_call | solution.py:119
  120.4 10.4 %collective-permute-done.10 = bf16[9,256,256]{2,1,0:T(8,128)(2,1)} collective-permute-done((bf16[9,256,256]{2,1,0:T(8,128)(2,1)S(1)}, bf16[9,256,256]{2,1,0:T(8,128)(2,1)}, u32[]{:S(2)}, u32[]{:S(2)}) %collective-permute-start.10) | collective-permute-done | bytes 1179680 | tf_op jit(solution)/shard_map/ppermute | solution.py:275
  144.8 11.3 %collective-permute-done.12 = bf16[9,256,256]{2,1,0:T(8,128)(2,1)} collective-permute-done((bf16[9,256,256]{2,1,0:T(8,128)(2,1)}, bf16[9,256,256]{2,1,0:T(8,128)(2,1)}, u32[]{:S(2)}, u32[]{:S(2)}) %collective-permute-start.12) | collective-permute-done | bytes 1179680 | tf_op jit(solution)/shard_map/ppermute | solution.py:275
  183.2 11.4 %collective-permute-done.2 = f32[4]{0:T(128)S(1)} collective-permute-done((f32[4]{0:T(128)S(1)}, f32[4]{0:T(128)S(1)}, u32[]{:S(2)}, u32[]{:S(2)}) %collective-permute-start.2) | collective-permute-done | bytes 48 | tf_op jit(solution)/shard_map/ppermute | solution.py:275
  194.6 22.5 %collective-permute-start.23 = (bf16[9,256,256]{2,1,0:T(8,128)(2,1)S(1)}, bf16[9,256,256]{2,1,0:T(8,128)(2,1)S(1)}, u32[]{:S(2)}, u32[]{:S(2)}) collective-permute-start(bf16[9,256,256]{2,1,0:T(8,128)(2,1)S(1)} %copy-done.13), channel_id=1, source_target_pairs={{0,8},{4,12},{24,16},{28,20},{1,9},{5,13},{25,17},{29,21},{2,10},{... | collective-permute-start | bytes 3538952 | tf_op jit(solution)/shard_map/ppermute | solution.py:275
  229.6 9.8 %collective-permute-done.3 = f32[4]{0:T(128)S(1)} collective-permute-done((f32[4]{0:T(128)S(1)}, f32[4]{0:T(128)S(1)}, u32[]{:S(2)}, u32[]{:S(2)}) %collective-permute-start.3) | collective-permute-done | bytes 48 | tf_op jit(solution)/shard_map/ppermute | solution.py:275
  246.8 21.1 %collective-permute-done.4 = f32[4]{0:T(128)S(1)} collective-permute-done((f32[4]{0:T(128)S(1)}, f32[4]{0:T(128)S(1)}, u32[]{:S(2)}, u32[]{:S(2)}) %collective-permute-start.4) | collective-permute-done | bytes 48 | tf_op jit(solution)/shard_map/ppermute | solution.py:275
  283.3 15.6 %collective-permute-done.31 = bf16[9,256,256]{2,1,0:T(8,128)(2,1)S(1)} collective-permute-done((bf16[9,256,256]{2,1,0:T(8,128)(2,1)}, bf16[9,256,256]{2,1,0:T(8,128)(2,1)S(1)}, u32[]{:S(2)}, u32[]{:S(2)}) %collective-permute-start.31) | collective-permute-done | bytes 1179680 | tf_op jit(solution)/shard_map/ppermute | solution.py:275
  305.5 22.0 %update.4 = bf16[1,896,2048]{2,1,0:T(8,128)(2,1)} custom-call(s32[1]{0:T(128)} %constant.127.clone.1.slot_ref, s32[2,36]{1,0:T(2,128)} %select_bitcast_fusion.place_ref, f32[1]{0:T(128)} %get-tuple-element.288.factor_ref, bf16[896,2048]{1,0:T(8,128)(2,1)} %get-tuple-element.142.rows_ref, bf16[9,256,256]{2,1,0:T(8,128)(2,1)} %copy-done, ...), custom_call_target="tpu_custom_call" | custom-call | flops 1048576 | bytes 1024 | tf_op jit(solution)/shard_map/update/pallas_call | solution.py:200
  339.8 9.3 %collective-permute-done.8 = bf16[9,256,256]{2,1,0:T(8,128)(2,1)S(1)} collective-permute-done((bf16[9,256,256]{2,1,0:T(8,128)(2,1)}, bf16[9,256,256]{2,1,0:T(8,128)(2,1)S(1)}, u32[]{:S(2)}, u32[]{:S(2)}) %collective-permute-start.8) | collective-permute-done | bytes 1179680 | tf_op jit(solution)/shard_map/ppermute | solution.py:275
  360.3 22.4 %collective-permute-done.39 = bf16[9,256,256]{2,1,0:T(8,128)(2,1)S(1)} collective-permute-done((bf16[9,256,256]{2,1,0:T(8,128)(2,1)S(1)}, bf16[9,256,256]{2,1,0:T(8,128)(2,1)S(1)}, u32[]{:S(2)}, u32[]{:S(2)}) %collective-permute-start.39) | collective-permute-done | bytes 1179680 | tf_op jit(solution)/shard_map/ppermute | solution.py:275
  390.3 22.1 %update.5 = bf16[1,896,2048]{2,1,0:T(8,128)(2,1)} custom-call(s32[1]{0:T(128)} %constant.127.clone.1.slot_ref, s32[2,36]{1,0:T(2,128)} %select_bitcast_fusion.place_ref, f32[1]{0:T(128)} %get-tuple-element.287.factor_ref, bf16[896,2048]{1,0:T(8,128)(2,1)} %get-tuple-element.153.rows_ref, bf16[9,256,256]{2,1,0:T(8,128)(2,1)} %copy-done.2, ...), custom_call_target="tpu_custom_call" | custom-call | flops 1048576 | bytes 1024 | tf_op jit(solution)/shard_map/update/pallas_call | solution.py:200
  452.1 10.1 %collective-permute-done.48 = bf16[9,256,256]{2,1,0:T(8,128)(2,1)S(1)} collective-permute-done((bf16[9,256,256]{2,1,0:T(8,128)(2,1)}, bf16[9,256,256]{2,1,0:T(8,128)(2,1)S(1)}, u32[]{:S(2)}, u32[]{:S(2)}) %collective-permute-start.48) | collective-permute-done | bytes 1179680 | tf_op jit(solution)/shard_map/ppermute | solution.py:275
  464.4 22.0 %update.6 = bf16[1,896,2048]{2,1,0:T(8,128)(2,1)} custom-call(s32[1]{0:T(128)} %constant.127.clone.1.slot_ref, s32[2,36]{1,0:T(2,128)} %select_bitcast_fusion.place_ref, f32[1]{0:T(128)} %get-tuple-element.286.factor_ref, bf16[896,2048]{1,0:T(8,128)(2,1)} %get-tuple-element.164.rows_ref, bf16[9,256,256]{2,1,0:T(8,128)(2,1)} %copy-done.1, ...), custom_call_target="tpu_custom_call" | custom-call | flops 1048576 | bytes 1024 | tf_op jit(solution)/shard_map/update/pallas_call | solution.py:200
  491.3 31.4 %collective-permute-done.44 = bf16[9,256,256]{2,1,0:T(8,128)(2,1)S(1)} collective-permute-done((bf16[9,256,256]{2,1,0:T(8,128)(2,1)S(1)}, bf16[9,256,256]{2,1,0:T(8,128)(2,1)S(1)}, u32[]{:S(2)}, u32[]{:S(2)}) %collective-permute-start.44) | collective-permute-done | bytes 1179680 | tf_op jit(solution)/shard_map/ppermute | solution.py:275
  528.5 19.5 %collective-permute-done.50 = bf16[9,256,256]{2,1,0:T(8,128)(2,1)S(1)} collective-permute-done((bf16[9,256,256]{2,1,0:T(8,128)(2,1)S(1)}, bf16[9,256,256]{2,1,0:T(8,128)(2,1)S(1)}, u32[]{:S(2)}, u32[]{:S(2)}) %collective-permute-start.50) | collective-permute-done | bytes 1179680 | tf_op jit(solution)/shard_map/ppermute | solution.py:275
  549.2 23.7 %collective-permute-done.51 = bf16[9,256,256]{2,1,0:T(8,128)(2,1)S(1)} collective-permute-done((bf16[9,256,256]{2,1,0:T(8,128)(2,1)S(1)}, bf16[9,256,256]{2,1,0:T(8,128)(2,1)S(1)}, u32[]{:S(2)}, u32[]{:S(2)}) %collective-permute-start.51) | collective-permute-done | bytes 1179680 | tf_op jit(solution)/shard_map/ppermute | solution.py:275
  580.2 22.6 %update.7 = bf16[4,896,2048]{2,1,0:T(8,128)(2,1)} custom-call(s32[1]{0:T(128)} %bitcast.7.slot_ref, s32[2,36]{1,0:T(2,128)} %select_bitcast_fusion.place_ref, f32[1]{0:T(128)} %get-tuple-element.289.factor_ref, bf16[896,2048]{1,0:T(8,128)(2,1)} %get-tuple-element.176.rows_ref, bf16[9,256,256]{2,1,0:T(8,128)(2,1)} %copy-done.3, ...), custom_call_target="tpu_custom_call", output_to_operand_aliasing={{}: (8, {})} | custom-call | flops 1048576 | bytes 1024 | tf_op jit(solution)/shard_map/update/pallas_call | solution.py:200
  (202 shorter events, 220.2 us)
Async XLA Ops:
  28.4 49.6 %collective-permute-start.1 = (bf16[9,256,256]{2,1,0:T(8,128)(2,1)}, bf16[9,256,256]{2,1,0:T(8,128)(2,1)S(1)}, u32[]{:S(2)}, u32[]{:S(2)}) collective-permute-start(bf16[9,256,256]{2,1,0:T(8,128)(2,1)} %get-tuple-element.147), channel_id=1, source_target_pairs={{0,4},{4,0},{8,12},{12,8},{16,20},{20,16},{24,28},{28,24},{1,5},{5... | collective-permute-start | bytes 3538952 | tf_op jit(solution)/shard_map/ppermute | solution.py:275
  30.0 72.0 %collective-permute-start.6 = (bf16[9,256,256]{2,1,0:T(8,128)(2,1)}, bf16[9,256,256]{2,1,0:T(8,128)(2,1)}, u32[]{:S(2)}, u32[]{:S(2)}) collective-permute-start(bf16[9,256,256]{2,1,0:T(8,128)(2,1)} %get-tuple-element.148), channel_id=1, source_target_pairs={{0,8},{4,12},{24,16},{28,20},{1,9},{5,13},{25,17},{29,21},{2,10},{... | collective-permute-start | bytes 3538952 | tf_op jit(solution)/shard_map/ppermute | solution.py:275
  78.3 52.4 %collective-permute-start.10 = (bf16[9,256,256]{2,1,0:T(8,128)(2,1)S(1)}, bf16[9,256,256]{2,1,0:T(8,128)(2,1)}, u32[]{:S(2)}, u32[]{:S(2)}) collective-permute-start(bf16[9,256,256]{2,1,0:T(8,128)(2,1)S(1)} %add_convert_fusion.26), channel_id=1, source_target_pairs={{0,8},{4,12},{24,16},{28,20},{1,9},{5,13},{25,17},{29,21},{2,10},{... | collective-permute-start | bytes 3538952 | tf_op jit(solution)/shard_map/ppermute | solution.py:275
  80.7 53.4 %collective-permute-start.15 = (bf16[9,256,256]{2,1,0:T(8,128)(2,1)}, bf16[9,256,256]{2,1,0:T(8,128)(2,1)}, u32[]{:S(2)}, u32[]{:S(2)}) collective-permute-start(bf16[9,256,256]{2,1,0:T(8,128)(2,1)} %get-tuple-element.156), channel_id=1, source_target_pairs={{0,4},{4,0},{8,12},{12,8},{16,20},{20,16},{24,28},{28,24},{1,5},{5... | collective-permute-start | bytes 3538952 | tf_op jit(solution)/shard_map/ppermute | solution.py:275
  159.6 57.6 %collective-permute-start.18 = (bf16[9,256,256]{2,1,0:T(8,128)(2,1)}, bf16[9,256,256]{2,1,0:T(8,128)(2,1)}, u32[]{:S(2)}, u32[]{:S(2)}) collective-permute-start(bf16[9,256,256]{2,1,0:T(8,128)(2,1)} %add_convert_fusion.18), channel_id=1, source_target_pairs={{8,12},{12,8},{16,20},{20,16},{9,13},{13,9},{17,21},{21,17},{10,14... | collective-permute-start | bytes 3538952 | tf_op jit(solution)/shard_map/ppermute | solution.py:275
  162.0 60.4 %collective-permute-start.17 = (bf16[9,256,256]{2,1,0:T(8,128)(2,1)S(1)}, bf16[9,256,256]{2,1,0:T(8,128)(2,1)}, u32[]{:S(2)}, u32[]{:S(2)}) collective-permute-start(bf16[9,256,256]{2,1,0:T(8,128)(2,1)S(1)} %add_convert_fusion.20), channel_id=1, source_target_pairs={{8,16},{12,20},{16,8},{20,12},{9,17},{13,21},{17,9},{21,13},{10,18... | collective-permute-start | bytes 3538952 | tf_op jit(solution)/shard_map/ppermute | solution.py:275
  166.3 58.2 %collective-permute-start.16 = (bf16[9,256,256]{2,1,0:T(8,128)(2,1)}, bf16[9,256,256]{2,1,0:T(8,128)(2,1)}, u32[]{:S(2)}, u32[]{:S(2)}) collective-permute-start(bf16[9,256,256]{2,1,0:T(8,128)(2,1)} %add_convert_fusion.17), channel_id=1, source_target_pairs={{8,0},{12,4},{16,24},{20,28},{9,1},{13,5},{17,25},{21,29},{10,2},{... | collective-permute-start | bytes 3538952 | tf_op jit(solution)/shard_map/ppermute | solution.py:275
  168.6 58.1 %collective-permute-start.9 = (bf16[9,256,256]{2,1,0:T(8,128)(2,1)}, bf16[9,256,256]{2,1,0:T(8,128)(2,1)}, u32[]{:S(2)}, u32[]{:S(2)}) collective-permute-start(bf16[9,256,256]{2,1,0:T(8,128)(2,1)} %get-tuple-element.170), channel_id=1, source_target_pairs={{0,4},{4,0},{8,12},{12,8},{16,20},{20,16},{24,28},{28,24},{1,5},{5... | collective-permute-start | bytes 3538952 | tf_op jit(solution)/shard_map/ppermute | solution.py:275
  194.6 51.8 %collective-permute-start.23 = (bf16[9,256,256]{2,1,0:T(8,128)(2,1)S(1)}, bf16[9,256,256]{2,1,0:T(8,128)(2,1)S(1)}, u32[]{:S(2)}, u32[]{:S(2)}) collective-permute-start(bf16[9,256,256]{2,1,0:T(8,128)(2,1)S(1)} %copy-done.13), channel_id=1, source_target_pairs={{0,8},{4,12},{24,16},{28,20},{1,9},{5,13},{25,17},{29,21},{2,10},{... | collective-permute-start | bytes 3538952 | tf_op jit(solution)/shard_map/ppermute | solution.py:275
  217.2 52.0 %collective-permute-start.22 = (bf16[9,256,256]{2,1,0:T(8,128)(2,1)S(1)}, bf16[9,256,256]{2,1,0:T(8,128)(2,1)S(1)}, u32[]{:S(2)}, u32[]{:S(2)}) collective-permute-start(bf16[9,256,256]{2,1,0:T(8,128)(2,1)S(1)} %add_convert_fusion.16), channel_id=1, source_target_pairs={{8,16},{12,20},{16,8},{20,12},{9,17},{13,21},{17,9},{21,13},{10,18... | collective-permute-start | bytes 3538952 | tf_op jit(solution)/shard_map/ppermute | solution.py:275
  224.6 47.9 %collective-permute-start.21 = (bf16[9,256,256]{2,1,0:T(8,128)(2,1)S(1)}, bf16[9,256,256]{2,1,0:T(8,128)(2,1)S(1)}, u32[]{:S(2)}, u32[]{:S(2)}) collective-permute-start(bf16[9,256,256]{2,1,0:T(8,128)(2,1)S(1)} %add_convert_fusion.15), channel_id=1, source_target_pairs={{8,16},{12,20},{16,8},{20,12},{9,17},{13,21},{17,9},{21,13},{10,18... | collective-permute-start | bytes 3538952 | tf_op jit(solution)/shard_map/ppermute | solution.py:275
  226.7 54.6 %collective-permute-start.30 = (bf16[9,256,256]{2,1,0:T(8,128)(2,1)S(1)}, bf16[9,256,256]{2,1,0:T(8,128)(2,1)S(1)}, u32[]{:S(2)}, u32[]{:S(2)}) collective-permute-start(bf16[9,256,256]{2,1,0:T(8,128)(2,1)S(1)} %add_convert_fusion.20), channel_id=1, source_target_pairs={{8,0},{12,4},{16,24},{20,28},{9,1},{13,5},{17,25},{21,29},{10,2},{... | collective-permute-start | bytes 3538952 | tf_op jit(solution)/shard_map/ppermute | solution.py:275
  272.5 55.0 %collective-permute-start.28 = (bf16[9,256,256]{2,1,0:T(8,128)(2,1)S(1)}, bf16[9,256,256]{2,1,0:T(8,128)(2,1)}, u32[]{:S(2)}, u32[]{:S(2)}) collective-permute-start(bf16[9,256,256]{2,1,0:T(8,128)(2,1)S(1)} %add_convert_fusion.12), channel_id=1, source_target_pairs={{8,0},{12,4},{16,24},{20,28},{9,1},{13,5},{17,25},{21,29},{10,2},{... | collective-permute-start | bytes 3538952 | tf_op jit(solution)/shard_map/ppermute | solution.py:275
  274.5 56.0 %collective-permute-start.26 = (bf16[9,256,256]{2,1,0:T(8,128)(2,1)}, bf16[9,256,256]{2,1,0:T(8,128)(2,1)}, u32[]{:S(2)}, u32[]{:S(2)}) collective-permute-start(bf16[9,256,256]{2,1,0:T(8,128)(2,1)} %get-tuple-element.206), channel_id=1, source_target_pairs={{0,8},{4,12},{24,16},{28,20},{1,9},{5,13},{25,17},{29,21},{2,10},{... | collective-permute-start | bytes 3538952 | tf_op jit(solution)/shard_map/ppermute | solution.py:275
  281.3 50.9 %collective-permute-start.27 = (bf16[9,256,256]{2,1,0:T(8,128)(2,1)}, bf16[9,256,256]{2,1,0:T(8,128)(2,1)}, u32[]{:S(2)}, u32[]{:S(2)}) collective-permute-start(bf16[9,256,256]{2,1,0:T(8,128)(2,1)} %add_convert_fusion.13), channel_id=1, source_target_pairs={{8,16},{12,20},{16,8},{20,12},{9,17},{13,21},{17,9},{21,13},{10,18... | collective-permute-start | bytes 3538952 | tf_op jit(solution)/shard_map/ppermute | solution.py:275
  332.2 97.2 %collective-permute-start.43 = (bf16[1,896,2048]{2,1,0:T(8,128)(2,1)}, bf16[1,896,2048]{2,1,0:T(8,128)(2,1)}, u32[]{:S(2)}, u32[]{:S(2)}) collective-permute-start(bf16[1,896,2048]{2,1,0:T(8,128)(2,1)} %update.4), channel_id=1, source_target_pairs={{0,3},{1,2},{2,1},{3,0},{4,7},{5,6},{6,5},{7,4},{8,11},{9,10},{10,... | collective-permute-start | bytes 11010056 | tf_op jit(solution)/shard_map/ppermute | solution.py:518
  334.7 48.0 %collective-permute-start.39 = (bf16[9,256,256]{2,1,0:T(8,128)(2,1)S(1)}, bf16[9,256,256]{2,1,0:T(8,128)(2,1)S(1)}, u32[]{:S(2)}, u32[]{:S(2)}) collective-permute-start(bf16[9,256,256]{2,1,0:T(8,128)(2,1)S(1)} %copy-done.20), channel_id=1, source_target_pairs={{8,0},{12,4},{16,24},{20,28},{9,1},{13,5},{17,25},{21,29},{10,2},{... | collective-permute-start | bytes 3538952 | tf_op jit(solution)/shard_map/ppermute | solution.py:275
  349.1 63.2 %collective-permute-start.36 = (bf16[9,256,256]{2,1,0:T(8,128)(2,1)S(1)}, bf16[9,256,256]{2,1,0:T(8,128)(2,1)}, u32[]{:S(2)}, u32[]{:S(2)}) collective-permute-start(bf16[9,256,256]{2,1,0:T(8,128)(2,1)S(1)} %add_convert_fusion.7), channel_id=1, source_target_pairs={{8,0},{12,4},{16,24},{20,28},{9,1},{13,5},{17,25},{21,29},{10,2},{... | collective-permute-start | bytes 3538952 | tf_op jit(solution)/shard_map/ppermute | solution.py:275
  357.4 57.7 %collective-permute-start.35 = (bf16[9,256,256]{2,1,0:T(8,128)(2,1)S(1)}, bf16[9,256,256]{2,1,0:T(8,128)(2,1)}, u32[]{:S(2)}, u32[]{:S(2)}) collective-permute-start(bf16[9,256,256]{2,1,0:T(8,128)(2,1)S(1)} %add_convert_fusion.9), channel_id=1, source_target_pairs={{8,12},{12,8},{16,20},{20,16},{9,13},{13,9},{17,21},{21,17},{10,14... | collective-permute-start | bytes 3538952 | tf_op jit(solution)/shard_map/ppermute | solution.py:275
  436.0 87.5 %collective-permute-start.52 = (bf16[1,896,2048]{2,1,0:T(8,128)(2,1)}, bf16[1,896,2048]{2,1,0:T(8,128)(2,1)}, u32[]{:S(2)}, u32[]{:S(2)}) collective-permute-start(bf16[1,896,2048]{2,1,0:T(8,128)(2,1)} %update.5), channel_id=1, source_target_pairs={{0,2},{1,3},{2,0},{3,1},{4,6},{5,7},{6,4},{7,5},{8,10},{9,11},{10,... | collective-permute-start | bytes 11010056 | tf_op jit(solution)/shard_map/ppermute | solution.py:518
  486.4 87.6 %collective-permute-start.53 = (bf16[1,896,2048]{2,1,0:T(8,128)(2,1)}, bf16[1,896,2048]{2,1,0:T(8,128)(2,1)}, u32[]{:S(2)}, u32[]{:S(2)}) collective-permute-start(bf16[1,896,2048]{2,1,0:T(8,128)(2,1)} %update.6), channel_id=1, source_target_pairs={{0,1},{1,0},{2,3},{3,2},{4,5},{5,4},{6,7},{7,6},{8,9},{9,8},{10,11... | collective-permute-start | bytes 11010056 | tf_op jit(solution)/shard_map/ppermute | solution.py:518
  488.5 59.5 %collective-permute-start.50 = (bf16[9,256,256]{2,1,0:T(8,128)(2,1)S(1)}, bf16[9,256,256]{2,1,0:T(8,128)(2,1)S(1)}, u32[]{:S(2)}, u32[]{:S(2)}) collective-permute-start(bf16[9,256,256]{2,1,0:T(8,128)(2,1)S(1)} %add_convert_fusion.1), channel_id=1, source_target_pairs={{8,0},{12,4},{16,24},{20,28},{9,1},{13,5},{17,25},{21,29},{10,2},{... | collective-permute-start | bytes 3538952 | tf_op jit(solution)/shard_map/ppermute | solution.py:275
  489.8 83.1 %collective-permute-start.51 = (bf16[9,256,256]{2,1,0:T(8,128)(2,1)S(1)}, bf16[9,256,256]{2,1,0:T(8,128)(2,1)S(1)}, u32[]{:S(2)}, u32[]{:S(2)}) collective-permute-start(bf16[9,256,256]{2,1,0:T(8,128)(2,1)S(1)} %collective-permute-done.45), channel_id=1, source_target_pairs={{8,0},{12,4},{16,24},{20,28},{9,1},{13,5},{17,25},{21,29},{10,2},{... | collective-permute-start | bytes 3538952 | tf_op jit(solution)/shard_map/ppermute | solution.py:275
  522.9 56.3 %collective-permute-start.49 = (bf16[9,256,256]{2,1,0:T(8,128)(2,1)S(1)}, bf16[9,256,256]{2,1,0:T(8,128)(2,1)S(1)}, u32[]{:S(2)}, u32[]{:S(2)}) collective-permute-start(bf16[9,256,256]{2,1,0:T(8,128)(2,1)S(1)} %broadcast_select_fusion.2.refs_0_), channel_id=1, source_target_pairs={{0,4},{4,0},{8,12},{12,8},{16,20},{20,16},{24,28},{28,24},{1,5},{5... | collective-permute-start | bytes 3538952 | tf_op jit(solution)/shard_map/ppermute | solution.py:275
  (53 other events, 1192.8 us)

commit v5 on v4

--- a/solution.py
+++ b/solution.py
@@ -10,6 +10,7 @@
 
 D = 7168
 BLOCK = 256
+STRIP = 512
 VMEM_BYTES = 56 * 2**20
 SMALL_COST = pl.CostEstimate(flops=2**20, bytes_accessed=2**10, transcendentals=0)
 
@@ -88,15 +89,16 @@
     copies = []
     place = 0
     for i in range(count):
-        turned = rows_ref[:, i * BLOCK : (i + 1) * BLOCK].T
-        for j in range(i, count):
+        start = i * BLOCK
+        strip = jnp.dot(
+            rows_ref[:, start : start + BLOCK].T,
+            rows_ref[:, start:],
+            preferred_element_type=jnp.float32,
+        ).astype(jnp.bfloat16)
+        for j in range(count - i):
             half, inside = divmod(place, 2 * quarter)
             part, slot = divmod(inside, quarter)
-            halves[half][part, slot] = jnp.dot(
-                turned,
-                rows_ref[:, j * BLOCK : (j + 1) * BLOCK],
-                preferred_element_type=jnp.float32,
-            ).astype(jnp.bfloat16)
+            halves[half][part, slot] = strip[:, j * BLOCK : (j + 1) * BLOCK]
             place += 1
             if place % (2 * quarter) == 0:
                 upper = upper_ref[half]
@@ -135,22 +137,6 @@
     )(uppers, moved)
 
 
-def times_gram(left_ref, gram_ref, j):
-    start = j * BLOCK
-    stop = start + BLOCK
-    total = lax.dot_general(
-        left_ref[:, start:],
-        gram_ref[start:stop, start:],
-        (((1,), (1,)), ((), ())),
-        preferred_element_type=jnp.float32,
-    )
-    if j > 0:
-        total += jnp.dot(
-            left_ref[:, :start], gram_ref[:start, start:stop], preferred_element_type=jnp.float32
-        )
-    return total
-
-
 def update_kernel(slot_ref, place_ref, factor_ref, rows_ref, *refs):
     pieces = refs[:4]
     out_ref, gram_ref, normal_ref, product_ref = refs[-4:]
@@ -163,22 +149,28 @@
                 index = number * piece_blocks + block
                 row = pl.multiple_of(place_ref[0, index], BLOCK)
                 column = pl.multiple_of(place_ref[1, index], BLOCK)
-                gram_ref[pl.ds(row, BLOCK), pl.ds(column, BLOCK)] = piece[block]
+                value = piece[block]
+                gram_ref[pl.ds(row, BLOCK), pl.ds(column, BLOCK)] = value
+                gram_ref[pl.ds(column, BLOCK), pl.ds(row, BLOCK)] = value.T
 
     factor = factor_ref[0]
     factor_squared = factor * factor
     normal_ref[...] = (rows_ref[...].astype(jnp.float32) * factor).astype(jnp.bfloat16)
-    count = gram_ref.shape[0] // BLOCK
-    for j in range(count):
-        product = times_gram(normal_ref, gram_ref, j) * factor_squared
-        product_ref[:, j * BLOCK : (j + 1) * BLOCK] = product.astype(jnp.bfloat16)
-    for j in range(count):
-        here = slice(j * BLOCK, (j + 1) * BLOCK)
-        second = times_gram(product_ref, gram_ref, j) * factor_squared
+    columns = gram_ref.shape[0]
+    strips = [slice(start, start + STRIP) for start in range(0, columns, STRIP)]
+    for here in strips:
+        product = jnp.dot(
+            normal_ref[...], gram_ref[:, here], preferred_element_type=jnp.float32
+        )
+        product_ref[:, here] = (product * factor_squared).astype(jnp.bfloat16)
+    for here in strips:
+        second = jnp.dot(
+            product_ref[...], gram_ref[:, here], preferred_element_type=jnp.float32
+        )
         orthogonal = (
             3.4445 * normal_ref[:, here].astype(jnp.float32)
             - 4.775 * product_ref[:, here].astype(jnp.float32)
-            + 2.0315 * second
+            + 2.0315 * (second * factor_squared)
         )
         out_ref[0, :, here] = (orthogonal * math.sqrt(D)).astype(jnp.bfloat16)
 
@@ -218,29 +210,33 @@
     )(*operands)
 
 
-def place_kernel(slot_ref, arrived_ref, *refs):
-    refs[-1][...] = arrived_ref[...]
+def place_kernel(cuts, slot_ref, *refs):
+    for number in range(cuts):
+
+        @pl.when(pl.program_id(0) == number)
+        def _():
+            refs[-1][...] = refs[number][...]
 
 
 def place_step(slot, arrived, earlier, count):
-    _, rows, columns = arrived.shape
-    step = row_block(rows, 256)
-    in_specs = [pl.BlockSpec((1, step, columns), lambda r, slot: (0, r, 0))]
-    operands = [slot, arrived]
+    cuts = len(arrived)
+    _, rows, columns = arrived[0].shape
+    in_specs = [pl.BlockSpec((1, rows, columns), lambda r, slot: (0, 0, 0))] * cuts
+    operands = [slot, *arrived]
     aliases = {}
     if earlier is not None:
         in_specs.append(pl.BlockSpec(memory_space=pl.ANY))
         operands.append(earlier)
-        aliases = {2: 0}
+        aliases = {cuts + 1: 0}
     return pl.pallas_call(
-        place_kernel,
+        functools.partial(place_kernel, cuts),
         grid_spec=pltpu.PrefetchScalarGridSpec(
             num_scalar_prefetch=1,
-            grid=(rows // step,),
+            grid=(cuts,),
             in_specs=in_specs,
-            out_specs=pl.BlockSpec((1, step, columns), lambda r, slot: (slot[0], r, 0)),
+            out_specs=pl.BlockSpec((1, rows, columns), lambda r, slot: (slot[0], r, 0)),
         ),
-        out_shape=jax.ShapeDtypeStruct((count, rows, columns), jnp.bfloat16),
+        out_shape=jax.ShapeDtypeStruct((count, cuts * rows, columns), jnp.bfloat16),
         input_output_aliases=aliases,
         compiler_params=pltpu.CompilerParams(vmem_limit_bytes=VMEM_BYTES),
         cost_estimate=SMALL_COST,
@@ -348,10 +344,10 @@
         )
 
 
-def plan(experts):
-    transfer, latency, issue, pass_over = 23.3, 3.0, 1.5, 1.6
-    takes = {"momentum": 12.0, "gram": 9.0, "update": 23.0, "place": 5.0}
-    swaps_take, near, far = 30.0, 20.0, 78.0
+def plan(experts, swap_count):
+    transfer, latency, issue, pass_over = 23.3, 5.0, 1.6, 1.6
+    takes = {"momentum": 12.0, "gram": 9.0, "update": 20.0, "place": 5.0}
+    near, far = 20.0, 78.0
     hops = {}
     for expert in range(experts):
         for kind in (LineFirst, SideFirst):
@@ -375,9 +371,18 @@
     update_arrival = {}
     far_free = 0.0
 
+    taken = set()
+    swapped = 0
+    swap_arrival = math.inf
+
+    def put(action, which):
+        arrived = [hop for hop in arrival if arrival[hop] <= now and hop not in taken]
+        taken.update(arrived)
+        order.append((action, which, arrived))
+
     def do(kernel):
         nonlocal now
-        order.append((kernel, count[kernel]))
+        put(kernel, count[kernel])
         count[kernel] += 1
         now += takes[kernel]
 
@@ -392,15 +397,19 @@
 
     do("momentum")
     do("gram")
-    while count["update"] < experts:
+    while count["place"] < experts - 1:
         hop = next_hop()
         updating = count["update"]
         last = updating == experts - 1
+        early = count["place"] < experts - 2 or updating == experts
         mine = [h for h in hops if h[0] == updating]
-        whole = all(arrival.get(h, math.inf) <= now for h in mine)
+        whole = updating < experts and all(arrival.get(h, math.inf) <= now for h in mine)
+        if updating == experts - 2:
+            whole = whole and len(arrival) == len(hops)
+        squares_in = swap_arrival if swapped == swap_count else math.inf
         if hop is not None:
             link, _, passes = hops[hop]
-            order.append(("hop", hop))
+            put("hop", hop)
             now += issue + passes * pass_over
             queue = queues[link]
             queue.append(max([now + 1, *queue[-1:]]) + transfer)
@@ -410,19 +419,23 @@
         elif count["momentum"] < experts:
             do("momentum")
             if count["momentum"] == experts:
-                order.append(("swaps", 0))
-                squares_arrival = now + swaps_take
-        elif whole and squares_arrival <= now and (not last or count["place"] == updating):
+                swap_arrival = now
+        elif swapped < swap_count and swap_arrival <= now:
+            put("swap", swapped)
+            now += issue + pass_over
+            swapped += 1
+            swap_arrival = max([now, *(queue[-1] for queue in queues.values() if queue)]) + latency
+        elif whole and squares_in <= now and (not last or count["place"] >= updating - 1):
             do("update")
             if updating < experts - 2:
                 far_free = max(now, far_free) + far
                 update_arrival[updating] = far_free
             else:
                 update_arrival[updating] = now + near
-        elif update_arrival.get(count["place"], math.inf) <= now:
+        elif early and update_arrival.get(count["place"], math.inf) <= now:
             do("place")
         else:
-            times = [*arrival.values(), *update_arrival.values(), squares_arrival]
+            times = [*arrival.values(), *update_arrival.values(), swap_arrival]
             now = min(time for time in times if time > now)
     return order
 
@@ -465,14 +478,18 @@
     distances = list(range(group_count - 1, -1, -1))
     momentum_new = None
     update = None
-    factors = None
+    factors, squares, other_squares = None, None, None
     moved, partial_squares, chains, got, leaving = {}, {}, {}, {}, {}
     front = ()
 
     def follow(*values):
         return lax.optimization_barrier((values, front))[0]
 
-    for action, which in plan(group_count):
+    for action, which, arrived_hops in plan(group_count, len(routes.swaps)):
+        taken = follow(*[got[e, kind][name] for e, kind, name in arrived_hops])
+        for (e, kind, name), arrival in zip(arrived_hops, taken):
+            got[e, kind][name] = arrival
+        front = (*front, *taken)
         if action == "hop":
             e, kind, name = which
             needs = kind.hops[name][1]
@@ -495,27 +512,38 @@
             chains[which, LineFirst] = LineFirst(routes, my_place, *parts[2:])
             got[which, SideFirst], got[which, LineFirst] = {}, {}
             front = tuple(parts[3:])
-        elif action == "swaps":
-            squares = jnp.stack([partial_squares[e] for e in range(group_count)])
-            for pairs in routes.swaps:
-                squares = squares + send(squares, pairs)
-            factors = 0.5 * math.sqrt(columns) / jnp.sqrt(squares + 1e-06)
+        elif action == "swap":
+            if which == 0:
+                squares = jnp.stack([partial_squares[e] for e in range(group_count)])
+            else:
+                squares = squares + follow(other_squares)[0]
+            (squares,) = follow(squares)
+            other_squares = send(squares, routes.swaps[which])
+            front = (squares,)
         elif action == "update":
             pieces = chains[which, SideFirst].pieces(got[which, SideFirst])
             pieces += chains[which, LineFirst].pieces(got[which, LineFirst])
             pieces = follow(*pieces)
             new_slot = route(my_group ^ distances[which], my_group)[1].reshape(1)
+            if which == 0:
+                squares = squares + follow(other_squares)[0]
+                factors = 0.5 * math.sqrt(columns) / jnp.sqrt(squares + 1e-06)
             factor = factors[which].reshape(1)
             rows = moved[which]
             if distances[which] == 0:
                 update = update_step(
                     new_slot, my_places, factor, rows, pieces, update, local_count
                 )
+                front = (update,)
             else:
                 here = jnp.zeros((1,), jnp.int32)
                 mine = update_step(here, my_places, factor, rows, pieces)
                 pairs = [(g, g ^ distances[which]) for g in range(group_count)]
-                leaving[which] = new_slot, lax.ppermute(mine, "expert", pairs)
+                cuts = 4 if distances[which] == 1 and row_count % 64 == 0 else 1
+                cut_rows = [
+                    lax.ppermute(cut, "expert", pairs) for cut in jnp.split(mine, cuts, axis=1)
+                ]
+                leaving[which] = new_slot, cut_rows
                 front = (mine,)
         else:
             new_slot, arrived = leaving[which]

time: 613 us -> 584 us (0.953)
  waiting for transfers between devices: 222 us -> 178 us
  starting transfers between devices: 123 us -> 134 us
    ppermute x51, waiting for transfers between devices: 222 us -> 159 us  [send(): return lax.ppermute(value, 'dp', pairs)]
    ppermute x3 -> x6, waiting for transfers between devices: 0.01 us -> 19.7 us  [shards(): lax.ppermute(cut, 'expert', pairs)]
    ppermute x51, starting transfers between devices: 121 us -> 132 us  [send(): return lax.ppermute(value, 'dp', pairs)]
  transfers between devices with their start and end apart: 54 -> 57, of which waited for: 16 -> 19; matrix products, arithmetic and copies ran while one was open for 11% -> 11% of each run, Pallas kernels for 24% -> 29%
where the time goes in v5:
time: 584 us; the launch traced here: 574 us
  Pallas kernels  191 us (33%)
  waiting for transfers between devices  178 us (30%)
  starting transfers between devices  134 us (23%)
  other arithmetic  59 us (10%)
  local copies, waits for them, and re-layouts  9.84 us (2%)
    ppermute x51, waiting for transfers between devices, send(): return lax.ppermute(value, 'dp', pairs)  159 us
    ppermute x51, starting transfers between devices, send(): return lax.ppermute(value, 'dp', pairs)  132 us
    pallas_call x4, Pallas kernels, update_step(): pl.pallas_call(update_kernel, grid_spec=pltpu.PrefetchScalarGridSpec(num_...  93.5 us
    pallas_call x4, Pallas kernels, momentum_step(): pl.pallas_call(momentum_kernel, grid_spec=pltpu.PrefetchScalarGridSpec(nu...  48.1 us
    pallas_call x4, Pallas kernels, gram_step(): pl.pallas_call(gram_kernel, in_specs=[pl.BlockSpec(memory_space=pltpu.SME...  34.6 us
    convert_element_type x24, other arithmetic, add_up(): (mine.astype(jnp.float32) + arrived.astype(jnp.float32)).astype(jnp.bfloa...  30.3 us
    ppermute x6, waiting for transfers between devices, shards(): lax.ppermute(cut, 'expert', pairs)  19.7 us
    pallas_call x3, Pallas kernels, place_step(): pl.pallas_call(functools.partial(place_kernel, cuts), grid_spec=pltpu.Pre...  14.5 us
  transfers between devices with their start and end apart: 57, of which 19 were waited for; matrix products, arithmetic and copies ran while one was open for 11% of the time, Pallas kernels for 29%

profile of v5, /device:TPU:0, one launch (start us, length us, event | category | flops | bytes accessed | tf_op | source)
XLA Modules:
  0.0 574.2 jit_solution(4210005920728480909)
XLA Ops:
  2.2 12.0 %momentum.4 = (f32[4,896,2048]{2,1,0:T(8,128)}, bf16[896,2048]{1,0:T(8,128)(2,1)}, f32[8,2048]{1,0:T(8,128)}) custom-call(s32[1]{0:T(128)} %bitcast.6.order_ref, bf16[4,896,2048]{2,1,0:T(8,128)(2,1)} %grad_ref.7, f32[4,896,2048]{2,1,0:T(8,128)} %momentum_ref.7), custom_call_target="tpu_custom_call" | custom-call | flops 1048576 | bytes 1024 | tf_op jit(solution)/shard_map/momentum/pallas_call | solution.py:55
  14.9 8.6 %gram.4 = (bf16[9,256,256]{2,1,0:T(8,128)(2,1)}, bf16[9,256,256]{2,1,0:T(8,128)(2,1)}, bf16[9,256,256]{2,1,0:T(8,128)(2,1)}, bf16[9,256,256]{2,1,0:T(8,128)(2,1)}) custom-call(s32[2]{0:T(128)} %pad_add_fusion.upper_ref, bf16[896,2048]{1,0:T(8,128)(2,1)} %get-tuple-element.196.rows_ref), custom_call_target="tpu_custom_call" | custom-call | flops 1048576 | bytes 1024 | tf_op jit(solution)/shard_map/gram/pallas_call | solution.py:121
  31.4 12.0 %momentum.5 = (f32[4,896,2048]{2,1,0:T(8,128)}, bf16[896,2048]{1,0:T(8,128)(2,1)}, f32[8,2048]{1,0:T(8,128)}) custom-call(s32[1]{0:T(128)} %bitcast.5.order_ref, bf16[4,896,2048]{2,1,0:T(8,128)(2,1)} %grad_ref.7, f32[4,896,2048]{2,1,0:T(8,128)} %momentum_ref.7, f32[4,896,2048]{2,1,0:T(8,128)} %get-tuple-element.204.refs_0_), custom_call_target="tpu_custom_call", output_to_operand_aliasing={{0}: (3, {})} | custom-call | flops 1048576 | bytes 1024 | tf_op jit(solution)/shard_map/momentum/pallas_call | solution.py:55
  43.4 8.6 %gram.5 = (bf16[9,256,256]{2,1,0:T(8,128)(2,1)}, bf16[9,256,256]{2,1,0:T(8,128)(2,1)}, bf16[9,256,256]{2,1,0:T(8,128)(2,1)}, bf16[9,256,256]{2,1,0:T(8,128)(2,1)}) custom-call(s32[2]{0:T(128)} %pad_add_fusion.upper_ref, bf16[896,2048]{1,0:T(8,128)(2,1)} %get-tuple-element.207.rows_ref), custom_call_target="tpu_custom_call" | custom-call | flops 1048576 | bytes 1024 | tf_op jit(solution)/shard_map/gram/pallas_call | solution.py:121
  54.0 12.1 %momentum.6 = (f32[4,896,2048]{2,1,0:T(8,128)}, bf16[896,2048]{1,0:T(8,128)(2,1)}, f32[8,2048]{1,0:T(8,128)}) custom-call(s32[1]{0:T(128)} %bitcast.4.order_ref, bf16[4,896,2048]{2,1,0:T(8,128)(2,1)} %grad_ref.7, f32[4,896,2048]{2,1,0:T(8,128)} %momentum_ref.7, f32[4,896,2048]{2,1,0:T(8,128)} %get-tuple-element.213.refs_0_), custom_call_target="tpu_custom_call", output_to_operand_aliasing={{0}: (3, {})} | custom-call | flops 1048576 | bytes 1024 | tf_op jit(solution)/shard_map/momentum/pallas_call | solution.py:55
  68.3 8.7 %gram.6 = (bf16[9,256,256]{2,1,0:T(8,128)(2,1)}, bf16[9,256,256]{2,1,0:T(8,128)(2,1)}, bf16[9,256,256]{2,1,0:T(8,128)(2,1)}, bf16[9,256,256]{2,1,0:T(8,128)(2,1)}) custom-call(s32[2]{0:T(128)} %pad_add_fusion.upper_ref, bf16[896,2048]{1,0:T(8,128)(2,1)} %get-tuple-element.220.rows_ref), custom_call_target="tpu_custom_call" | custom-call | flops 1048576 | bytes 1024 | tf_op jit(solution)/shard_map/gram/pallas_call | solution.py:121
  88.9 12.0 %momentum.7 = (f32[4,896,2048]{2,1,0:T(8,128)}, bf16[896,2048]{1,0:T(8,128)(2,1)}, f32[8,2048]{1,0:T(8,128)}) custom-call(s32[1]{0:T(128)} %bitcast.1.order_ref, bf16[4,896,2048]{2,1,0:T(8,128)(2,1)} %grad_ref.7, f32[4,896,2048]{2,1,0:T(8,128)} %momentum_ref.7, f32[4,896,2048]{2,1,0:T(8,128)} %get-tuple-element.230.refs_0_), custom_call_target="tpu_custom_call", output_to_operand_aliasing={{0}: (3, {})} | custom-call | flops 1048576 | bytes 1024 | tf_op jit(solution)/shard_map/momentum/pallas_call | solution.py:55
  100.9 8.7 %gram.7 = (bf16[9,256,256]{2,1,0:T(8,128)(2,1)}, bf16[9,256,256]{2,1,0:T(8,128)(2,1)}, bf16[9,256,256]{2,1,0:T(8,128)(2,1)}, bf16[9,256,256]{2,1,0:T(8,128)(2,1)}) custom-call(s32[2]{0:T(128)} %pad_add_fusion.upper_ref, bf16[896,2048]{1,0:T(8,128)(2,1)} %get-tuple-element.234.rows_ref), custom_call_target="tpu_custom_call" | custom-call | flops 1048576 | bytes 1024 | tf_op jit(solution)/shard_map/gram/pallas_call | solution.py:121
  135.2 9.2 %collective-permute-start.19 = (bf16[9,256,256]{2,1,0:T(8,128)(2,1)S(1)}, bf16[9,256,256]{2,1,0:T(8,128)(2,1)S(1)}, u32[]{:S(2)}, u32[]{:S(2)}) collective-permute-start(bf16[9,256,256]{2,1,0:T(8,128)(2,1)S(1)} %add_convert_fusion.21), channel_id=1, source_target_pairs={{0,8},{4,12},{24,16},{28,20},{1,9},{5,13},{25,17},{29,21},{2,10},{... | collective-permute-start | bytes 3538952 | tf_op jit(solution)/shard_map/ppermute | solution.py:271
  147.2 10.6 %collective-permute-done.8 = bf16[9,256,256]{2,1,0:T(8,128)(2,1)} collective-permute-done((bf16[9,256,256]{2,1,0:T(8,128)(2,1)}, bf16[9,256,256]{2,1,0:T(8,128)(2,1)}, u32[]{:S(2)}, u32[]{:S(2)}) %collective-permute-start.8) | collective-permute-done | bytes 1179680 | tf_op jit(solution)/shard_map/ppermute | solution.py:271
  165.4 27.3 %collective-permute-start.17 = (bf16[9,256,256]{2,1,0:T(8,128)(2,1)}, bf16[9,256,256]{2,1,0:T(8,128)(2,1)}, u32[]{:S(2)}, u32[]{:S(2)}) collective-permute-start(bf16[9,256,256]{2,1,0:T(8,128)(2,1)} %get-tuple-element.264), channel_id=1, source_target_pairs={{0,8},{4,12},{24,16},{28,20},{1,9},{5,13},{25,17},{29,21},{2,10},{... | collective-permute-start | bytes 3538952 | tf_op jit(solution)/shard_map/ppermute | solution.py:271
  235.3 9.4 %collective-permute-done.22 = bf16[9,256,256]{2,1,0:T(8,128)(2,1)} collective-permute-done((bf16[9,256,256]{2,1,0:T(8,128)(2,1)}, bf16[9,256,256]{2,1,0:T(8,128)(2,1)}, u32[]{:S(2)}, u32[]{:S(2)}) %collective-permute-start.22) | collective-permute-done | bytes 1179680 | tf_op jit(solution)/shard_map/ppermute | solution.py:271
  251.3 6.1 %collective-permute-start.30 = (bf16[9,256,256]{2,1,0:T(8,128)(2,1)S(1)}, bf16[9,256,256]{2,1,0:T(8,128)(2,1)S(1)}, u32[]{:S(2)}, u32[]{:S(2)}) collective-permute-start(bf16[9,256,256]{2,1,0:T(8,128)(2,1)S(1)} %copy-done.10), channel_id=1, source_target_pairs={{0,8},{4,12},{24,16},{28,20},{1,9},{5,13},{25,17},{29,21},{2,10},{... | collective-permute-start | bytes 3538952 | tf_op jit(solution)/shard_map/ppermute | solution.py:271
  257.4 12.5 %collective-permute-done.25 = bf16[9,256,256]{2,1,0:T(8,128)(2,1)} collective-permute-done((bf16[9,256,256]{2,1,0:T(8,128)(2,1)S(1)}, bf16[9,256,256]{2,1,0:T(8,128)(2,1)}, u32[]{:S(2)}, u32[]{:S(2)}) %collective-permute-start.25) | collective-permute-done | bytes 1179680 | tf_op jit(solution)/shard_map/ppermute | solution.py:271
  283.7 19.2 %collective-permute-done.21 = f32[4]{0:T(128)S(1)} collective-permute-done((f32[4]{0:T(128)S(1)}, f32[4]{0:T(128)S(1)}, u32[]{:S(2)}, u32[]{:S(2)}) %collective-permute-start.21) | collective-permute-done | bytes 48 | tf_op jit(solution)/shard_map/ppermute | solution.py:271
  306.3 23.2 %update.4 = bf16[1,896,2048]{2,1,0:T(8,128)(2,1)} custom-call(s32[1]{0:T(128)} %constant.127.clone.1.slot_ref, s32[2,36]{1,0:T(2,128)} %select_bitcast_fusion.place_ref, f32[1]{0:T(128)} %get-tuple-element.400.factor_ref, bf16[896,2048]{1,0:T(8,128)(2,1)} %get-tuple-element.196.rows_ref, bf16[9,256,256]{2,1,0:T(8,128)(2,1)} %copy-done.1, ...), custom_call_target="tpu_custom_call" | custom-call | flops 1048576 | bytes 1024 | tf_op jit(solution)/shard_map/update/pallas_call | solution.py:192
  349.4 11.9 %collective-permute-done.38.refs_1_ = bf16[9,256,256]{2,1,0:T(8,128)(2,1)S(1)} collective-permute-done((bf16[9,256,256]{2,1,0:T(8,128)(2,1)S(1)}, bf16[9,256,256]{2,1,0:T(8,128)(2,1)S(1)}, u32[]{:S(2)}, u32[]{:S(2)}) %collective-permute-start.38) | collective-permute-done | bytes 1179680 | tf_op jit(solution)/shard_map/ppermute | solution.py:271
  365.8 23.2 %update.5 = bf16[1,896,2048]{2,1,0:T(8,128)(2,1)} custom-call(s32[1]{0:T(128)} %constant.127.clone.1.slot_ref, s32[2,36]{1,0:T(2,128)} %select_bitcast_fusion.place_ref, f32[1]{0:T(128)} %get-tuple-element.399.factor_ref, bf16[896,2048]{1,0:T(8,128)(2,1)} %get-tuple-element.207.rows_ref, bf16[9,256,256]{2,1,0:T(8,128)(2,1)} %copy-done.3, ...), custom_call_target="tpu_custom_call" | custom-call | flops 1048576 | bytes 1024 | tf_op jit(solution)/shard_map/update/pallas_call | solution.py:192
  398.0 14.9 %collective-permute-done.43.refs_0_ = bf16[1,896,2048]{2,1,0:T(8,128)(2,1)} collective-permute-done((bf16[1,896,2048]{2,1,0:T(8,128)(2,1)}, bf16[1,896,2048]{2,1,0:T(8,128)(2,1)}, u32[]{:S(2)}, u32[]{:S(2)}) %collective-permute-start.43) | collective-permute-done | bytes 3670048 | tf_op jit(solution)/shard_map/ppermute | solution.py:544
  432.3 25.4 %collective-permute-done.44 = bf16[9,256,256]{2,1,0:T(8,128)(2,1)} collective-permute-done((bf16[9,256,256]{2,1,0:T(8,128)(2,1)}, bf16[9,256,256]{2,1,0:T(8,128)(2,1)}, u32[]{:S(2)}, u32[]{:S(2)}) %collective-permute-start.44) | collective-permute-done | bytes 1179680 | tf_op jit(solution)/shard_map/ppermute | solution.py:271
  461.8 23.8 %collective-permute-done.49 = bf16[9,256,256]{2,1,0:T(8,128)(2,1)S(1)} collective-permute-done((bf16[9,256,256]{2,1,0:T(8,128)(2,1)S(1)}, bf16[9,256,256]{2,1,0:T(8,128)(2,1)S(1)}, u32[]{:S(2)}, u32[]{:S(2)}) %collective-permute-start.49) | collective-permute-done | bytes 1179680 | tf_op jit(solution)/shard_map/ppermute | solution.py:271
  496.4 14.4 %collective-permute-done.47 = bf16[9,256,256]{2,1,0:T(8,128)(2,1)S(1)} collective-permute-done((bf16[9,256,256]{2,1,0:T(8,128)(2,1)S(1)}, bf16[9,256,256]{2,1,0:T(8,128)(2,1)S(1)}, u32[]{:S(2)}, u32[]{:S(2)}) %collective-permute-start.47) | collective-permute-done | bytes 1179680 | tf_op jit(solution)/shard_map/ppermute | solution.py:271
  515.0 23.1 %update.6 = bf16[1,896,2048]{2,1,0:T(8,128)(2,1)} custom-call(s32[1]{0:T(128)} %constant.127.clone.1.slot_ref, s32[2,36]{1,0:T(2,128)} %select_bitcast_fusion.place_ref, f32[1]{0:T(128)} %get-tuple-element.398.factor_ref, bf16[896,2048]{1,0:T(8,128)(2,1)} %get-tuple-element.220.rows_ref, bf16[9,256,256]{2,1,0:T(8,128)(2,1)} %copy-done, ...), custom_call_target="tpu_custom_call" | custom-call | flops 1048576 | bytes 1024 | tf_op jit(solution)/shard_map/update/pallas_call | solution.py:192
  544.7 24.0 %update.7.refs_4_ = bf16[4,896,2048]{2,1,0:T(8,128)(2,1)} custom-call(s32[1]{0:T(128)} %bitcast.9.slot_ref, s32[2,36]{1,0:T(2,128)} %select_bitcast_fusion.place_ref, f32[1]{0:T(128)} %get-tuple-element.401.factor_ref, bf16[896,2048]{1,0:T(8,128)(2,1)} %get-tuple-element.234.rows_ref, ...), custom_call_target="tpu_custom_call", output_to_operand_aliasing={{}: (8, {})} | custom-call | flops 1048576 | bytes 1024 | tf_op jit(solution)/shard_map/update/pallas_call | solution.py:192
  (228 shorter events, 211.5 us)
Async XLA Ops:
  30.0 51.9 %collective-permute-start.2 = (bf16[9,256,256]{2,1,0:T(8,128)(2,1)}, bf16[9,256,256]{2,1,0:T(8,128)(2,1)S(1)}, u32[]{:S(2)}, u32[]{:S(2)}) collective-permute-start(bf16[9,256,256]{2,1,0:T(8,128)(2,1)} %get-tuple-element.202), channel_id=1, source_target_pairs={{0,8},{4,12},{24,16},{28,20},{1,9},{5,13},{25,17},{29,21},{2,10},{... | collective-permute-start | bytes 3538952 | tf_op jit(solution)/shard_map/ppermute | solution.py:271
  52.6 57.0 %collective-permute-start.4 = (bf16[9,256,256]{2,1,0:T(8,128)(2,1)}, bf16[9,256,256]{2,1,0:T(8,128)(2,1)S(1)}, u32[]{:S(2)}, u32[]{:S(2)}) collective-permute-start(bf16[9,256,256]{2,1,0:T(8,128)(2,1)} %get-tuple-element.211), channel_id=1, source_target_pairs={{0,8},{4,12},{24,16},{28,20},{1,9},{5,13},{25,17},{29,21},{2,10},{... | collective-permute-start | bytes 3538952 | tf_op jit(solution)/shard_map/ppermute | solution.py:271
  66.4 43.3 %collective-permute-start.5 = (bf16[9,256,256]{2,1,0:T(8,128)(2,1)S(1)}, bf16[9,256,256]{2,1,0:T(8,128)(2,1)}, u32[]{:S(2)}, u32[]{:S(2)}) collective-permute-start(bf16[9,256,256]{2,1,0:T(8,128)(2,1)S(1)} %add_convert_fusion.27), channel_id=1, source_target_pairs={{8,16},{12,20},{16,8},{20,12},{9,17},{13,21},{17,9},{21,13},{10,18... | collective-permute-start | bytes 3538952 | tf_op jit(solution)/shard_map/ppermute | solution.py:271
  83.0 47.1 %collective-permute-start.6 = (bf16[9,256,256]{2,1,0:T(8,128)(2,1)}, bf16[9,256,256]{2,1,0:T(8,128)(2,1)S(1)}, u32[]{:S(2)}, u32[]{:S(2)}) collective-permute-start(bf16[9,256,256]{2,1,0:T(8,128)(2,1)} %get-tuple-element.227), channel_id=1, source_target_pairs={{0,4},{4,0},{8,12},{12,8},{16,20},{20,16},{24,28},{28,24},{1,5},{5... | collective-permute-start | bytes 3538952 | tf_op jit(solution)/shard_map/ppermute | solution.py:271
  83.5 48.9 %collective-permute-start.11 = (bf16[9,256,256]{2,1,0:T(8,128)(2,1)S(1)}, bf16[9,256,256]{2,1,0:T(8,128)(2,1)}, u32[]{:S(2)}, u32[]{:S(2)}) collective-permute-start(bf16[9,256,256]{2,1,0:T(8,128)(2,1)S(1)} %add_convert_fusion.26), channel_id=1, source_target_pairs={{0,8},{4,12},{24,16},{28,20},{1,9},{5,13},{25,17},{29,21},{2,10},{... | collective-permute-start | bytes 3538952 | tf_op jit(solution)/shard_map/ppermute | solution.py:271
  134.0 58.7 %collective-permute-start.14 = (bf16[9,256,256]{2,1,0:T(8,128)(2,1)S(1)}, bf16[9,256,256]{2,1,0:T(8,128)(2,1)S(1)}, u32[]{:S(2)}, u32[]{:S(2)}) collective-permute-start(bf16[9,256,256]{2,1,0:T(8,128)(2,1)S(1)} %add_convert_fusion.22), channel_id=1, source_target_pairs={{8,16},{12,20},{16,8},{20,12},{9,17},{13,21},{17,9},{21,13},{10,18... | collective-permute-start | bytes 3538952 | tf_op jit(solution)/shard_map/ppermute | solution.py:271
  135.2 61.0 %collective-permute-start.19 = (bf16[9,256,256]{2,1,0:T(8,128)(2,1)S(1)}, bf16[9,256,256]{2,1,0:T(8,128)(2,1)S(1)}, u32[]{:S(2)}, u32[]{:S(2)}) collective-permute-start(bf16[9,256,256]{2,1,0:T(8,128)(2,1)S(1)} %add_convert_fusion.21), channel_id=1, source_target_pairs={{0,8},{4,12},{24,16},{28,20},{1,9},{5,13},{25,17},{29,21},{2,10},{... | collective-permute-start | bytes 3538952 | tf_op jit(solution)/shard_map/ppermute | solution.py:271
  145.9 51.6 %collective-permute-start.20 = (bf16[9,256,256]{2,1,0:T(8,128)(2,1)S(1)}, bf16[9,256,256]{2,1,0:T(8,128)(2,1)}, u32[]{:S(2)}, u32[]{:S(2)}) collective-permute-start(bf16[9,256,256]{2,1,0:T(8,128)(2,1)S(1)} %add_convert_fusion.20), channel_id=1, source_target_pairs={{8,0},{12,4},{16,24},{20,28},{9,1},{13,5},{17,25},{21,29},{10,2},{... | collective-permute-start | bytes 3538952 | tf_op jit(solution)/shard_map/ppermute | solution.py:271
  165.4 48.2 %collective-permute-start.17 = (bf16[9,256,256]{2,1,0:T(8,128)(2,1)}, bf16[9,256,256]{2,1,0:T(8,128)(2,1)}, u32[]{:S(2)}, u32[]{:S(2)}) collective-permute-start(bf16[9,256,256]{2,1,0:T(8,128)(2,1)} %get-tuple-element.264), channel_id=1, source_target_pairs={{0,8},{4,12},{24,16},{28,20},{1,9},{5,13},{25,17},{29,21},{2,10},{... | collective-permute-start | bytes 3538952 | tf_op jit(solution)/shard_map/ppermute | solution.py:271
  219.0 51.6 %collective-permute-start.24 = (bf16[9,256,256]{2,1,0:T(8,128)(2,1)}, bf16[9,256,256]{2,1,0:T(8,128)(2,1)}, u32[]{:S(2)}, u32[]{:S(2)}) collective-permute-start(bf16[9,256,256]{2,1,0:T(8,128)(2,1)} %add_convert_fusion.15), channel_id=1, source_target_pairs={{8,0},{12,4},{16,24},{20,28},{9,1},{13,5},{17,25},{21,29},{10,2},{... | collective-permute-start | bytes 3538952 | tf_op jit(solution)/shard_map/ppermute | solution.py:271
  225.6 44.3 %collective-permute-start.25 = (bf16[9,256,256]{2,1,0:T(8,128)(2,1)S(1)}, bf16[9,256,256]{2,1,0:T(8,128)(2,1)}, u32[]{:S(2)}, u32[]{:S(2)}) collective-permute-start(bf16[9,256,256]{2,1,0:T(8,128)(2,1)S(1)} %add_convert_fusion.14), channel_id=1, source_target_pairs={{0,8},{4,12},{24,16},{28,20},{1,9},{5,13},{25,17},{29,21},{2,10},{... | collective-permute-start | bytes 3538952 | tf_op jit(solution)/shard_map/ppermute | solution.py:271
  230.2 44.1 %collective-permute-start.23 = (bf16[9,256,256]{2,1,0:T(8,128)(2,1)}, bf16[9,256,256]{2,1,0:T(8,128)(2,1)}, u32[]{:S(2)}, u32[]{:S(2)}) collective-permute-start(bf16[9,256,256]{2,1,0:T(8,128)(2,1)} %add_convert_fusion.15), channel_id=1, source_target_pairs={{8,16},{12,20},{16,8},{20,12},{9,17},{13,21},{17,9},{21,13},{10,18... | collective-permute-start | bytes 3538952 | tf_op jit(solution)/shard_map/ppermute | solution.py:271
  251.3 79.6 %collective-permute-start.30 = (bf16[9,256,256]{2,1,0:T(8,128)(2,1)S(1)}, bf16[9,256,256]{2,1,0:T(8,128)(2,1)S(1)}, u32[]{:S(2)}, u32[]{:S(2)}) collective-permute-start(bf16[9,256,256]{2,1,0:T(8,128)(2,1)S(1)} %copy-done.10), channel_id=1, source_target_pairs={{0,8},{4,12},{24,16},{28,20},{1,9},{5,13},{25,17},{29,21},{2,10},{... | collective-permute-start | bytes 3538952 | tf_op jit(solution)/shard_map/ppermute | solution.py:271
  269.9 61.2 %collective-permute-start.29 = (bf16[9,256,256]{2,1,0:T(8,128)(2,1)}, bf16[9,256,256]{2,1,0:T(8,128)(2,1)S(1)}, u32[]{:S(2)}, u32[]{:S(2)}) collective-permute-start(bf16[9,256,256]{2,1,0:T(8,128)(2,1)} %add_convert_fusion.13), channel_id=1, source_target_pairs={{8,16},{12,20},{16,8},{20,12},{9,17},{13,21},{17,9},{21,13},{10,18... | collective-permute-start | bytes 3538952 | tf_op jit(solution)/shard_map/ppermute | solution.py:271
  270.6 58.9 %collective-permute-start.31 = (bf16[9,256,256]{2,1,0:T(8,128)(2,1)S(1)}, bf16[9,256,256]{2,1,0:T(8,128)(2,1)}, u32[]{:S(2)}, u32[]{:S(2)}) collective-permute-start(bf16[9,256,256]{2,1,0:T(8,128)(2,1)S(1)} %add_convert_fusion.12), channel_id=1, source_target_pairs={{8,0},{12,4},{16,24},{20,28},{9,1},{13,5},{17,25},{21,29},{10,2},{... | collective-permute-start | bytes 3538952 | tf_op jit(solution)/shard_map/ppermute | solution.py:271
  280.9 57.2 %collective-permute-start.34 = (bf16[9,256,256]{2,1,0:T(8,128)(2,1)S(1)}, bf16[9,256,256]{2,1,0:T(8,128)(2,1)}, u32[]{:S(2)}, u32[]{:S(2)}) collective-permute-start(bf16[9,256,256]{2,1,0:T(8,128)(2,1)S(1)} %add_convert_fusion.11), channel_id=1, source_target_pairs={{8,16},{12,20},{16,8},{20,12},{9,17},{13,21},{17,9},{21,13},{10,18... | collective-permute-start | bytes 3538952 | tf_op jit(solution)/shard_map/ppermute | solution.py:271
  331.0 81.9 %collective-permute-start.43 = (bf16[1,896,2048]{2,1,0:T(8,128)(2,1)}, bf16[1,896,2048]{2,1,0:T(8,128)(2,1)}, u32[]{:S(2)}, u32[]{:S(2)}) collective-permute-start(bf16[1,896,2048]{2,1,0:T(8,128)(2,1)} %update.4), channel_id=1, source_target_pairs={{0,3},{1,2},{2,1},{3,0},{4,7},{5,6},{6,5},{7,4},{8,11},{9,10},{10,... | collective-permute-start | bytes 11010056 | tf_op jit(solution)/shard_map/ppermute | solution.py:544
  338.1 50.9 %collective-permute-start.33 = (bf16[9,256,256]{2,1,0:T(8,128)(2,1)S(1)}, bf16[9,256,256]{2,1,0:T(8,128)(2,1)S(1)}, u32[]{:S(2)}, u32[]{:S(2)}) collective-permute-start(bf16[9,256,256]{2,1,0:T(8,128)(2,1)S(1)} %add_convert_fusion.7), channel_id=1, source_target_pairs={{0,8},{4,12},{24,16},{28,20},{1,9},{5,13},{25,17},{29,21},{2,10},{... | collective-permute-start | bytes 3538952 | tf_op jit(solution)/shard_map/ppermute | solution.py:271
  343.5 45.4 %collective-permute-start.35 = (bf16[9,256,256]{2,1,0:T(8,128)(2,1)S(1)}, bf16[9,256,256]{2,1,0:T(8,128)(2,1)S(1)}, u32[]{:S(2)}, u32[]{:S(2)}) collective-permute-start(bf16[9,256,256]{2,1,0:T(8,128)(2,1)S(1)} %add_convert_fusion.6), channel_id=1, source_target_pairs={{8,0},{12,4},{16,24},{20,28},{9,1},{13,5},{17,25},{21,29},{10,2},{... | collective-permute-start | bytes 3538952 | tf_op jit(solution)/shard_map/ppermute | solution.py:271
  395.6 96.0 %collective-permute-start.50 = (bf16[1,896,2048]{2,1,0:T(8,128)(2,1)}, bf16[1,896,2048]{2,1,0:T(8,128)(2,1)}, u32[]{:S(2)}, u32[]{:S(2)}) collective-permute-start(bf16[1,896,2048]{2,1,0:T(8,128)(2,1)} %update.5), channel_id=1, source_target_pairs={{0,2},{1,3},{2,0},{3,1},{4,6},{5,7},{6,4},{7,5},{8,10},{9,11},{10,... | collective-permute-start | bytes 11010056 | tf_op jit(solution)/shard_map/ppermute | solution.py:544
  430.2 55.3 %collective-permute-start.48 = (bf16[9,256,256]{2,1,0:T(8,128)(2,1)S(1)}, bf16[9,256,256]{2,1,0:T(8,128)(2,1)S(1)}, u32[]{:S(2)}, u32[]{:S(2)}) collective-permute-start(bf16[9,256,256]{2,1,0:T(8,128)(2,1)S(1)} %add_convert_fusion.1), channel_id=1, source_target_pairs={{8,16},{12,20},{16,8},{20,12},{9,17},{13,21},{17,9},{21,13},{10,18... | collective-permute-start | bytes 3538952 | tf_op jit(solution)/shard_map/ppermute | solution.py:271
  431.0 54.6 %collective-permute-start.49 = (bf16[9,256,256]{2,1,0:T(8,128)(2,1)S(1)}, bf16[9,256,256]{2,1,0:T(8,128)(2,1)S(1)}, u32[]{:S(2)}, u32[]{:S(2)}) collective-permute-start(bf16[9,256,256]{2,1,0:T(8,128)(2,1)S(1)} %add_convert_fusion.1), channel_id=1, source_target_pairs={{8,0},{12,4},{16,24},{20,28},{9,1},{13,5},{17,25},{21,29},{10,2},{... | collective-permute-start | bytes 3538952 | tf_op jit(solution)/shard_map/ppermute | solution.py:271
  458.0 52.8 %collective-permute-start.47 = (bf16[9,256,256]{2,1,0:T(8,128)(2,1)S(1)}, bf16[9,256,256]{2,1,0:T(8,128)(2,1)S(1)}, u32[]{:S(2)}, u32[]{:S(2)}) collective-permute-start(bf16[9,256,256]{2,1,0:T(8,128)(2,1)S(1)} %add_convert_fusion), channel_id=1, source_target_pairs={{8,0},{12,4},{16,24},{20,28},{9,1},{13,5},{17,25},{21,29},{10,2},{... | collective-permute-start | bytes 3538952 | tf_op jit(solution)/shard_map/ppermute | solution.py:271
  485.6 56.7 %collective-permute-start.51 = (bf16[9,256,256]{2,1,0:T(8,128)(2,1)S(1)}, bf16[9,256,256]{2,1,0:T(8,128)(2,1)S(1)}, u32[]{:S(2)}, u32[]{:S(2)}) collective-permute-start(bf16[9,256,256]{2,1,0:T(8,128)(2,1)S(1)} %collective-permute-done.48), channel_id=1, source_target_pairs={{8,0},{12,4},{16,24},{20,28},{9,1},{13,5},{17,25},{21,29},{10,2},{... | collective-permute-start | bytes 3538952 | tf_op jit(solution)/shard_map/ppermute | solution.py:271
  (66 other events, 1288.3 us)

commit v6 on v5

--- a/solution.py
+++ b/solution.py
@@ -10,7 +10,7 @@
 
 D = 7168
 BLOCK = 256
-STRIP = 512
+EXTRA_ROWS = 16
 VMEM_BYTES = 56 * 2**20
 SMALL_COST = pl.CostEstimate(flops=2**20, bytes_accessed=2**10, transcendentals=0)
 
@@ -23,22 +23,10 @@
 
 
 def momentum_kernel(order_ref, grad_ref, momentum_ref, *refs):
-    new_ref, moved_ref, squares_ref = refs[-3:]
+    new_ref, moved_ref = refs[-2:]
     new = 0.95 * momentum_ref[0] + grad_ref[0].astype(jnp.float32)
     new_ref[0] = new
-    moved = new.astype(jnp.bfloat16)
-    moved_ref[...] = moved
-    values = moved.astype(jnp.float32)
-    rows, columns = values.shape
-    partial_sum = jnp.sum((values * values).reshape(rows // 8, 8, columns), axis=0)
-
-    @pl.when(pl.program_id(0) == 0)
-    def _():
-        squares_ref[...] = partial_sum
-
-    @pl.when(pl.program_id(0) > 0)
-    def _():
-        squares_ref[...] += partial_sum
+    moved_ref[...] = new.astype(jnp.bfloat16)
 
 
 def momentum_step(source, grad, momentum, earlier):
@@ -58,16 +46,11 @@
             num_scalar_prefetch=1,
             grid=(rows // step,),
             in_specs=in_specs,
-            out_specs=[
-                spot,
-                pl.BlockSpec((step, columns), lambda r, order: (r, 0)),
-                pl.BlockSpec((8, columns), lambda r, order: (0, 0)),
-            ],
+            out_specs=[spot, pl.BlockSpec((step, columns), lambda r, order: (r, 0))],
         ),
         out_shape=[
             jax.ShapeDtypeStruct(momentum.shape, jnp.float32),
             jax.ShapeDtypeStruct((rows, columns), jnp.bfloat16),
-            jax.ShapeDtypeStruct((8, columns), jnp.float32),
         ],
         input_output_aliases=aliases,
         compiler_params=pltpu.CompilerParams(vmem_limit_bytes=VMEM_BYTES),
@@ -81,12 +64,41 @@
     return [(i, j) for i in range(count) for j in range(i, count)]
 
 
-def gram_kernel(upper_ref, rows_ref, *refs):
+def squares_tile(squares, index):
+    top = float(jnp.finfo(jnp.bfloat16).max)
+    spot = lax.broadcasted_iota(jnp.int32, (EXTRA_ROWS, BLOCK), 0) * BLOCK
+    spot += lax.broadcasted_iota(jnp.int32, (EXTRA_ROWS, BLOCK), 1)
+    tile = jnp.zeros((EXTRA_ROWS, BLOCK), jnp.float32)
+    rest = squares
+    for number in range(3):
+        piece = jnp.minimum(rest, top).astype(jnp.bfloat16).astype(jnp.float32)
+        tile = jnp.where(spot == 3 * index + number, piece, tile)
+        rest = rest - piece
+    return tile.astype(jnp.bfloat16)
+
+
+def gram_kernel(where_ref, rows_ref, *refs):
     outputs, halves, sems = refs[:4], refs[4:6], refs[6]
     columns = rows_ref.shape[1]
     count = columns // BLOCK
-    quarter = halves[0].shape[1]
+    quarter = halves[0].shape[1] // BLOCK
+    diagonal = lax.broadcasted_iota(jnp.int32, (BLOCK, BLOCK), 0) == lax.broadcasted_iota(
+        jnp.int32, (BLOCK, BLOCK), 1
+    )
+    on_diagonal = jnp.zeros((BLOCK, BLOCK), jnp.float32)
     copies = []
+
+    def send_out(half):
+        upper = where_ref[half]
+        for given in range(2):
+            number = 2 * half + given
+            source = upper if given == 0 else 1 - upper
+            copy = pltpu.make_async_copy(
+                halves[half].at[source], outputs[number], sems.at[number]
+            )
+            copy.start()
+            copies.append(copy)
+
     place = 0
     for i in range(count):
         start = i * BLOCK
@@ -94,30 +106,29 @@
             rows_ref[:, start : start + BLOCK].T,
             rows_ref[:, start:],
             preferred_element_type=jnp.float32,
-        ).astype(jnp.bfloat16)
+        )
+        on_diagonal += jnp.where(diagonal, strip[:, :BLOCK], 0.0)
         for j in range(count - i):
             half, inside = divmod(place, 2 * quarter)
             part, slot = divmod(inside, quarter)
-            halves[half][part, slot] = strip[:, j * BLOCK : (j + 1) * BLOCK]
+            halves[half][part, slot * BLOCK : (slot + 1) * BLOCK] = strip[
+                :, j * BLOCK : (j + 1) * BLOCK
+            ].astype(jnp.bfloat16)
             place += 1
-            if place % (2 * quarter) == 0:
-                upper = upper_ref[half]
-                for given in range(2):
-                    number = 2 * half + given
-                    source = upper if given == 0 else 1 - upper
-                    copy = pltpu.make_async_copy(
-                        halves[half].at[source], outputs[number], sems.at[number]
-                    )
-                    copy.start()
-                    copies.append(copy)
+            if place == 2 * quarter:
+                send_out(0)
+    squares = jnp.sum(on_diagonal, keepdims=True)
+    halves[1][0, quarter * BLOCK :] = squares_tile(squares, where_ref[2])
+    halves[1][1, quarter * BLOCK :] = jnp.zeros((EXTRA_ROWS, BLOCK), jnp.bfloat16)
+    send_out(1)
     for copy in copies:
         copy.wait()
 
 
-def gram_step(uppers, moved):
-    rows, columns = moved.shape
-    quarter = len(block_places(columns)) // 4
-    part = jax.ShapeDtypeStruct((quarter, BLOCK, BLOCK), jnp.bfloat16)
+def gram_step(where, moved):
+    columns = moved.shape[1]
+    quarter = len(block_places(columns)) // 4 * BLOCK
+    shapes = [(quarter, BLOCK), (quarter + EXTRA_ROWS, BLOCK)]
     return pl.pallas_call(
         gram_kernel,
         in_specs=[
@@ -125,70 +136,83 @@
             pl.BlockSpec(memory_space=pltpu.VMEM),
         ],
         out_specs=[pl.BlockSpec(memory_space=pl.ANY)] * 4,
-        out_shape=[part] * 4,
-        scratch_shapes=[
-            pltpu.VMEM((2, quarter, BLOCK, BLOCK), jnp.bfloat16),
-            pltpu.VMEM((2, quarter, BLOCK, BLOCK), jnp.bfloat16),
-            pltpu.SemaphoreType.DMA((4,)),
-        ],
+        out_shape=[jax.ShapeDtypeStruct(shapes[n // 2], jnp.bfloat16) for n in range(4)],
+        scratch_shapes=[pltpu.VMEM((2, *shape), jnp.bfloat16) for shape in shapes]
+        + [pltpu.SemaphoreType.DMA((4,))],
         compiler_params=pltpu.CompilerParams(vmem_limit_bytes=VMEM_BYTES),
         cost_estimate=SMALL_COST,
         name="gram",
-    )(uppers, moved)
-
-
-def update_kernel(slot_ref, place_ref, factor_ref, rows_ref, *refs):
+    )(where, moved)
+
+
+def times_gram(left_ref, gram_ref, j):
+    start = j * BLOCK
+    stop = start + BLOCK
+    total = lax.dot_general(
+        left_ref[:, start:],
+        gram_ref[start:stop, start:],
+        (((1,), (1,)), ((), ())),
+        preferred_element_type=jnp.float32,
+    )
+    if j > 0:
+        total += jnp.dot(
+            left_ref[:, :start], gram_ref[:start, start:stop], preferred_element_type=jnp.float32
+        )
+    return total
+
+
+def update_kernel(slot_ref, place_ref, rows_ref, *refs):
     pieces = refs[:4]
     out_ref, gram_ref, normal_ref, product_ref = refs[-4:]
-    piece_blocks = pieces[0].shape[0]
+    columns = gram_ref.shape[0]
+    count = columns // BLOCK
+    piece_blocks = pieces[0].shape[0] // BLOCK
+    squares = sum(
+        jnp.sum(piece[piece_blocks * BLOCK :].astype(jnp.float32), keepdims=True)
+        for piece in pieces[2:]
+    )
+    factor = 0.5 * math.sqrt(columns) / jnp.sqrt(squares + 1e-06)
+    factor_squared = factor * factor
 
     @pl.when(pl.program_id(0) == 0)
     def _():
+        finite = squares < math.inf
         for number, piece in enumerate(pieces):
             for block in range(piece_blocks):
                 index = number * piece_blocks + block
                 row = pl.multiple_of(place_ref[0, index], BLOCK)
                 column = pl.multiple_of(place_ref[1, index], BLOCK)
-                value = piece[block]
-                gram_ref[pl.ds(row, BLOCK), pl.ds(column, BLOCK)] = value
-                gram_ref[pl.ds(column, BLOCK), pl.ds(row, BLOCK)] = value.T
-
-    factor = factor_ref[0]
-    factor_squared = factor * factor
+                value = piece[block * BLOCK : (block + 1) * BLOCK]
+                gram_ref[pl.ds(row, BLOCK), pl.ds(column, BLOCK)] = jnp.where(
+                    finite, value, jnp.zeros_like(value)
+                )
+
     normal_ref[...] = (rows_ref[...].astype(jnp.float32) * factor).astype(jnp.bfloat16)
-    columns = gram_ref.shape[0]
-    strips = [slice(start, start + STRIP) for start in range(0, columns, STRIP)]
-    for here in strips:
-        product = jnp.dot(
-            normal_ref[...], gram_ref[:, here], preferred_element_type=jnp.float32
-        )
-        product_ref[:, here] = (product * factor_squared).astype(jnp.bfloat16)
-    for here in strips:
-        second = jnp.dot(
-            product_ref[...], gram_ref[:, here], preferred_element_type=jnp.float32
-        )
+    for j in range(count):
+        product = times_gram(normal_ref, gram_ref, j) * factor_squared
+        product_ref[:, j * BLOCK : (j + 1) * BLOCK] = product.astype(jnp.bfloat16)
+    for j in range(count):
+        here = slice(j * BLOCK, (j + 1) * BLOCK)
+        second = times_gram(product_ref, gram_ref, j) * factor_squared
         orthogonal = (
             3.4445 * normal_ref[:, here].astype(jnp.float32)
             - 4.775 * product_ref[:, here].astype(jnp.float32)
-            + 2.0315 * (second * factor_squared)
+            + 2.0315 * second
         )
         out_ref[0, :, here] = (orthogonal * math.sqrt(D)).astype(jnp.bfloat16)
 
 
-def update_step(slot, places, factor, moved, pieces, earlier=None, count=1):
+def update_step(slot, places, moved, pieces, earlier=None, count=1):
     rows, columns = moved.shape
     step = rows // 2 if rows % 32 == 0 and rows >= 512 else rows
-    whole = pl.BlockSpec(pieces[0].shape, lambda r, *_: (0, 0, 0))
-    in_specs = [
-        pl.BlockSpec(memory_space=pltpu.SMEM),
-        pl.BlockSpec((step, columns), lambda r, *_: (r, 0)),
-    ] + [whole] * 4
-    operands = [slot, places, factor, moved, *pieces]
+    in_specs = [pl.BlockSpec((step, columns), lambda r, *_: (r, 0))]
+    in_specs += [pl.BlockSpec(piece.shape, lambda r, *_: (0, 0)) for piece in pieces]
+    operands = [slot, places, moved, *pieces]
     aliases = {}
     if earlier is not None:
         in_specs.append(pl.BlockSpec(memory_space=pl.ANY))
         operands.append(earlier)
-        aliases = {8: 0}
+        aliases = {7: 0}
     return pl.pallas_call(
         update_kernel,
         grid_spec=pltpu.PrefetchScalarGridSpec(
@@ -259,7 +283,6 @@
         self.outward = [(b, a) for a, b in self.inward]
         self.middle = [(i, i + 2) for i in everyone if line(i) == 1]
         self.middle += [(i, i - 2) for i in everyone if line(i) == 2]
-        self.swaps = [[(i, i ^ 1 << bit) for i in everyone] for bit in range(dp_count.bit_length() - 1)]
         self.far = []
         distance = 8
         while distance < dp_count:
@@ -344,36 +367,37 @@
         )
 
 
-def plan(experts, swap_count):
-    transfer, latency, issue, pass_over = 23.3, 5.0, 1.6, 1.6
-    takes = {"momentum": 12.0, "gram": 9.0, "update": 20.0, "place": 5.0}
-    near, far = 20.0, 78.0
+def plan(experts):
+    transfer, latency, issue, pass_over = 23.3, 3.0, 2.5, 1.8
+    takes = {"momentum": 12.0, "gram": 9.0, "update": 28.0, "place": 5.0}
+    near, far = 12.0, 78.0
+    deepest, patience, backlog = 4, 4.0, 10.0
     hops = {}
     for expert in range(experts):
         for kind in (LineFirst, SideFirst):
             for name, (link, needs, passes) in kind.hops.items():
                 needed = [(expert, kind, need) for need in needs]
                 hops[expert, kind, name] = (link.replace("inner_", ""), needed, passes)
-    last_hops = {}
+    lengths = {}
 
     def length(hop):
-        if hop not in last_hops:
+        if hop not in lengths:
             later = [length(h) for h in hops if hop in hops[h][1]]
-            last_hops[hop] = 1 + max(later, default=0)
-        return last_hops[hop]
-
-    first_choice = sorted(hops, key=lambda hop: (hop[0], -length(hop)))
+            lengths[hop] = 1 + max(later, default=0)
+        return lengths[hop]
+
+    def rank(hop):
+        return hop[0] - length(hop) - (0.5 if hop[1] is SideFirst else 0), hop[0]
+
+    first_choice = sorted(hops, key=rank)
     order = []
     now = 0.0
     count = dict.fromkeys(takes, 0)
     arrival = {}
-    queues = {}
+    queues = {link: [] for link, _, _ in hops.values()}
     update_arrival = {}
     far_free = 0.0
-
     taken = set()
-    swapped = 0
-    swap_arrival = math.inf
 
     def put(action, which):
         arrived = [hop for hop in arrival if arrival[hop] <= now and hop not in taken]
@@ -389,8 +413,8 @@
     def next_hop():
         for hop in first_choice:
             link, needed, _ = hops[hop]
-            queued = sum(time > now for time in queues.setdefault(link, []))
-            if hop[0] < count["gram"] and hop not in arrival and queued < 2:
+            queued = sum(time > now for time in queues[link])
+            if hop[0] < count["gram"] and hop not in arrival and queued < deepest:
                 if all(arrival.get(need, math.inf) <= now for need in needed):
                     return hop
         return None
@@ -398,7 +422,6 @@
     do("momentum")
     do("gram")
     while count["place"] < experts - 1:
-        hop = next_hop()
         updating = count["update"]
         last = updating == experts - 1
         early = count["place"] < experts - 2 or updating == experts
@@ -406,7 +429,12 @@
         whole = updating < experts and all(arrival.get(h, math.inf) <= now for h in mine)
         if updating == experts - 2:
             whole = whole and len(arrival) == len(hops)
-        squares_in = swap_arrival if swapped == swap_count else math.inf
+        if last:
+            whole = whole and count["place"] >= updating - 1
+        coming = min((time for time in arrival.values() if time > now), default=math.inf)
+        ahead = min(max([0.0] + [time - now for time in queue]) for queue in queues.values())
+        free = last or coming - now >= patience or ahead >= backlog
+        hop = next_hop()
         if hop is not None:
             link, _, passes = hops[hop]
             put("hop", hop)
@@ -418,14 +446,7 @@
             do("gram")
         elif count["momentum"] < experts:
             do("momentum")
-            if count["momentum"] == experts:
-                swap_arrival = now
-        elif swapped < swap_count and swap_arrival <= now:
-            put("swap", swapped)
-            now += issue + pass_over
-            swapped += 1
-            swap_arrival = max([now, *(queue[-1] for queue in queues.values() if queue)]) + latency
-        elif whole and squares_in <= now and (not last or count["place"] >= updating - 1):
+        elif whole and free:
             do("update")
             if updating < experts - 2:
                 far_free = max(now, far_free) + far
@@ -435,7 +456,7 @@
         elif early and update_arrival.get(count["place"], math.inf) <= now:
             do("place")
         else:
-            times = [*arrival.values(), *update_arrival.values(), swap_arrival]
+            times = [*arrival.values(), *update_arrival.values()]
             now = min(time for time in times if time > now)
     return order
 
@@ -473,19 +494,18 @@
     )
     my_places = jnp.take(quarters, order, axis=0).reshape(4 * quarter, 2).T
 
-    uppers = jnp.stack([my_place.side, my_place.upper_line])
+    where = jnp.stack([my_place.side, my_place.upper_line, lax.axis_index("dp")])
 
     distances = list(range(group_count - 1, -1, -1))
     momentum_new = None
     update = None
-    factors, squares, other_squares = None, None, None
-    moved, partial_squares, chains, got, leaving = {}, {}, {}, {}, {}
+    moved, chains, got, leaving = {}, {}, {}, {}
     front = ()
 
     def follow(*values):
         return lax.optimization_barrier((values, front))[0]
 
-    for action, which, arrived_hops in plan(group_count, len(routes.swaps)):
+    for action, which, arrived_hops in plan(group_count):
         taken = follow(*[got[e, kind][name] for e, kind, name in arrived_hops])
         for (e, kind, name), arrival in zip(arrived_hops, taken):
             got[e, kind][name] = arrival
@@ -500,44 +520,29 @@
         elif action == "momentum":
             old_slot, _ = route(my_group, my_group ^ distances[which])
             (old_slot,) = follow(old_slot.reshape(1))
-            momentum_new, moved[which], sums = momentum_step(
-                old_slot, grad, momentum, momentum_new
-            )
-            partial_squares[which] = jnp.sum(sums)
-            front = (sums,)
+            momentum_new, moved[which] = momentum_step(old_slot, grad, momentum, momentum_new)
+            front = (moved[which],)
         elif action == "gram":
             (rows,) = follow(moved[which])
-            parts = gram_step(uppers, rows)
+            parts = gram_step(where, rows)
             chains[which, SideFirst] = SideFirst(routes, my_place, *parts[:2])
             chains[which, LineFirst] = LineFirst(routes, my_place, *parts[2:])
             got[which, SideFirst], got[which, LineFirst] = {}, {}
             front = tuple(parts[3:])
-        elif action == "swap":
-            if which == 0:
-                squares = jnp.stack([partial_squares[e] for e in range(group_count)])
-            else:
-                squares = squares + follow(other_squares)[0]
-            (squares,) = follow(squares)
-            other_squares = send(squares, routes.swaps[which])
-            front = (squares,)
         elif action == "update":
             pieces = chains[which, SideFirst].pieces(got[which, SideFirst])
             pieces += chains[which, LineFirst].pieces(got[which, LineFirst])
             pieces = follow(*pieces)
             new_slot = route(my_group ^ distances[which], my_group)[1].reshape(1)
-            if which == 0:
-                squares = squares + follow(other_squares)[0]
-                factors = 0.5 * math.sqrt(columns) / jnp.sqrt(squares + 1e-06)
-            factor = factors[which].reshape(1)
             rows = moved[which]
             if distances[which] == 0:
                 update = update_step(
-                    new_slot, my_places, factor, rows, pieces, update, local_count
+                    new_slot, my_places, rows, pieces, update, local_count
                 )
                 front = (update,)
             else:
                 here = jnp.zeros((1,), jnp.int32)
-                mine = update_step(here, my_places, factor, rows, pieces)
+                mine = update_step(here, my_places, rows, pieces)
                 pairs = [(g, g ^ distances[which]) for g in range(group_count)]
                 cuts = 4 if distances[which] == 1 and row_count % 64 == 0 else 1
                 cut_rows = [

time: 584 us -> 541 us (0.926)
  starting transfers between devices: 134 us -> 94.9 us
  waiting for transfers between devices: 178 us -> 197 us
  other arithmetic: 59 us -> 43.1 us
  Pallas kernels: 191 us -> 183 us
    ppermute x51 -> x48, starting transfers between devices: 132 us -> 93.5 us  [send(): return lax.ppermute(value, 'dp', pairs)]
    ppermute x6, waiting for transfers between devices: 19.7 us -> 53.5 us  [shards(): lax.ppermute(cut, 'expert', pairs)]
    ppermute x51 -> x48, waiting for transfers between devices: 159 us -> 144 us  [send(): return lax.ppermute(value, 'dp', pairs)]
    convert_element_type x24, other arithmetic: 30.3 us -> 23.7 us  [add_up(): (mine.astype(jnp.float32) + arrived.astype(jnp.float32)).astype(jnp.bfloa...]
    reduce_sum x4 -> x0, other arithmetic: 5.92 us -> none  [shards(): partial_squares[which] = jnp.sum(sums)]
    pallas_call x4, Pallas kernels: 93.5 us -> 87.7 us  [update_step(): pl.pallas_call(update_kernel, grid_spec=pltpu.PrefetchScalarGridSpec(num_...]
  transfers between devices with their start and end apart: 57 -> 54, of which waited for: 19 -> 16; matrix products, arithmetic and copies ran while one was open for 11% -> 9% of each run, Pallas kernels for 29% -> 30%
where the time goes in v6:
time: 541 us; the launch traced here: 531 us
  waiting for transfers between devices  197 us (36%)
  Pallas kernels  183 us (34%)
  starting transfers between devices  94.9 us (18%)
  other arithmetic  43.1 us (8%)
  local copies, waits for them, and re-layouts  10.6 us (2%)
    ppermute x48, waiting for transfers between devices, send(): return lax.ppermute(value, 'dp', pairs)  144 us
    ppermute x48, starting transfers between devices, send(): return lax.ppermute(value, 'dp', pairs)  93.5 us
    pallas_call x4, Pallas kernels, update_step(): pl.pallas_call(update_kernel, grid_spec=pltpu.PrefetchScalarGridSpec(num_...  87.7 us
    ppermute x6, waiting for transfers between devices, shards(): lax.ppermute(cut, 'expert', pairs)  53.5 us
    pallas_call x4, Pallas kernels, momentum_step(): pl.pallas_call(momentum_kernel, grid_spec=pltpu.PrefetchScalarGridSpec(nu...  46 us
    pallas_call x4, Pallas kernels, gram_step(): pl.pallas_call(gram_kernel, in_specs=[pl.BlockSpec(memory_space=pltpu.SME...  35.2 us
    convert_element_type x24, other arithmetic, add_up(): (mine.astype(jnp.float32) + arrived.astype(jnp.float32)).astype(jnp.bfloa...  23.7 us
    pallas_call x3, Pallas kernels, place_step(): pl.pallas_call(functools.partial(place_kernel, cuts), grid_spec=pltpu.Pre...  14.5 us
  transfers between devices with their start and end apart: 54, of which 16 were waited for; matrix products, arithmetic and copies ran while one was open for 9% of the time, Pallas kernels for 30%

profile of v6, /device:TPU:0, one launch (start us, length us, event | category | flops | bytes accessed | tf_op | source)
XLA Modules:
  0.0 531.3 jit_solution(5357564123485520956)
XLA Ops:
  2.2 11.4 %momentum.4 = (f32[4,896,2048]{2,1,0:T(8,128)}, bf16[896,2048]{1,0:T(8,128)(2,1)}) custom-call(s32[1]{0:T(128)} %bitcast.5.order_ref, bf16[4,896,2048]{2,1,0:T(8,128)(2,1)} %grad_ref.7, f32[4,896,2048]{2,1,0:T(8,128)} %momentum_ref.7), custom_call_target="tpu_custom_call" | custom-call | flops 1048576 | bytes 1024 | tf_op jit(solution)/shard_map/momentum/pallas_call | solution.py:43
  14.2 8.8 %gram.4 = (bf16[2304,256]{1,0:T(8,128)(2,1)}, bf16[2304,256]{1,0:T(8,128)(2,1)}, bf16[2320,256]{1,0:T(8,128)(2,1)}, bf16[2320,256]{1,0:T(8,128)(2,1)}) custom-call(s32[3]{0:T(128)} %pad_add_fusion.where_ref, bf16[896,2048]{1,0:T(8,128)(2,1)} %get-tuple-element.185.rows_ref), custom_call_target="tpu_custom_call" | custom-call | flops 1048576 | bytes 1024 | tf_op jit(solution)/shard_map/gram/pallas_call | solution.py:132
  32.9 11.5 %momentum.5 = (f32[4,896,2048]{2,1,0:T(8,128)}, bf16[896,2048]{1,0:T(8,128)(2,1)}) custom-call(s32[1]{0:T(128)} %bitcast.6.order_ref, bf16[4,896,2048]{2,1,0:T(8,128)(2,1)} %grad_ref.7, f32[4,896,2048]{2,1,0:T(8,128)} %momentum_ref.7, f32[4,896,2048]{2,1,0:T(8,128)} %get-tuple-element.194.refs_0_), custom_call_target="tpu_custom_call", output_to_operand_aliasing={{0}: (3, {})} | custom-call | flops 1048576 | bytes 1024 | tf_op jit(solution)/shard_map/momentum/pallas_call | solution.py:43
  44.4 8.9 %gram.5 = (bf16[2304,256]{1,0:T(8,128)(2,1)}, bf16[2304,256]{1,0:T(8,128)(2,1)}, bf16[2320,256]{1,0:T(8,128)(2,1)}, bf16[2320,256]{1,0:T(8,128)(2,1)}) custom-call(s32[3]{0:T(128)} %pad_add_fusion.where_ref, bf16[896,2048]{1,0:T(8,128)(2,1)} %get-tuple-element.196.rows_ref), custom_call_target="tpu_custom_call" | custom-call | flops 1048576 | bytes 1024 | tf_op jit(solution)/shard_map/gram/pallas_call | solution.py:132
  66.3 7.2 %collective-permute-start.1 = (bf16[2304,256]{1,0:T(8,128)(2,1)S(1)}, bf16[2304,256]{1,0:T(8,128)(2,1)}, u32[]{:S(2)}, u32[]{:S(2)}) collective-permute-start(bf16[2304,256]{1,0:T(8,128)(2,1)S(1)} %add_convert_fusion.27), channel_id=1, source_target_pairs={{0,8},{4,12},{24,16},{28,20},{1,9},{5,13},{25,17},{29,21},{2,10},{... | collective-permute-start | bytes 3538952 | tf_op jit(solution)/shard_map/ppermute | solution.py:294
  74.9 11.5 %momentum.6 = (f32[4,896,2048]{2,1,0:T(8,128)}, bf16[896,2048]{1,0:T(8,128)(2,1)}) custom-call(s32[1]{0:T(128)} %bitcast.7.order_ref, bf16[4,896,2048]{2,1,0:T(8,128)(2,1)} %grad_ref.7, f32[4,896,2048]{2,1,0:T(8,128)} %momentum_ref.7, f32[4,896,2048]{2,1,0:T(8,128)} %get-tuple-element.210.refs_0_), custom_call_target="tpu_custom_call", output_to_operand_aliasing={{0}: (3, {})} | custom-call | flops 1048576 | bytes 1024 | tf_op jit(solution)/shard_map/momentum/pallas_call | solution.py:43
  88.9 8.8 %gram.6 = (bf16[2304,256]{1,0:T(8,128)(2,1)}, bf16[2304,256]{1,0:T(8,128)(2,1)}, bf16[2320,256]{1,0:T(8,128)(2,1)}, bf16[2320,256]{1,0:T(8,128)(2,1)}) custom-call(s32[3]{0:T(128)} %pad_add_fusion.where_ref, bf16[896,2048]{1,0:T(8,128)(2,1)} %get-tuple-element.213.rows_ref), custom_call_target="tpu_custom_call" | custom-call | flops 1048576 | bytes 1024 | tf_op jit(solution)/shard_map/gram/pallas_call | solution.py:132
  110.3 11.5 %momentum.7 = (f32[4,896,2048]{2,1,0:T(8,128)}, bf16[896,2048]{1,0:T(8,128)(2,1)}) custom-call(s32[1]{0:T(128)} %bitcast.1.order_ref, bf16[4,896,2048]{2,1,0:T(8,128)(2,1)} %grad_ref.7, f32[4,896,2048]{2,1,0:T(8,128)} %momentum_ref.7, f32[4,896,2048]{2,1,0:T(8,128)} %get-tuple-element.230.refs_0_), custom_call_target="tpu_custom_call", output_to_operand_aliasing={{0}: (3, {})} | custom-call | flops 1048576 | bytes 1024 | tf_op jit(solution)/shard_map/momentum/pallas_call | solution.py:43
  121.8 8.7 %gram.7 = (bf16[2304,256]{1,0:T(8,128)(2,1)}, bf16[2304,256]{1,0:T(8,128)(2,1)}, bf16[2320,256]{1,0:T(8,128)(2,1)}, bf16[2320,256]{1,0:T(8,128)(2,1)}) custom-call(s32[3]{0:T(128)} %pad_add_fusion.where_ref, bf16[896,2048]{1,0:T(8,128)(2,1)} %get-tuple-element.233.rows_ref), custom_call_target="tpu_custom_call" | custom-call | flops 1048576 | bytes 1024 | tf_op jit(solution)/shard_map/gram/pallas_call | solution.py:132
  138.9 19.1 %collective-permute-done.11 = bf16[2320,256]{1,0:T(8,128)(2,1)} collective-permute-done((bf16[2320,256]{1,0:T(8,128)(2,1)}, bf16[2320,256]{1,0:T(8,128)(2,1)}, u32[]{:S(2)}, u32[]{:S(2)}) %collective-permute-start.11) | collective-permute-done | bytes 1187872 | tf_op jit(solution)/shard_map/ppermute | solution.py:294
  158.1 7.9 %collective-permute-start.18 = (bf16[2320,256]{1,0:T(8,128)(2,1)S(1)}, bf16[2320,256]{1,0:T(8,128)(2,1)S(1)}, u32[]{:S(2)}, u32[]{:S(2)}) collective-permute-start(bf16[2320,256]{1,0:T(8,128)(2,1)S(1)} %copy-done.7), channel_id=1, source_target_pairs={{0,8},{4,12},{24,16},{28,20},{1,9},{5,13},{25,17},{29,21},{2,10},{... | collective-permute-start | bytes 3563528 | tf_op jit(solution)/shard_map/ppermute | solution.py:294
  170.9 12.3 %collective-permute-done.6 = bf16[2304,256]{1,0:T(8,128)(2,1)} collective-permute-done((bf16[2304,256]{1,0:T(8,128)(2,1)S(1)}, bf16[2304,256]{1,0:T(8,128)(2,1)}, u32[]{:S(2)}, u32[]{:S(2)}) %collective-permute-start.6) | collective-permute-done | bytes 1179680 | tf_op jit(solution)/shard_map/ppermute | solution.py:294
  193.1 17.5 %collective-permute-done.16 = bf16[2320,256]{1,0:T(8,128)(2,1)S(1)} collective-permute-done((bf16[2320,256]{1,0:T(8,128)(2,1)S(1)}, bf16[2320,256]{1,0:T(8,128)(2,1)S(1)}, u32[]{:S(2)}, u32[]{:S(2)}) %collective-permute-start.16) | collective-permute-done | bytes 1187872 | tf_op jit(solution)/shard_map/ppermute | solution.py:294
  217.2 30.5 %collective-permute-done.27 = bf16[2320,256]{1,0:T(8,128)(2,1)S(1)} collective-permute-done((bf16[2320,256]{1,0:T(8,128)(2,1)S(1)}, bf16[2320,256]{1,0:T(8,128)(2,1)S(1)}, u32[]{:S(2)}, u32[]{:S(2)}) %collective-permute-start.27) | collective-permute-done | bytes 1187872 | tf_op jit(solution)/shard_map/ppermute | solution.py:294
  253.9 21.8 %update.4 = bf16[1,896,2048]{2,1,0:T(8,128)(2,1)} custom-call(s32[1]{0:T(128)} %constant.121.clone.1.slot_ref, s32[2,36]{1,0:T(2,128)} %select_bitcast_fusion.place_ref, bf16[896,2048]{1,0:T(8,128)(2,1)} %get-tuple-element.185.rows_ref, bf16[2304,256]{1,0:T(8,128)(2,1)} %copy-done.2, bf16[2304,256]{1,0:T(8,128)(2,1)} %copy-done.16, ...), custom_call_target="tpu_custom_call" | custom-call | flops 1048576 | bytes 1024 | tf_op jit(solution)/shard_map/update/pallas_call | solution.py:216
  296.2 9.6 %collective-permute-done.31 = bf16[2320,256]{1,0:T(8,128)(2,1)S(1)} collective-permute-done((bf16[2320,256]{1,0:T(8,128)(2,1)S(1)}, bf16[2320,256]{1,0:T(8,128)(2,1)S(1)}, u32[]{:S(2)}, u32[]{:S(2)}) %collective-permute-start.31) | collective-permute-done | bytes 1187872 | tf_op jit(solution)/shard_map/ppermute | solution.py:294
  309.7 18.7 %collective-permute-done.17 = bf16[2304,256]{1,0:T(8,128)(2,1)S(1)} collective-permute-done((bf16[2304,256]{1,0:T(8,128)(2,1)S(1)}, bf16[2304,256]{1,0:T(8,128)(2,1)S(1)}, u32[]{:S(2)}, u32[]{:S(2)}) %collective-permute-start.17) | collective-permute-done | bytes 1179680 | tf_op jit(solution)/shard_map/ppermute | solution.py:294
  333.6 11.2 %collective-permute-done.37 = bf16[2304,256]{1,0:T(8,128)(2,1)S(1)} collective-permute-done((bf16[2304,256]{1,0:T(8,128)(2,1)S(1)}, bf16[2304,256]{1,0:T(8,128)(2,1)S(1)}, u32[]{:S(2)}, u32[]{:S(2)}) %collective-permute-start.37) | collective-permute-done | bytes 1179680 | tf_op jit(solution)/shard_map/ppermute | solution.py:294
  357.0 8.6 %collective-permute-done.38.refs_1_ = bf16[2304,256]{1,0:T(8,128)(2,1)S(1)} collective-permute-done((bf16[2304,256]{1,0:T(8,128)(2,1)S(1)}, bf16[2304,256]{1,0:T(8,128)(2,1)S(1)}, u32[]{:S(2)}, u32[]{:S(2)}) %collective-permute-start.38) | collective-permute-done | bytes 1179680 | tf_op jit(solution)/shard_map/ppermute | solution.py:294
  368.2 21.6 %update.5 = bf16[1,896,2048]{2,1,0:T(8,128)(2,1)} custom-call(s32[1]{0:T(128)} %constant.121.clone.1.slot_ref, s32[2,36]{1,0:T(2,128)} %select_bitcast_fusion.place_ref, bf16[896,2048]{1,0:T(8,128)(2,1)} %get-tuple-element.196.rows_ref, bf16[2304,256]{1,0:T(8,128)(2,1)} %copy-done.1, bf16[2304,256]{1,0:T(8,128)(2,1)} %copy-done.14, ...), custom_call_target="tpu_custom_call" | custom-call | flops 1048576 | bytes 1024 | tf_op jit(solution)/shard_map/update/pallas_call | solution.py:216
  397.1 18.0 %collective-permute-done.44.refs_0_ = bf16[1,896,2048]{2,1,0:T(8,128)(2,1)} collective-permute-done((bf16[1,896,2048]{2,1,0:T(8,128)(2,1)}, bf16[1,896,2048]{2,1,0:T(8,128)(2,1)}, u32[]{:S(2)}, u32[]{:S(2)}) %collective-permute-start.44) | collective-permute-done | bytes 3670048 | tf_op jit(solution)/shard_map/ppermute | solution.py:549
  433.0 21.7 %update.6 = bf16[1,896,2048]{2,1,0:T(8,128)(2,1)} custom-call(s32[1]{0:T(128)} %constant.121.clone.1.slot_ref, s32[2,36]{1,0:T(2,128)} %select_bitcast_fusion.place_ref, bf16[896,2048]{1,0:T(8,128)(2,1)} %get-tuple-element.213.rows_ref, bf16[2304,256]{1,0:T(8,128)(2,1)} %copy-done, bf16[2304,256]{1,0:T(8,128)(2,1)} %copy-done.13, ...), custom_call_target="tpu_custom_call" | custom-call | flops 1048576 | bytes 1024 | tf_op jit(solution)/shard_map/update/pallas_call | solution.py:216
  458.3 35.5 %collective-permute-done.49.refs_0_ = bf16[1,896,2048]{2,1,0:T(8,128)(2,1)} collective-permute-done((bf16[1,896,2048]{2,1,0:T(8,128)(2,1)}, bf16[1,896,2048]{2,1,0:T(8,128)(2,1)}, u32[]{:S(2)}, u32[]{:S(2)}) %collective-permute-start.49) | collective-permute-done | bytes 3670048 | tf_op jit(solution)/shard_map/ppermute | solution.py:549
  502.3 22.6 %update.7.refs_4_ = bf16[4,896,2048]{2,1,0:T(8,128)(2,1)} custom-call(s32[1]{0:T(128)} %bitcast.10.slot_ref, s32[2,36]{1,0:T(2,128)} %select_bitcast_fusion.place_ref, bf16[896,2048]{1,0:T(8,128)(2,1)} %get-tuple-element.233.rows_ref, bf16[2304,256]{1,0:T(8,128)(2,1)} %copy-done.3, bf16[2304,256]{1,0:T(8,128)(2,1)} %copy-done.15, ...), custom_call_target="tpu_custom_call", output_to_operand_aliasing={{}: (7, {})} | custom-call | flops 1048576 | bytes 1024 | tf_op jit(solution)/shard_map/update/pallas_call | solution.py:216
  (193 shorter events, 164.4 us)
Async XLA Ops:
  30.5 55.9 %collective-permute-start.3 = (bf16[2320,256]{1,0:T(8,128)(2,1)}, bf16[2320,256]{1,0:T(8,128)(2,1)}, u32[]{:S(2)}, u32[]{:S(2)}) collective-permute-start(bf16[2320,256]{1,0:T(8,128)(2,1)} %get-tuple-element.192), channel_id=1, source_target_pairs={{0,8},{4,12},{24,16},{28,20},{1,9},{5,13},{25,17},{29,21},{2,10},{... | collective-permute-start | bytes 3563528 | tf_op jit(solution)/shard_map/ppermute | solution.py:294
  53.3 44.4 %collective-permute-start.5 = (bf16[2304,256]{1,0:T(8,128)(2,1)}, bf16[2304,256]{1,0:T(8,128)(2,1)}, u32[]{:S(2)}, u32[]{:S(2)}) collective-permute-start(bf16[2304,256]{1,0:T(8,128)(2,1)} %get-tuple-element.199), channel_id=1, source_target_pairs={{0,4},{4,0},{8,12},{12,8},{16,20},{20,16},{24,28},{28,24},{1,5},{5... | collective-permute-start | bytes 3538952 | tf_op jit(solution)/shard_map/ppermute | solution.py:294
  58.1 43.7 %collective-permute-start.4 = (bf16[2320,256]{1,0:T(8,128)(2,1)S(1)}, bf16[2320,256]{1,0:T(8,128)(2,1)}, u32[]{:S(2)}, u32[]{:S(2)}) collective-permute-start(bf16[2320,256]{1,0:T(8,128)(2,1)S(1)} %add_convert_fusion.15), channel_id=1, source_target_pairs={{8,16},{12,20},{16,8},{20,12},{9,17},{13,21},{17,9},{21,13},{10,18... | collective-permute-start | bytes 3563528 | tf_op jit(solution)/shard_map/ppermute | solution.py:294
  66.3 40.8 %collective-permute-start.1 = (bf16[2304,256]{1,0:T(8,128)(2,1)S(1)}, bf16[2304,256]{1,0:T(8,128)(2,1)}, u32[]{:S(2)}, u32[]{:S(2)}) collective-permute-start(bf16[2304,256]{1,0:T(8,128)(2,1)S(1)} %add_convert_fusion.27), channel_id=1, source_target_pairs={{0,8},{4,12},{24,16},{28,20},{1,9},{5,13},{25,17},{29,21},{2,10},{... | collective-permute-start | bytes 3538952 | tf_op jit(solution)/shard_map/ppermute | solution.py:294
  73.5 59.0 %collective-permute-start.8 = (bf16[2320,256]{1,0:T(8,128)(2,1)S(1)}, bf16[2320,256]{1,0:T(8,128)(2,1)S(1)}, u32[]{:S(2)}, u32[]{:S(2)}) collective-permute-start(bf16[2320,256]{1,0:T(8,128)(2,1)S(1)} %copy-done.8), channel_id=1, source_target_pairs={{0,8},{4,12},{24,16},{28,20},{1,9},{5,13},{25,17},{29,21},{2,10},{... | collective-permute-start | bytes 3563528 | tf_op jit(solution)/shard_map/ppermute | solution.py:294
  86.4 71.6 %collective-permute-start.11 = (bf16[2320,256]{1,0:T(8,128)(2,1)}, bf16[2320,256]{1,0:T(8,128)(2,1)}, u32[]{:S(2)}, u32[]{:S(2)}) collective-permute-start(bf16[2320,256]{1,0:T(8,128)(2,1)} %get-tuple-element.208), channel_id=1, source_target_pairs={{0,8},{4,12},{24,16},{28,20},{1,9},{5,13},{25,17},{29,21},{2,10},{... | collective-permute-start | bytes 3563528 | tf_op jit(solution)/shard_map/ppermute | solution.py:294
  99.5 83.8 %collective-permute-start.6 = (bf16[2304,256]{1,0:T(8,128)(2,1)S(1)}, bf16[2304,256]{1,0:T(8,128)(2,1)}, u32[]{:S(2)}, u32[]{:S(2)}) collective-permute-start(bf16[2304,256]{1,0:T(8,128)(2,1)S(1)} %add_convert_fusion.26), channel_id=1, source_target_pairs={{0,8},{4,12},{24,16},{28,20},{1,9},{5,13},{25,17},{29,21},{2,10},{... | collective-permute-start | bytes 3538952 | tf_op jit(solution)/shard_map/ppermute | solution.py:294
  137.9 46.6 %collective-permute-start.10 = (bf16[2304,256]{1,0:T(8,128)(2,1)S(1)}, bf16[2304,256]{1,0:T(8,128)(2,1)S(1)}, u32[]{:S(2)}, u32[]{:S(2)}) collective-permute-start(bf16[2304,256]{1,0:T(8,128)(2,1)S(1)} %copy-done.22), channel_id=1, source_target_pairs={{0,4},{4,0},{8,12},{12,8},{16,20},{20,16},{24,28},{28,24},{1,5},{5... | collective-permute-start | bytes 3538952 | tf_op jit(solution)/shard_map/ppermute | solution.py:294
  158.1 54.7 %collective-permute-start.18 = (bf16[2320,256]{1,0:T(8,128)(2,1)S(1)}, bf16[2320,256]{1,0:T(8,128)(2,1)S(1)}, u32[]{:S(2)}, u32[]{:S(2)}) collective-permute-start(bf16[2320,256]{1,0:T(8,128)(2,1)S(1)} %copy-done.7), channel_id=1, source_target_pairs={{0,8},{4,12},{24,16},{28,20},{1,9},{5,13},{25,17},{29,21},{2,10},{... | collective-permute-start | bytes 3563528 | tf_op jit(solution)/shard_map/ppermute | solution.py:294
  166.0 84.5 %collective-permute-start.24 = (bf16[2304,256]{1,0:T(8,128)(2,1)S(1)}, bf16[2304,256]{1,0:T(8,128)(2,1)S(1)}, u32[]{:S(2)}, u32[]{:S(2)}) collective-permute-start(bf16[2304,256]{1,0:T(8,128)(2,1)S(1)} %add_convert_fusion.24), channel_id=1, source_target_pairs={{0,8},{4,12},{24,16},{28,20},{1,9},{5,13},{25,17},{29,21},{2,10},{... | collective-permute-start | bytes 3538952 | tf_op jit(solution)/shard_map/ppermute | solution.py:294
  184.5 91.2 %collective-permute-start.21 = (bf16[2320,256]{1,0:T(8,128)(2,1)S(1)}, bf16[2320,256]{1,0:T(8,128)(2,1)}, u32[]{:S(2)}, u32[]{:S(2)}) collective-permute-start(bf16[2320,256]{1,0:T(8,128)(2,1)S(1)} %copy-done.11), channel_id=1, source_target_pairs={{0,8},{4,12},{24,16},{28,20},{1,9},{5,13},{25,17},{29,21},{2,10},{... | collective-permute-start | bytes 3563528 | tf_op jit(solution)/shard_map/ppermute | solution.py:294
  212.8 39.5 %collective-permute-start.25 = (bf16[2304,256]{1,0:T(8,128)(2,1)S(1)}, bf16[2304,256]{1,0:T(8,128)(2,1)S(1)}, u32[]{:S(2)}, u32[]{:S(2)}) collective-permute-start(bf16[2304,256]{1,0:T(8,128)(2,1)S(1)} %broadcast_select_fusion.11.refs_0_), channel_id=1, source_target_pairs={{0,4},{4,0},{8,12},{12,8},{16,20},{20,16},{24,28},{28,24},{1,5},{5... | collective-permute-start | bytes 3538952 | tf_op jit(solution)/shard_map/ppermute | solution.py:294
  215.5 66.0 %collective-permute-start.23 = (bf16[2320,256]{1,0:T(8,128)(2,1)S(1)}, bf16[2320,256]{1,0:T(8,128)(2,1)}, u32[]{:S(2)}, u32[]{:S(2)}) collective-permute-start(bf16[2320,256]{1,0:T(8,128)(2,1)S(1)} %add_convert_fusion.7), channel_id=1, source_target_pairs={{8,0},{12,4},{16,24},{20,28},{9,1},{13,5},{17,25},{21,29},{10,2},{... | collective-permute-start | bytes 3563528 | tf_op jit(solution)/shard_map/ppermute | solution.py:294
  252.3 41.2 %collective-permute-start.32 = (bf16[2304,256]{1,0:T(8,128)(2,1)S(1)}, bf16[2304,256]{1,0:T(8,128)(2,1)}, u32[]{:S(2)}, u32[]{:S(2)}) collective-permute-start(bf16[2304,256]{1,0:T(8,128)(2,1)S(1)} %add_convert_fusion.20), channel_id=1, source_target_pairs={{8,0},{12,4},{16,24},{20,28},{9,1},{13,5},{17,25},{21,29},{10,2},{... | collective-permute-start | bytes 3538952 | tf_op jit(solution)/shard_map/ppermute | solution.py:294
  281.5 46.9 %collective-permute-start.17 = (bf16[2304,256]{1,0:T(8,128)(2,1)S(1)}, bf16[2304,256]{1,0:T(8,128)(2,1)S(1)}, u32[]{:S(2)}, u32[]{:S(2)}) collective-permute-start(bf16[2304,256]{1,0:T(8,128)(2,1)S(1)} %add_convert_fusion.21), channel_id=1, source_target_pairs={{0,8},{4,12},{24,16},{28,20},{1,9},{5,13},{25,17},{29,21},{2,10},{... | collective-permute-start | bytes 3538952 | tf_op jit(solution)/shard_map/ppermute | solution.py:294
  293.5 39.6 %collective-permute-start.28 = (bf16[2320,256]{1,0:T(8,128)(2,1)}, bf16[2320,256]{1,0:T(8,128)(2,1)S(1)}, u32[]{:S(2)}, u32[]{:S(2)}) collective-permute-start(bf16[2320,256]{1,0:T(8,128)(2,1)} %collective-permute-done.20), channel_id=1, source_target_pairs={{8,0},{12,4},{16,24},{20,28},{9,1},{13,5},{17,25},{21,29},{10,2},{... | collective-permute-start | bytes 3563528 | tf_op jit(solution)/shard_map/ppermute | solution.py:294
  305.8 39.7 %collective-permute-start.35 = (bf16[2304,256]{1,0:T(8,128)(2,1)S(1)}, bf16[2304,256]{1,0:T(8,128)(2,1)S(1)}, u32[]{:S(2)}, u32[]{:S(2)}) collective-permute-start(bf16[2304,256]{1,0:T(8,128)(2,1)S(1)} %broadcast_select_fusion.10.refs_0_), channel_id=1, source_target_pairs={{0,4},{4,0},{8,12},{12,8},{16,20},{20,16},{24,28},{28,24},{1,5},{5... | collective-permute-start | bytes 3538952 | tf_op jit(solution)/shard_map/ppermute | solution.py:294
  333.1 82.0 %collective-permute-start.44 = (bf16[1,896,2048]{2,1,0:T(8,128)(2,1)}, bf16[1,896,2048]{2,1,0:T(8,128)(2,1)}, u32[]{:S(2)}, u32[]{:S(2)}) collective-permute-start(bf16[1,896,2048]{2,1,0:T(8,128)(2,1)} %update.4), channel_id=1, source_target_pairs={{0,3},{1,2},{2,1},{3,0},{4,7},{5,6},{6,5},{7,4},{8,11},{9,10},{10,... | collective-permute-start | bytes 11010056 | tf_op jit(solution)/shard_map/ppermute | solution.py:549
  355.2 64.6 %collective-permute-start.42 = (bf16[2320,256]{1,0:T(8,128)(2,1)S(1)}, bf16[2320,256]{1,0:T(8,128)(2,1)}, u32[]{:S(2)}, u32[]{:S(2)}) collective-permute-start(bf16[2320,256]{1,0:T(8,128)(2,1)S(1)} %add_convert_fusion.1), channel_id=1, source_target_pairs={{8,12},{12,8},{16,20},{20,16},{9,13},{13,9},{17,21},{21,17},{10,14... | collective-permute-start | bytes 3563528 | tf_op jit(solution)/shard_map/ppermute | solution.py:294
  393.2 100.6 %collective-permute-start.49 = (bf16[1,896,2048]{2,1,0:T(8,128)(2,1)}, bf16[1,896,2048]{2,1,0:T(8,128)(2,1)}, u32[]{:S(2)}, u32[]{:S(2)}) collective-permute-start(bf16[1,896,2048]{2,1,0:T(8,128)(2,1)} %update.5), channel_id=1, source_target_pairs={{0,2},{1,3},{2,0},{3,1},{4,6},{5,7},{6,4},{7,5},{8,10},{9,11},{10,... | collective-permute-start | bytes 11010056 | tf_op jit(solution)/shard_map/ppermute | solution.py:549
  431.5 69.6 %collective-permute-start.48 = (bf16[2320,256]{1,0:T(8,128)(2,1)}, bf16[2320,256]{1,0:T(8,128)(2,1)S(1)}, u32[]{:S(2)}, u32[]{:S(2)}) collective-permute-start(bf16[2320,256]{1,0:T(8,128)(2,1)} %collective-permute-done.47), channel_id=1, source_target_pairs={{8,0},{12,4},{16,24},{20,28},{9,1},{13,5},{17,25},{21,29},{10,2},{... | collective-permute-start | bytes 3563528 | tf_op jit(solution)/shard_map/ppermute | solution.py:294
  457.6 67.3 %collective-permute-start.50 = (bf16[1,224,2048]{2,1,0:T(8,128)(2,1)S(1)}, bf16[1,224,2048]{2,1,0:T(8,128)(2,1)S(1)}, u32[]{:S(2)}, u32[]{:S(2)}) collective-permute-start(bf16[1,224,2048]{2,1,0:T(8,128)(2,1)S(1)} %get-tuple-element.377), channel_id=1, source_target_pairs={{0,1},{1,0},{2,3},{3,2},{4,5},{5,4},{6,7},{7,6},{8,9},{9,8},{10,11... | collective-permute-start | bytes 2752520 | tf_op jit(solution)/shard_map/ppermute | solution.py:549
  457.7 67.2 %collective-permute-start.51 = (bf16[1,224,2048]{2,1,0:T(8,128)(2,1)S(1)}, bf16[1,224,2048]{2,1,0:T(8,128)(2,1)}, u32[]{:S(2)}, u32[]{:S(2)}) collective-permute-start(bf16[1,224,2048]{2,1,0:T(8,128)(2,1)S(1)} %get-tuple-element.376), channel_id=1, source_target_pairs={{0,1},{1,0},{2,3},{3,2},{4,5},{5,4},{6,7},{7,6},{8,9},{9,8},{10,11... | collective-permute-start | bytes 2752520 | tf_op jit(solution)/shard_map/ppermute | solution.py:549
  458.2 66.7 %collective-permute-start.52 = (bf16[1,224,2048]{2,1,0:T(8,128)(2,1)S(1)}, bf16[1,224,2048]{2,1,0:T(8,128)(2,1)}, u32[]{:S(2)}, u32[]{:S(2)}) collective-permute-start(bf16[1,224,2048]{2,1,0:T(8,128)(2,1)S(1)} %get-tuple-element.375), channel_id=1, source_target_pairs={{0,1},{1,0},{2,3},{3,2},{4,5},{5,4},{6,7},{7,6},{8,9},{9,8},{10,11... | collective-permute-start | bytes 2752520 | tf_op jit(solution)/shard_map/ppermute | solution.py:549
  (53 other events, 1026.0 us)

commit v7 on v6

--- a/solution.py
+++ b/solution.py
@@ -161,9 +161,10 @@
     return total
 
 
-def update_kernel(slot_ref, place_ref, rows_ref, *refs):
+def update_kernel(cuts, slot_ref, place_ref, rows_ref, *refs):
     pieces = refs[:4]
-    out_ref, gram_ref, normal_ref, product_ref = refs[-4:]
+    gram_ref, normal_ref, product_ref = refs[-3:]
+    out_refs = refs[-3 - cuts : -3]
     columns = gram_ref.shape[0]
     count = columns // BLOCK
     piece_blocks = pieces[0].shape[0] // BLOCK
@@ -199,7 +200,12 @@
             - 4.775 * product_ref[:, here].astype(jnp.float32)
             + 2.0315 * second
         )
-        out_ref[0, :, here] = (orthogonal * math.sqrt(D)).astype(jnp.bfloat16)
+        result = (orthogonal * math.sqrt(D)).astype(jnp.bfloat16)
+        for number, out_ref in enumerate(out_refs):
+
+            @pl.when((pl.program_id(0) == number) | (cuts == 1))
+            def _():
+                out_ref[0, :, here] = result
 
 
 def update_step(slot, places, moved, pieces, earlier=None, count=1):
@@ -208,25 +214,32 @@
     in_specs = [pl.BlockSpec((step, columns), lambda r, *_: (r, 0))]
     in_specs += [pl.BlockSpec(piece.shape, lambda r, *_: (0, 0)) for piece in pieces]
     operands = [slot, places, moved, *pieces]
-    aliases = {}
-    if earlier is not None:
+    if earlier is None:
+        aliases = {}
+        cuts = rows // step
+        out_specs = [pl.BlockSpec((1, step, columns), lambda r, *_: (0, 0, 0))] * cuts
+        out_shape = [jax.ShapeDtypeStruct((1, step, columns), jnp.bfloat16)] * cuts
+    else:
         in_specs.append(pl.BlockSpec(memory_space=pl.ANY))
         operands.append(earlier)
         aliases = {7: 0}
+        cuts = 1
+        out_specs = [pl.BlockSpec((1, step, columns), lambda r, slot, *_: (slot[0], r, 0))]
+        out_shape = [jax.ShapeDtypeStruct((count, rows, columns), jnp.bfloat16)]
     return pl.pallas_call(
-        update_kernel,
+        functools.partial(update_kernel, cuts),
         grid_spec=pltpu.PrefetchScalarGridSpec(
             num_scalar_prefetch=2,
             grid=(rows // step,),
             in_specs=in_specs,
-            out_specs=pl.BlockSpec((1, step, columns), lambda r, slot, *_: (slot[0], r, 0)),
+            out_specs=out_specs,
             scratch_shapes=[
                 pltpu.VMEM((columns, columns), jnp.bfloat16),
                 pltpu.VMEM((step, columns), jnp.bfloat16),
                 pltpu.VMEM((step, columns), jnp.bfloat16),
             ],
         ),
-        out_shape=jax.ShapeDtypeStruct((count, rows, columns), jnp.bfloat16),
+        out_shape=out_shape,
         input_output_aliases=aliases,
         compiler_params=pltpu.CompilerParams(vmem_limit_bytes=VMEM_BYTES),
         cost_estimate=SMALL_COST,
@@ -370,7 +383,7 @@
 def plan(experts):
     transfer, latency, issue, pass_over = 23.3, 3.0, 2.5, 1.8
     takes = {"momentum": 12.0, "gram": 9.0, "update": 28.0, "place": 5.0}
-    near, far = 12.0, 78.0
+    near, far = 12.0, 96.0
     deepest, patience, backlog = 4, 4.0, 10.0
     hops = {}
     for expert in range(experts):
@@ -397,6 +410,7 @@
     queues = {link: [] for link, _, _ in hops.values()}
     update_arrival = {}
     far_free = 0.0
+    halfway = {}
     taken = set()
 
     def put(action, which):
@@ -424,13 +438,12 @@
     while count["place"] < experts - 1:
         updating = count["update"]
         last = updating == experts - 1
-        early = count["place"] < experts - 2 or updating == experts
         mine = [h for h in hops if h[0] == updating]
         whole = updating < experts and all(arrival.get(h, math.inf) <= now for h in mine)
         if updating == experts - 2:
             whole = whole and len(arrival) == len(hops)
         if last:
-            whole = whole and count["place"] >= updating - 1
+            whole = whole and update_arrival.get(count["place"], math.inf) > now
         coming = min((time for time in arrival.values() if time > now), default=math.inf)
         ahead = min(max([0.0] + [time - now for time in queue]) for queue in queues.values())
         free = last or coming - now >= patience or ahead >= backlog
@@ -449,14 +462,18 @@
         elif whole and free:
             do("update")
             if updating < experts - 2:
+                halfway[updating] = max(now, far_free) + far / 3
                 far_free = max(now, far_free) + far
                 update_arrival[updating] = far_free
             else:
                 update_arrival[updating] = now + near
-        elif early and update_arrival.get(count["place"], math.inf) <= now:
+        elif any(time <= now for time in halfway.values()):
+            put("half", min(halfway))
+            del halfway[min(halfway)]
+        elif update_arrival.get(count["place"], math.inf) <= now:
             do("place")
         else:
-            times = [*arrival.values(), *update_arrival.values()]
+            times = [*arrival.values(), *update_arrival.values(), *halfway.values()]
             now = min(time for time in times if time > now)
     return order
 
@@ -536,20 +553,22 @@
             new_slot = route(my_group ^ distances[which], my_group)[1].reshape(1)
             rows = moved[which]
             if distances[which] == 0:
-                update = update_step(
+                (update,) = update_step(
                     new_slot, my_places, rows, pieces, update, local_count
                 )
                 front = (update,)
             else:
                 here = jnp.zeros((1,), jnp.int32)
-                mine = update_step(here, my_places, rows, pieces)
+                cuts = update_step(here, my_places, rows, pieces)
+                front = (cuts[0],)
+                if distances[which] == 1 and row_count % 64 == 0:
+                    cuts = [part for cut in cuts for part in jnp.split(cut, 4 // len(cuts), axis=1)]
                 pairs = [(g, g ^ distances[which]) for g in range(group_count)]
-                cuts = 4 if distances[which] == 1 and row_count % 64 == 0 else 1
-                cut_rows = [
-                    lax.ppermute(cut, "expert", pairs) for cut in jnp.split(mine, cuts, axis=1)
-                ]
-                leaving[which] = new_slot, cut_rows
-                front = (mine,)
+                leaving[which] = new_slot, [lax.ppermute(cut, "expert", pairs) for cut in cuts]
+        elif action == "half":
+            new_slot, arrived = leaving[which]
+            front = (*front, *follow(arrived[0]))
+            leaving[which] = new_slot, [front[-1], *arrived[1:]]
         else:
             new_slot, arrived = leaving[which]
             (new_slot,) = follow(new_slot)

time: 541 us -> 576 us (1.065)
  Pallas kernels: 183 us -> 214 us
  starting transfers between devices: 94.9 us -> 105 us
    pallas_call x4, Pallas kernels: 87.7 us -> 119 us  [update_step(): pl.pallas_call(functools.partial(update_kernel, cuts), grid_spec=pltpu.Pr...]
    ppermute x48, waiting for transfers between devices: 144 us -> 163 us  [send(): return lax.ppermute(value, 'dp', pairs)]
    ppermute x6 -> x8, waiting for transfers between devices: 53.5 us -> 35.4 us  [shards(): lax.ppermute(cut, 'expert', pairs)]
    ppermute x48, starting transfers between devices: 93.5 us -> 101 us  [send(): return lax.ppermute(value, 'dp', pairs)]
  transfers between devices with their start and end apart: 54 -> 56, of which waited for: 16 -> 13; matrix products, arithmetic and copies ran while one was open for 9% -> 8% of each run, Pallas kernels for 30% -> 33%
where the time goes in v7:
time: 576 us; the launch traced here: 571 us
  Pallas kernels  214 us (37%)
  waiting for transfers between devices  199 us (35%)
  starting transfers between devices  105 us (18%)
  other arithmetic  40.2 us (7%)
  local copies, waits for them, and re-layouts  11.6 us (2%)
    ppermute x48, waiting for transfers between devices, send(): return lax.ppermute(value, 'dp', pairs)  163 us
    pallas_call x4, Pallas kernels, update_step(): pl.pallas_call(functools.partial(update_kernel, cuts), grid_spec=pltpu.Pr...  119 us
    ppermute x48, starting transfers between devices, send(): return lax.ppermute(value, 'dp', pairs)  101 us
    pallas_call x4, Pallas kernels, momentum_step(): pl.pallas_call(momentum_kernel, grid_spec=pltpu.PrefetchScalarGridSpec(nu...  46.1 us
    ppermute x8, waiting for transfers between devices, shards(): lax.ppermute(cut, 'expert', pairs)  35.4 us
    pallas_call x4, Pallas kernels, gram_step(): pl.pallas_call(gram_kernel, in_specs=[pl.BlockSpec(memory_space=pltpu.SME...  35 us
    convert_element_type x24, other arithmetic, add_up(): (mine.astype(jnp.float32) + arrived.astype(jnp.float32)).astype(jnp.bfloa...  21.6 us
    pallas_call x3, Pallas kernels, place_step(): pl.pallas_call(functools.partial(place_kernel, cuts), grid_spec=pltpu.Pre...  14.2 us
  transfers between devices with their start and end apart: 56, of which 13 were waited for; matrix products, arithmetic and copies ran while one was open for 8% of the time, Pallas kernels for 33%

profile of v7, /device:TPU:0, one launch (start us, length us, event | category | flops | bytes accessed | tf_op | source)
XLA Modules:
  0.0 570.8 jit_solution(8845209880583655522)
XLA Ops:
  2.2 11.5 %momentum.4 = (f32[4,896,2048]{2,1,0:T(8,128)}, bf16[896,2048]{1,0:T(8,128)(2,1)}) custom-call(s32[1]{0:T(128)} %bitcast.5.order_ref, bf16[4,896,2048]{2,1,0:T(8,128)(2,1)} %grad_ref.7, f32[4,896,2048]{2,1,0:T(8,128)} %momentum_ref.7), custom_call_target="tpu_custom_call" | custom-call | flops 1048576 | bytes 1024 | tf_op jit(solution)/shard_map/momentum/pallas_call | solution.py:43
  14.4 8.8 %gram.4 = (bf16[2304,256]{1,0:T(8,128)(2,1)}, bf16[2304,256]{1,0:T(8,128)(2,1)}, bf16[2320,256]{1,0:T(8,128)(2,1)}, bf16[2320,256]{1,0:T(8,128)(2,1)}) custom-call(s32[3]{0:T(128)} %pad_add_fusion.where_ref, bf16[896,2048]{1,0:T(8,128)(2,1)} %get-tuple-element.193.rows_ref), custom_call_target="tpu_custom_call" | custom-call | flops 1048576 | bytes 1024 | tf_op jit(solution)/shard_map/gram/pallas_call | solution.py:132
  32.0 11.6 %momentum.5 = (f32[4,896,2048]{2,1,0:T(8,128)}, bf16[896,2048]{1,0:T(8,128)(2,1)}) custom-call(s32[1]{0:T(128)} %bitcast.6.order_ref, bf16[4,896,2048]{2,1,0:T(8,128)(2,1)} %grad_ref.7, f32[4,896,2048]{2,1,0:T(8,128)} %momentum_ref.7, f32[4,896,2048]{2,1,0:T(8,128)} %get-tuple-element.202.refs_0_), custom_call_target="tpu_custom_call", output_to_operand_aliasing={{0}: (3, {})} | custom-call | flops 1048576 | bytes 1024 | tf_op jit(solution)/shard_map/momentum/pallas_call | solution.py:43
  43.6 8.8 %gram.5 = (bf16[2304,256]{1,0:T(8,128)(2,1)}, bf16[2304,256]{1,0:T(8,128)(2,1)}, bf16[2320,256]{1,0:T(8,128)(2,1)}, bf16[2320,256]{1,0:T(8,128)(2,1)}) custom-call(s32[3]{0:T(128)} %pad_add_fusion.where_ref, bf16[896,2048]{1,0:T(8,128)(2,1)} %get-tuple-element.204.rows_ref), custom_call_target="tpu_custom_call" | custom-call | flops 1048576 | bytes 1024 | tf_op jit(solution)/shard_map/gram/pallas_call | solution.py:132
  62.4 6.1 %collective-permute-start.1 = (bf16[2304,256]{1,0:T(8,128)(2,1)S(1)}, bf16[2304,256]{1,0:T(8,128)(2,1)S(1)}, u32[]{:S(2)}, u32[]{:S(2)}) collective-permute-start(bf16[2304,256]{1,0:T(8,128)(2,1)S(1)} %add_convert_fusion.27), channel_id=1, source_target_pairs={{0,8},{4,12},{24,16},{28,20},{1,9},{5,13},{25,17},{29,21},{2,10},{... | collective-permute-start | bytes 3538952 | tf_op jit(solution)/shard_map/ppermute | solution.py:307
  69.8 11.5 %momentum.6 = (f32[4,896,2048]{2,1,0:T(8,128)}, bf16[896,2048]{1,0:T(8,128)(2,1)}) custom-call(s32[1]{0:T(128)} %bitcast.7.order_ref, bf16[4,896,2048]{2,1,0:T(8,128)(2,1)} %grad_ref.7, f32[4,896,2048]{2,1,0:T(8,128)} %momentum_ref.7, f32[4,896,2048]{2,1,0:T(8,128)} %get-tuple-element.218.refs_0_), custom_call_target="tpu_custom_call", output_to_operand_aliasing={{0}: (3, {})} | custom-call | flops 1048576 | bytes 1024 | tf_op jit(solution)/shard_map/momentum/pallas_call | solution.py:43
  87.6 8.8 %gram.6 = (bf16[2304,256]{1,0:T(8,128)(2,1)}, bf16[2304,256]{1,0:T(8,128)(2,1)}, bf16[2320,256]{1,0:T(8,128)(2,1)}, bf16[2320,256]{1,0:T(8,128)(2,1)}) custom-call(s32[3]{0:T(128)} %pad_add_fusion.where_ref, bf16[896,2048]{1,0:T(8,128)(2,1)} %get-tuple-element.221.rows_ref), custom_call_target="tpu_custom_call" | custom-call | flops 1048576 | bytes 1024 | tf_op jit(solution)/shard_map/gram/pallas_call | solution.py:132
  108.2 11.5 %momentum.7 = (f32[4,896,2048]{2,1,0:T(8,128)}, bf16[896,2048]{1,0:T(8,128)(2,1)}) custom-call(s32[1]{0:T(128)} %bitcast.1.order_ref, bf16[4,896,2048]{2,1,0:T(8,128)(2,1)} %grad_ref.7, f32[4,896,2048]{2,1,0:T(8,128)} %momentum_ref.7, f32[4,896,2048]{2,1,0:T(8,128)} %get-tuple-element.238.refs_0_), custom_call_target="tpu_custom_call", output_to_operand_aliasing={{0}: (3, {})} | custom-call | flops 1048576 | bytes 1024 | tf_op jit(solution)/shard_map/momentum/pallas_call | solution.py:43
  119.7 8.7 %gram.7 = (bf16[2304,256]{1,0:T(8,128)(2,1)}, bf16[2304,256]{1,0:T(8,128)(2,1)}, bf16[2320,256]{1,0:T(8,128)(2,1)}, bf16[2320,256]{1,0:T(8,128)(2,1)}) custom-call(s32[3]{0:T(128)} %pad_add_fusion.where_ref, bf16[896,2048]{1,0:T(8,128)(2,1)} %get-tuple-element.241.rows_ref), custom_call_target="tpu_custom_call" | custom-call | flops 1048576 | bytes 1024 | tf_op jit(solution)/shard_map/gram/pallas_call | solution.py:132
  138.9 19.3 %collective-permute-done.11 = bf16[2320,256]{1,0:T(8,128)(2,1)} collective-permute-done((bf16[2320,256]{1,0:T(8,128)(2,1)}, bf16[2320,256]{1,0:T(8,128)(2,1)}, u32[]{:S(2)}, u32[]{:S(2)}) %collective-permute-start.11) | collective-permute-done | bytes 1187872 | tf_op jit(solution)/shard_map/ppermute | solution.py:307
  158.2 7.9 %collective-permute-start.18 = (bf16[2320,256]{1,0:T(8,128)(2,1)S(1)}, bf16[2320,256]{1,0:T(8,128)(2,1)S(1)}, u32[]{:S(2)}, u32[]{:S(2)}) collective-permute-start(bf16[2320,256]{1,0:T(8,128)(2,1)S(1)} %copy-done.8), channel_id=1, source_target_pairs={{0,8},{4,12},{24,16},{28,20},{1,9},{5,13},{25,17},{29,21},{2,10},{... | collective-permute-start | bytes 3563528 | tf_op jit(solution)/shard_map/ppermute | solution.py:307
  166.1 12.8 %collective-permute-start.24 = (bf16[2304,256]{1,0:T(8,128)(2,1)S(1)}, bf16[2304,256]{1,0:T(8,128)(2,1)S(1)}, u32[]{:S(2)}, u32[]{:S(2)}) collective-permute-start(bf16[2304,256]{1,0:T(8,128)(2,1)S(1)} %add_convert_fusion.24), channel_id=1, source_target_pairs={{0,8},{4,12},{24,16},{28,20},{1,9},{5,13},{25,17},{29,21},{2,10},{... | collective-permute-start | bytes 3538952 | tf_op jit(solution)/shard_map/ppermute | solution.py:307
  193.0 17.7 %collective-permute-done.16 = bf16[2320,256]{1,0:T(8,128)(2,1)S(1)} collective-permute-done((bf16[2320,256]{1,0:T(8,128)(2,1)S(1)}, bf16[2320,256]{1,0:T(8,128)(2,1)S(1)}, u32[]{:S(2)}, u32[]{:S(2)}) %collective-permute-start.16) | collective-permute-done | bytes 1187872 | tf_op jit(solution)/shard_map/ppermute | solution.py:307
  217.3 47.4 %collective-permute-done.27 = bf16[2320,256]{1,0:T(8,128)(2,1)S(1)} collective-permute-done((bf16[2320,256]{1,0:T(8,128)(2,1)S(1)}, bf16[2320,256]{1,0:T(8,128)(2,1)S(1)}, u32[]{:S(2)}, u32[]{:S(2)}) %collective-permute-start.27) | collective-permute-done | bytes 1187872 | tf_op jit(solution)/shard_map/ppermute | solution.py:307
  270.9 32.2 %update.4 = (bf16[1,448,2048]{2,1,0:T(8,128)(2,1)}, bf16[1,448,2048]{2,1,0:T(8,128)(2,1)}) custom-call(s32[1]{0:T(128)} %constant.121.clone.1.slot_ref, s32[2,36]{1,0:T(2,128)} %select_bitcast_fusion.place_ref, bf16[896,2048]{1,0:T(8,128)(2,1)} %get-tuple-element.193.rows_ref, bf16[2304,256]{1,0:T(8,128)(2,1)} %copy-done.2, bf16[2304,256]{1,0:T(8,128)(2,1)} %copy-done.19, ...), custom_call_target="tpu_custom_call" | custom-call | flops 1048576 | bytes 1024 | tf_op jit(solution)/shard_map/update/pallas_call | solution.py:229
  315.5 8.1 %collective-permute-done.31 = bf16[2320,256]{1,0:T(8,128)(2,1)S(1)} collective-permute-done((bf16[2320,256]{1,0:T(8,128)(2,1)S(1)}, bf16[2320,256]{1,0:T(8,128)(2,1)S(1)}, u32[]{:S(2)}, u32[]{:S(2)}) %collective-permute-start.31) | collective-permute-done | bytes 1187872 | tf_op jit(solution)/shard_map/ppermute | solution.py:307
  326.4 29.1 %collective-permute-done.33.refs_0_ = bf16[1,448,2048]{2,1,0:T(8,128)(2,1)S(1)} collective-permute-done((bf16[1,448,2048]{2,1,0:T(8,128)(2,1)S(1)}, bf16[1,448,2048]{2,1,0:T(8,128)(2,1)S(1)}, u32[]{:S(2)}, u32[]{:S(2)}) %collective-permute-start.33) | collective-permute-done | bytes 1835040 | tf_op jit(solution)/shard_map/ppermute | solution.py:567
  364.3 21.1 %collective-permute-done.38 = bf16[2304,256]{1,0:T(8,128)(2,1)S(1)} collective-permute-done((bf16[2304,256]{1,0:T(8,128)(2,1)S(1)}, bf16[2304,256]{1,0:T(8,128)(2,1)S(1)}, u32[]{:S(2)}, u32[]{:S(2)}) %collective-permute-start.38) | collective-permute-done | bytes 1179680 | tf_op jit(solution)/shard_map/ppermute | solution.py:307
  396.6 19.0 %collective-permute-done.39.refs_1_ = bf16[2304,256]{1,0:T(8,128)(2,1)S(1)} collective-permute-done((bf16[2304,256]{1,0:T(8,128)(2,1)S(1)}, bf16[2304,256]{1,0:T(8,128)(2,1)S(1)}, u32[]{:S(2)}, u32[]{:S(2)}) %collective-permute-start.39) | collective-permute-done | bytes 1179680 | tf_op jit(solution)/shard_map/ppermute | solution.py:307
  418.1 32.1 %update.5 = (bf16[1,448,2048]{2,1,0:T(8,128)(2,1)}, bf16[1,448,2048]{2,1,0:T(8,128)(2,1)}) custom-call(s32[1]{0:T(128)} %constant.121.clone.1.slot_ref, s32[2,36]{1,0:T(2,128)} %select_bitcast_fusion.place_ref, bf16[896,2048]{1,0:T(8,128)(2,1)} %get-tuple-element.204.rows_ref, bf16[2304,256]{1,0:T(8,128)(2,1)} %copy-done.1, bf16[2304,256]{1,0:T(8,128)(2,1)} %copy-done.17, ...), custom_call_target="tpu_custom_call" | custom-call | flops 1048576 | bytes 1024 | tf_op jit(solution)/shard_map/update/pallas_call | solution.py:229
  464.9 20.3 %collective-permute-done.42 = bf16[2304,256]{1,0:T(8,128)(2,1)} collective-permute-done((bf16[2304,256]{1,0:T(8,128)(2,1)S(1)}, bf16[2304,256]{1,0:T(8,128)(2,1)}, u32[]{:S(2)}, u32[]{:S(2)}) %collective-permute-start.42) | collective-permute-done | bytes 1179680 | tf_op jit(solution)/shard_map/ppermute | solution.py:307
  487.2 6.3 %collective-permute-done.49.refs_0_ = bf16[1,448,2048]{2,1,0:T(8,128)(2,1)} collective-permute-done((bf16[1,448,2048]{2,1,0:T(8,128)(2,1)}, bf16[1,448,2048]{2,1,0:T(8,128)(2,1)}, u32[]{:S(2)}, u32[]{:S(2)}) %collective-permute-start.49) | collective-permute-done | bytes 1835040 | tf_op jit(solution)/shard_map/ppermute | solution.py:567
  495.9 32.0 %update.6 = (bf16[1,448,2048]{2,1,0:T(8,128)(2,1)}, bf16[1,448,2048]{2,1,0:T(8,128)(2,1)}) custom-call(s32[1]{0:T(128)} %constant.121.clone.1.slot_ref, s32[2,36]{1,0:T(2,128)} %select_bitcast_fusion.place_ref, bf16[896,2048]{1,0:T(8,128)(2,1)} %get-tuple-element.221.rows_ref, bf16[2304,256]{1,0:T(8,128)(2,1)} %copy-done, bf16[2304,256]{1,0:T(8,128)(2,1)} %copy-done.16, ...), custom_call_target="tpu_custom_call" | custom-call | flops 1048576 | bytes 1024 | tf_op jit(solution)/shard_map/update/pallas_call | solution.py:229
  536.4 22.4 %update.7.refs_2_ = bf16[4,896,2048]{2,1,0:T(8,128)(2,1)} custom-call(s32[1]{0:T(128)} %bitcast.12.slot_ref, s32[2,36]{1,0:T(2,128)} %select_bitcast_fusion.place_ref, bf16[896,2048]{1,0:T(8,128)(2,1)} %get-tuple-element.241.rows_ref, bf16[2304,256]{1,0:T(8,128)(2,1)} %copy-done.3, bf16[2304,256]{1,0:T(8,128)(2,1)} %copy-done.18, ...), custom_call_target="tpu_custom_call", output_to_operand_aliasing={{}: (7, {})} | custom-call | flops 1048576 | bytes 1024 | tf_op jit(solution)/shard_map/update/pallas_call | solution.py:229
  (208 shorter events, 154.1 us)
Async XLA Ops:
  29.7 52.3 %collective-permute-start.3 = (bf16[2320,256]{1,0:T(8,128)(2,1)}, bf16[2320,256]{1,0:T(8,128)(2,1)}, u32[]{:S(2)}, u32[]{:S(2)}) collective-permute-start(bf16[2320,256]{1,0:T(8,128)(2,1)} %get-tuple-element.200), channel_id=1, source_target_pairs={{0,8},{4,12},{24,16},{28,20},{1,9},{5,13},{25,17},{29,21},{2,10},{... | collective-permute-start | bytes 3563528 | tf_op jit(solution)/shard_map/ppermute | solution.py:307
  62.4 44.8 %collective-permute-start.1 = (bf16[2304,256]{1,0:T(8,128)(2,1)S(1)}, bf16[2304,256]{1,0:T(8,128)(2,1)S(1)}, u32[]{:S(2)}, u32[]{:S(2)}) collective-permute-start(bf16[2304,256]{1,0:T(8,128)(2,1)S(1)} %add_convert_fusion.27), channel_id=1, source_target_pairs={{0,8},{4,12},{24,16},{28,20},{1,9},{5,13},{25,17},{29,21},{2,10},{... | collective-permute-start | bytes 3538952 | tf_op jit(solution)/shard_map/ppermute | solution.py:307
  68.5 64.1 %collective-permute-start.8 = (bf16[2320,256]{1,0:T(8,128)(2,1)S(1)}, bf16[2320,256]{1,0:T(8,128)(2,1)S(1)}, u32[]{:S(2)}, u32[]{:S(2)}) collective-permute-start(bf16[2320,256]{1,0:T(8,128)(2,1)S(1)} %copy-done.9), channel_id=1, source_target_pairs={{0,8},{4,12},{24,16},{28,20},{1,9},{5,13},{25,17},{29,21},{2,10},{... | collective-permute-start | bytes 3563528 | tf_op jit(solution)/shard_map/ppermute | solution.py:307
  82.0 76.2 %collective-permute-start.11 = (bf16[2320,256]{1,0:T(8,128)(2,1)}, bf16[2320,256]{1,0:T(8,128)(2,1)}, u32[]{:S(2)}, u32[]{:S(2)}) collective-permute-start(bf16[2320,256]{1,0:T(8,128)(2,1)} %get-tuple-element.216), channel_id=1, source_target_pairs={{0,8},{4,12},{24,16},{28,20},{1,9},{5,13},{25,17},{29,21},{2,10},{... | collective-permute-start | bytes 3563528 | tf_op jit(solution)/shard_map/ppermute | solution.py:307
  98.2 85.2 %collective-permute-start.6 = (bf16[2304,256]{1,0:T(8,128)(2,1)S(1)}, bf16[2304,256]{1,0:T(8,128)(2,1)}, u32[]{:S(2)}, u32[]{:S(2)}) collective-permute-start(bf16[2304,256]{1,0:T(8,128)(2,1)S(1)} %add_convert_fusion.26), channel_id=1, source_target_pairs={{0,8},{4,12},{24,16},{28,20},{1,9},{5,13},{25,17},{29,21},{2,10},{... | collective-permute-start | bytes 3538952 | tf_op jit(solution)/shard_map/ppermute | solution.py:307
  136.5 44.5 %collective-permute-start.14 = (bf16[2304,256]{1,0:T(8,128)(2,1)S(1)}, bf16[2304,256]{1,0:T(8,128)(2,1)S(1)}, u32[]{:S(2)}, u32[]{:S(2)}) collective-permute-start(bf16[2304,256]{1,0:T(8,128)(2,1)S(1)} %add_convert_fusion.23), channel_id=1, source_target_pairs={{8,0},{12,4},{16,24},{20,28},{9,1},{13,5},{17,25},{21,29},{10,2},{... | collective-permute-start | bytes 3538952 | tf_op jit(solution)/shard_map/ppermute | solution.py:307
  137.9 46.8 %collective-permute-start.10 = (bf16[2304,256]{1,0:T(8,128)(2,1)S(1)}, bf16[2304,256]{1,0:T(8,128)(2,1)S(1)}, u32[]{:S(2)}, u32[]{:S(2)}) collective-permute-start(bf16[2304,256]{1,0:T(8,128)(2,1)S(1)} %copy-done.27), channel_id=1, source_target_pairs={{0,4},{4,0},{8,12},{12,8},{16,20},{20,16},{24,28},{28,24},{1,5},{5... | collective-permute-start | bytes 3538952 | tf_op jit(solution)/shard_map/ppermute | solution.py:307
  158.2 54.9 %collective-permute-start.18 = (bf16[2320,256]{1,0:T(8,128)(2,1)S(1)}, bf16[2320,256]{1,0:T(8,128)(2,1)S(1)}, u32[]{:S(2)}, u32[]{:S(2)}) collective-permute-start(bf16[2320,256]{1,0:T(8,128)(2,1)S(1)} %copy-done.8), channel_id=1, source_target_pairs={{0,8},{4,12},{24,16},{28,20},{1,9},{5,13},{25,17},{29,21},{2,10},{... | collective-permute-start | bytes 3563528 | tf_op jit(solution)/shard_map/ppermute | solution.py:307
  166.1 101.5 %collective-permute-start.24 = (bf16[2304,256]{1,0:T(8,128)(2,1)S(1)}, bf16[2304,256]{1,0:T(8,128)(2,1)S(1)}, u32[]{:S(2)}, u32[]{:S(2)}) collective-permute-start(bf16[2304,256]{1,0:T(8,128)(2,1)S(1)} %add_convert_fusion.24), channel_id=1, source_target_pairs={{0,8},{4,12},{24,16},{28,20},{1,9},{5,13},{25,17},{29,21},{2,10},{... | collective-permute-start | bytes 3538952 | tf_op jit(solution)/shard_map/ppermute | solution.py:307
  184.6 118.4 %collective-permute-start.21 = (bf16[2320,256]{1,0:T(8,128)(2,1)S(1)}, bf16[2320,256]{1,0:T(8,128)(2,1)}, u32[]{:S(2)}, u32[]{:S(2)}) collective-permute-start(bf16[2320,256]{1,0:T(8,128)(2,1)S(1)} %copy-done.12), channel_id=1, source_target_pairs={{0,8},{4,12},{24,16},{28,20},{1,9},{5,13},{25,17},{29,21},{2,10},{... | collective-permute-start | bytes 3563528 | tf_op jit(solution)/shard_map/ppermute | solution.py:307
  213.0 56.3 %collective-permute-start.25 = (bf16[2304,256]{1,0:T(8,128)(2,1)S(1)}, bf16[2304,256]{1,0:T(8,128)(2,1)S(1)}, u32[]{:S(2)}, u32[]{:S(2)}) collective-permute-start(bf16[2304,256]{1,0:T(8,128)(2,1)S(1)} %broadcast_select_fusion.11.refs_0_), channel_id=1, source_target_pairs={{0,4},{4,0},{8,12},{12,8},{16,20},{20,16},{24,28},{28,24},{1,5},{5... | collective-permute-start | bytes 3538952 | tf_op jit(solution)/shard_map/ppermute | solution.py:307
  213.5 51.2 %collective-permute-start.27 = (bf16[2320,256]{1,0:T(8,128)(2,1)S(1)}, bf16[2320,256]{1,0:T(8,128)(2,1)S(1)}, u32[]{:S(2)}, u32[]{:S(2)}) collective-permute-start(bf16[2320,256]{1,0:T(8,128)(2,1)S(1)} %collective-permute-done.15), channel_id=1, source_target_pairs={{8,0},{12,4},{16,24},{20,28},{9,1},{13,5},{17,25},{21,29},{10,2},{... | collective-permute-start | bytes 3563528 | tf_op jit(solution)/shard_map/ppermute | solution.py:307
  215.7 93.1 %collective-permute-start.23 = (bf16[2320,256]{1,0:T(8,128)(2,1)S(1)}, bf16[2320,256]{1,0:T(8,128)(2,1)}, u32[]{:S(2)}, u32[]{:S(2)}) collective-permute-start(bf16[2320,256]{1,0:T(8,128)(2,1)S(1)} %add_convert_fusion.7), channel_id=1, source_target_pairs={{8,0},{12,4},{16,24},{20,28},{9,1},{13,5},{17,25},{21,29},{10,2},{... | collective-permute-start | bytes 3563528 | tf_op jit(solution)/shard_map/ppermute | solution.py:307
  264.8 45.3 %collective-permute-start.22 = (bf16[2320,256]{1,0:T(8,128)(2,1)S(1)}, bf16[2320,256]{1,0:T(8,128)(2,1)}, u32[]{:S(2)}, u32[]{:S(2)}) collective-permute-start(bf16[2320,256]{1,0:T(8,128)(2,1)S(1)} %add_convert_fusion.8), channel_id=1, source_target_pairs={{8,16},{12,20},{16,8},{20,12},{9,17},{13,21},{17,9},{21,13},{10,18... | collective-permute-start | bytes 3563528 | tf_op jit(solution)/shard_map/ppermute | solution.py:307
  267.6 45.6 %collective-permute-start.20 = (bf16[2320,256]{1,0:T(8,128)(2,1)S(1)}, bf16[2320,256]{1,0:T(8,128)(2,1)}, u32[]{:S(2)}, u32[]{:S(2)}) collective-permute-start(bf16[2320,256]{1,0:T(8,128)(2,1)S(1)} %add_convert_fusion.7), channel_id=1, source_target_pairs={{8,16},{12,20},{16,8},{20,12},{9,17},{13,21},{17,9},{21,13},{10,18... | collective-permute-start | bytes 3563528 | tf_op jit(solution)/shard_map/ppermute | solution.py:307
  308.7 50.4 %collective-permute-start.17 = (bf16[2304,256]{1,0:T(8,128)(2,1)S(1)}, bf16[2304,256]{1,0:T(8,128)(2,1)S(1)}, u32[]{:S(2)}, u32[]{:S(2)}) collective-permute-start(bf16[2304,256]{1,0:T(8,128)(2,1)S(1)} %add_convert_fusion.21), channel_id=1, source_target_pairs={{0,8},{4,12},{24,16},{28,20},{1,9},{5,13},{25,17},{29,21},{2,10},{... | collective-permute-start | bytes 3538952 | tf_op jit(solution)/shard_map/ppermute | solution.py:307
  325.3 62.9 %collective-permute-start.37 = (bf16[2320,256]{1,0:T(8,128)(2,1)S(1)}, bf16[2320,256]{1,0:T(8,128)(2,1)S(1)}, u32[]{:S(2)}, u32[]{:S(2)}) collective-permute-start(bf16[2320,256]{1,0:T(8,128)(2,1)S(1)} %add_convert_fusion.4), channel_id=1, source_target_pairs={{8,16},{12,20},{16,8},{20,12},{9,17},{13,21},{17,9},{21,13},{10,18... | collective-permute-start | bytes 3563528 | tf_op jit(solution)/shard_map/ppermute | solution.py:307
  363.9 89.4 %collective-permute-start.45 = (bf16[1,448,2048]{2,1,0:T(8,128)(2,1)}, bf16[1,448,2048]{2,1,0:T(8,128)(2,1)}, u32[]{:S(2)}, u32[]{:S(2)}) collective-permute-start(bf16[1,448,2048]{2,1,0:T(8,128)(2,1)} %get-tuple-element.354), channel_id=1, source_target_pairs={{0,3},{1,2},{2,1},{3,0},{4,7},{5,6},{6,5},{7,4},{8,11},{9,10},{10,... | collective-permute-start | bytes 5505032 | tf_op jit(solution)/shard_map/ppermute | solution.py:567
  392.3 57.9 %collective-permute-start.35 = (bf16[2320,256]{1,0:T(8,128)(2,1)S(1)}, bf16[2320,256]{1,0:T(8,128)(2,1)}, u32[]{:S(2)}, u32[]{:S(2)}) collective-permute-start(bf16[2320,256]{1,0:T(8,128)(2,1)S(1)} %add_convert_fusion.3), channel_id=1, source_target_pairs={{8,0},{12,4},{16,24},{20,28},{9,1},{13,5},{17,25},{21,29},{10,2},{... | collective-permute-start | bytes 3563528 | tf_op jit(solution)/shard_map/ppermute | solution.py:307
  393.6 56.5 %collective-permute-start.34 = (bf16[2304,256]{1,0:T(8,128)(2,1)S(1)}, bf16[2304,256]{1,0:T(8,128)(2,1)}, u32[]{:S(2)}, u32[]{:S(2)}) collective-permute-start(bf16[2304,256]{1,0:T(8,128)(2,1)S(1)} %add_convert_fusion.17), channel_id=1, source_target_pairs={{8,16},{12,20},{16,8},{20,12},{9,17},{13,21},{17,9},{21,13},{10,18... | collective-permute-start | bytes 3538952 | tf_op jit(solution)/shard_map/ppermute | solution.py:307
  395.9 62.1 %collective-permute-start.43 = (bf16[2320,256]{1,0:T(8,128)(2,1)S(1)}, bf16[2320,256]{1,0:T(8,128)(2,1)S(1)}, u32[]{:S(2)}, u32[]{:S(2)}) collective-permute-start(bf16[2320,256]{1,0:T(8,128)(2,1)S(1)} %add_convert_fusion.1), channel_id=1, source_target_pairs={{8,12},{12,8},{16,20},{20,16},{9,13},{13,9},{17,21},{21,17},{10,14... | collective-permute-start | bytes 3563528 | tf_op jit(solution)/shard_map/ppermute | solution.py:307
  461.6 97.2 %collective-permute-start.51 = (bf16[1,448,2048]{2,1,0:T(8,128)(2,1)}, bf16[1,448,2048]{2,1,0:T(8,128)(2,1)S(1)}, u32[]{:S(2)}, u32[]{:S(2)}) collective-permute-start(bf16[1,448,2048]{2,1,0:T(8,128)(2,1)} %get-tuple-element.379), channel_id=1, source_target_pairs={{0,2},{1,3},{2,0},{3,1},{4,6},{5,7},{6,4},{7,5},{8,10},{9,11},{10,... | collective-permute-start | bytes 5505032 | tf_op jit(solution)/shard_map/ppermute | solution.py:567
  463.6 69.2 %collective-permute-start.46 = (bf16[2320,256]{1,0:T(8,128)(2,1)S(1)}, bf16[2320,256]{1,0:T(8,128)(2,1)S(1)}, u32[]{:S(2)}, u32[]{:S(2)}) collective-permute-start(bf16[2320,256]{1,0:T(8,128)(2,1)S(1)} %add_convert_fusion), channel_id=1, source_target_pairs={{8,0},{12,4},{16,24},{20,28},{9,1},{13,5},{17,25},{21,29},{10,2},{... | collective-permute-start | bytes 3563528 | tf_op jit(solution)/shard_map/ppermute | solution.py:307
  486.6 45.6 %collective-permute-start.47 = (bf16[2304,256]{1,0:T(8,128)(2,1)S(1)}, bf16[2304,256]{1,0:T(8,128)(2,1)S(1)}, u32[]{:S(2)}, u32[]{:S(2)}) collective-permute-start(bf16[2304,256]{1,0:T(8,128)(2,1)S(1)} %broadcast_select_fusion.8.refs_0_), channel_id=1, source_target_pairs={{0,4},{4,0},{8,12},{12,8},{16,20},{20,16},{24,28},{28,24},{1,5},{5... | collective-permute-start | bytes 3538952 | tf_op jit(solution)/shard_map/ppermute | solution.py:307
  (60 other events, 1267.8 us)
